TPU v7x, 32 devices: a whole 2x2x4 slice. The times are simulated.
32 devices in a mesh: rows: 16 (over z, x, core), seq: 2 (over y).
Axes of the slice: x: 2, y: 2, z: 4, core: 2. Of those that a mesh axis runs over, the one named last changes fastest.
Arguments:
- target_states: bfloat16 [16, 1024, 512], P('rows', 'seq'), may hold values from -6 to 6
- source_states: bfloat16 [16, 336, 512], P('rows', 'seq'), may hold values from -6 to 6
- target_segments: int32 [16, 1024], P('rows'), may hold values from 0 to 8, as said below
- source_segments: int32 [16, 336], P('rows'), may hold values from 0 to 9, as said below
- output_grad: bfloat16 [16, 1024, 512], P('rows', 'seq'), may hold values from -6 to 6
- self_project: bfloat16 [512, 1536], P(('rows', 'seq')), may hold values from -0.25 to 0.25
- self_output: bfloat16 [512, 512], P(('rows', 'seq')), may hold values from -1 to 1
- cross_query: bfloat16 [512, 512], P(('rows', 'seq')), may hold values from -0.25 to 0.25
- cross_keyval: bfloat16 [512, 1024], P(('rows', 'seq')), may hold values from -0.25 to 0.25
- cross_output: bfloat16 [512, 512], P(('rows', 'seq')), may hold values from -1 to 1
- hidden_up: bfloat16 [512, 2048], P(('rows', 'seq')), may hold values from -0.25 to 0.25
- hidden_bias: bfloat16 [2048], P(('rows', 'seq')), may hold values from -3 to 3
- hidden_down: bfloat16 [2048, 512], P(('rows', 'seq')), may hold values from -0.25 to 0.25
- output_bias: bfloat16 [512], P(('rows', 'seq')), may hold values from -3 to 3
- first_gain: bfloat16 [512], P(('rows', 'seq')), may hold values from 0.25 to 1.75
- first_shift: bfloat16 [512], P(('rows', 'seq')), may hold values from -3 to 3
- second_gain: bfloat16 [512], P(('rows', 'seq')), may hold values from 0.25 to 1.75
- second_shift: bfloat16 [512], P(('rows', 'seq')), may hold values from -3 to 3
- third_gain: bfloat16 [512], P(('rows', 'seq')), may hold values from 0.25 to 1.75
- third_shift: bfloat16 [512], P(('rows', 'seq')), may hold values from -3 to 3
Outputs:
- layer_output: bfloat16 [16, 1024, 512], P('rows', 'seq')
- grad_target: float32 [16, 1024, 512], P('rows', 'seq')
- grad_source: float32 [16, 336, 512], P('rows', 'seq')
- grad_self_project: float32 [512, 1536], P(('rows', 'seq'))
- grad_self_output: float32 [512, 512], P(('rows', 'seq'))
- grad_cross_query: float32 [512, 512], P(('rows', 'seq'))
- grad_cross_keyval: float32 [512, 1024], P(('rows', 'seq'))
- grad_cross_output: float32 [512, 512], P(('rows', 'seq'))
- grad_hidden_up: float32 [512, 2048], P(('rows', 'seq'))
- grad_hidden_bias: float32 [2048], P(('rows', 'seq'))
- grad_hidden_down: float32 [2048, 512], P(('rows', 'seq'))
- grad_output_bias: float32 [512], P(('rows', 'seq'))
- grad_first_gain: float32 [512], P(('rows', 'seq'))
- grad_first_shift: float32 [512], P(('rows', 'seq'))
- grad_second_gain: float32 [512], P(('rows', 'seq'))
- grad_second_shift: float32 [512], P(('rows', 'seq'))
- grad_third_gain: float32 [512], P(('rows', 'seq'))
- grad_third_shift: float32 [512], P(('rows', 'seq'))
Inputs may be any that keep to these rules, and one draw needn't show every extreme that they name: `target_segments`: in each row the numbers 0 to 8 rise along the positions, each used. Sentences 0 to 3 and 5 to 8 each hold 64 to 127 positions; sentence 4 begins within the first 512 positions and ends within the last 512. `source_segments`: in each row the numbers 0 to 9 rise along the positions, each used; each sentence's source positions are roughly in proportion to its target positions, and 9 marks padding at the end of the row.
All inputs are finite; a program needn't handle non-finite values.
Results may differ from a plain program's by a relative error of at most 0.024.
Values may be sent and summed in bfloat16 or wider, within the bound.
No kernel may reach another device: no remote copies, remote signals or barrier semaphores. Data moves between devices by JAX's collectives and lax.ppermute only.
A program may use at most 256 MiB of HBM per device.

v0:
```python
import jax
import jax.numpy as jnp
from jax import lax
from jax.experimental import pallas as pl
from jax.experimental.pallas import tpu as pltpu
from jax.sharding import PartitionSpec as P

HEADS = 8
HD = 64


def layer_norm(value, gain, shift):
    row_mean = jnp.mean(value, -1, keepdims=True)
    centered = value - row_mean
    variance = jnp.mean(centered * centered, -1, keepdims=True)
    inverse = lax.rsqrt(variance + 1e-05)
    normed = centered * inverse
    return (normed * gain + shift, normed, inverse)


def norm_back(upstream, normed, inverse, gain):
    scaled = upstream * gain
    first_mean = jnp.mean(scaled, -1, keepdims=True)
    second_mean = jnp.mean(scaled * normed, -1, keepdims=True)
    grad_input = inverse * (scaled - first_mean - normed * second_mean)
    return (grad_input, jnp.sum(upstream * normed, 0), jnp.sum(upstream, 0))


def matmul(left, right):
    return jnp.dot(left, right, preferred_element_type=jnp.float32)


def transposed(left, right):
    return lax.dot_general(
        left, right, (((0,), (0,)), ((), ())), preferred_element_type=jnp.float32
    )


def against(left, right):
    return lax.dot_general(
        left, right, (((1,), (1,)), ((), ())), preferred_element_type=jnp.float32
    )


def head_split(value):
    return value.reshape(value.shape[0], HEADS, HD)


def head_join(value):
    return value.reshape(value.shape[0], HEADS * HD)


def scores_of(queries, key_rows, query_seg, key_seg):
    raw_scores = jnp.einsum(
        "qhd,khd->hqk", queries, key_rows, preferred_element_type=jnp.float32
    ) * HD ** (-0.5)
    same_seg = (query_seg[:, None] == key_seg[None, :])[None]
    return (raw_scores, same_seg)


def block_weights(queries, key_rows, query_seg, key_seg, log_total):
    raw_scores, same_seg = scores_of(queries, key_rows, query_seg, key_seg)
    return jnp.where(same_seg, jnp.exp(raw_scores - log_total[..., None]), 0.0)


def log_totals(queries, key_blocks, seg_blocks, query_seg):

    def log_advance(carry, inputs_now):
        row_max, row_total = carry
        key_rows, key_seg = inputs_now
        raw_scores, same_seg = scores_of(queries, key_rows, query_seg, key_seg)
        masked = jnp.where(same_seg, raw_scores, -1000000000.0)
        new_max = jnp.maximum(row_max, jnp.max(masked, -1))
        shifted = jnp.where(same_seg, jnp.exp(masked - new_max[..., None]), 0.0)
        return ((new_max, row_total * jnp.exp(row_max - new_max) + jnp.sum(shifted, -1)), None)

    start = (
        jnp.full((HEADS, queries.shape[0]), -1000000000.0, jnp.float32),
        jnp.zeros((HEADS, queries.shape[0]), jnp.float32),
    )
    (row_max, row_total), unused = lax.scan(log_advance, start, (key_blocks, seg_blocks))
    return row_max + jnp.log(row_total)


def weighted_sum(queries, key_blocks, value_blocks, seg_blocks, query_seg, log_total):

    def weighted_advance(carry, inputs_now):
        key_rows, value_rows, key_seg = inputs_now
        weights = block_weights(queries, key_rows, query_seg, key_seg, log_total).astype(
            jnp.bfloat16
        )
        return (
            carry
            + jnp.einsum("hqk,khd->qhd", weights, value_rows, preferred_element_type=jnp.float32),
            None,
        )

    total, unused = lax.scan(
        weighted_advance,
        jnp.zeros(queries.shape, jnp.float32),
        (key_blocks, value_blocks, seg_blocks),
    )
    return total


def grad_dots(queries, grad_heads, key_blocks, value_blocks, seg_blocks, query_seg, log_total):

    def grad_advance(carry, inputs_now):
        key_rows, value_rows, key_seg = inputs_now
        weights = block_weights(queries, key_rows, query_seg, key_seg, log_total)
        grad_weights = jnp.einsum(
            "qhd,khd->hqk", grad_heads, value_rows, preferred_element_type=jnp.float32
        )
        return (carry + jnp.sum(weights * grad_weights, -1), None)

    start = jnp.zeros((HEADS, queries.shape[0]), jnp.float32)
    total, unused = lax.scan(grad_advance, start, (key_blocks, value_blocks, seg_blocks))
    return total


def query_grads(
    queries, grad_heads, key_blocks, value_blocks, seg_blocks, query_seg, log_total, row_dots
):
    score_scale = HD ** (-0.5)

    def query_advance(carry, inputs_now):
        key_rows, value_rows, key_seg = inputs_now
        weights = block_weights(queries, key_rows, query_seg, key_seg, log_total)
        grad_weights = jnp.einsum(
            "qhd,khd->hqk", grad_heads, value_rows, preferred_element_type=jnp.float32
        )
        grad_scores = (weights * (grad_weights - row_dots[..., None])).astype(jnp.bfloat16)
        carry = (
            carry
            + jnp.einsum("hqk,khd->qhd", grad_scores, key_rows, preferred_element_type=jnp.float32)
            * score_scale
        )
        grad_keys = (
            jnp.einsum("hqk,qhd->khd", grad_scores, queries, preferred_element_type=jnp.float32)
            * score_scale
        )
        grad_values = jnp.einsum(
            "hqk,qhd->khd",
            weights.astype(jnp.bfloat16),
            grad_heads,
            preferred_element_type=jnp.float32,
        )
        return (carry, jnp.concatenate([head_join(grad_keys), head_join(grad_values)], 1))

    return lax.scan(
        query_advance, jnp.zeros(queries.shape, jnp.float32), (key_blocks, value_blocks, seg_blocks)
    )


def general_device(
    target_states,
    source_states,
    target_segments,
    source_segments,
    output_grad,
    self_project,
    self_output,
    cross_query,
    cross_keyval,
    cross_output,
    hidden_up,
    hidden_bias,
    hidden_down,
    output_bias,
    first_gain,
    first_shift,
    second_gain,
    second_shift,
    third_gain,
    third_shift,
):
    (
        full_project,
        full_output,
        full_query,
        full_keyval,
        full_crossout,
        full_up,
        full_upbias,
        full_down,
        full_downbias,
        gain_one,
        shift_one,
        gain_two,
        shift_two,
        gain_three,
        shift_three,
    ) = (
        lax.all_gather(self_project, ("rows", "seq"), axis=0, tiled=True),
        lax.all_gather(self_output, ("rows", "seq"), axis=0, tiled=True),
        lax.all_gather(cross_query, ("rows", "seq"), axis=0, tiled=True),
        lax.all_gather(cross_keyval, ("rows", "seq"), axis=0, tiled=True),
        lax.all_gather(cross_output, ("rows", "seq"), axis=0, tiled=True),
        lax.all_gather(hidden_up, ("rows", "seq"), axis=0, tiled=True),
        lax.all_gather(hidden_bias, ("rows", "seq"), axis=0, tiled=True),
        lax.all_gather(hidden_down, ("rows", "seq"), axis=0, tiled=True),
        lax.all_gather(output_bias, ("rows", "seq"), axis=0, tiled=True),
        lax.all_gather(first_gain, ("rows", "seq"), axis=0, tiled=True),
        lax.all_gather(first_shift, ("rows", "seq"), axis=0, tiled=True),
        lax.all_gather(second_gain, ("rows", "seq"), axis=0, tiled=True),
        lax.all_gather(second_shift, ("rows", "seq"), axis=0, tiled=True),
        lax.all_gather(third_gain, ("rows", "seq"), axis=0, tiled=True),
        lax.all_gather(third_shift, ("rows", "seq"), axis=0, tiled=True),
    )
    gain_one = gain_one.astype(jnp.float32)
    gain_two = gain_two.astype(jnp.float32)
    gain_three = gain_three.astype(jnp.float32)
    score_scale = HD ** (-0.5)
    states = target_states[0].astype(jnp.float32)
    local_rows = states.shape[0]
    model_width = states.shape[1]
    seq_count = lax.axis_size("seq")
    row_segments = target_segments[0]
    seq_length = row_segments.shape[0]
    own_segments = lax.dynamic_slice_in_dim(
        row_segments, lax.axis_index("seq") * local_rows, local_rows
    )
    block_rows = max(1, min(seq_count, 512 // local_rows)) * local_rows
    block_count = seq_length // block_rows
    seg_blocks = row_segments.reshape(block_count, block_rows)
    normed_value, normed_one, inverse_one = layer_norm(
        states, gain_one, shift_one.astype(jnp.float32)
    )
    lowered_one = normed_value.astype(jnp.bfloat16)
    projected = matmul(lowered_one, full_project).astype(jnp.bfloat16)
    query_flat = projected[:, :model_width]
    key_local = projected[:, model_width : 2 * model_width]
    value_local = projected[:, 2 * model_width :]
    queries = head_split(query_flat)
    key_all, value_all = (
        lax.all_gather(key_local, "seq", axis=0, tiled=True),
        lax.all_gather(value_local, "seq", axis=0, tiled=True),
    )
    key_blocks = key_all.reshape(block_count, block_rows, HEADS, HD)
    value_blocks = value_all.reshape(block_count, block_rows, HEADS, HD)
    log_total = log_totals(queries, key_blocks, seg_blocks, own_segments)
    self_mixed = head_join(
        weighted_sum(queries, key_blocks, value_blocks, seg_blocks, own_segments, log_total)
    ).astype(jnp.bfloat16)
    after_self = states + matmul(self_mixed, full_output)
    normed_value, normed_two, inverse_two = layer_norm(
        after_self, gain_two, shift_two.astype(jnp.float32)
    )
    lowered_two = normed_value.astype(jnp.bfloat16)
    cross_asked = matmul(lowered_two, full_query).astype(jnp.bfloat16)
    source_low = source_states[0]
    source_all = lax.all_gather(source_low, "seq", axis=0, tiled=True)
    key_value = matmul(source_all, full_keyval).astype(jnp.bfloat16)
    cross_key_heads = head_split(key_value[:, :model_width])
    cross_value_heads = head_split(key_value[:, model_width:])
    asked_heads = head_split(cross_asked)
    raw_scores, same_seg = scores_of(asked_heads, cross_key_heads, own_segments, source_segments[0])
    cross_probs = jax.nn.softmax(jnp.where(same_seg, raw_scores, -1000000000.0), axis=-1)
    cross_mixed = head_join(
        jnp.einsum(
            "hqk,khd->qhd",
            cross_probs.astype(jnp.bfloat16),
            cross_value_heads,
            preferred_element_type=jnp.float32,
        )
    ).astype(jnp.bfloat16)
    after_cross = after_self + matmul(cross_mixed, full_crossout)
    normed_value, normed_three, inverse_three = layer_norm(
        after_cross, gain_three, shift_three.astype(jnp.float32)
    )
    lowered_three = normed_value.astype(jnp.bfloat16)
    hidden = matmul(lowered_three, full_up) + full_upbias.astype(jnp.float32)
    activated = jax.nn.gelu(hidden).astype(jnp.bfloat16)
    layer_out = after_cross + matmul(activated, full_down) + full_downbias.astype(jnp.float32)
    grad_low = output_grad[0]
    out_grad = grad_low.astype(jnp.float32)
    grad_down = transposed(activated, grad_low)
    grad_downbias = jnp.sum(out_grad, 0)
    grad_act = against(grad_low, full_down)
    grad_hidden = jax.vjp(jax.nn.gelu, hidden)[1](grad_act)[0].astype(jnp.bfloat16)
    grad_upbias = jnp.sum(grad_hidden.astype(jnp.float32), 0)
    grad_up = transposed(lowered_three, grad_hidden)
    dx_three, grad_gain_three, grad_shift_three = norm_back(
        against(grad_hidden, full_up), normed_three, inverse_three, gain_three
    )
    grad_cross = out_grad + dx_three
    grad_cross_low = grad_cross.astype(jnp.bfloat16)
    grad_crossout = transposed(cross_mixed, grad_cross_low)
    grad_cross_heads = head_split(against(grad_cross_low, full_crossout).astype(jnp.bfloat16))
    grad_weights = jnp.einsum(
        "qhd,khd->hqk", grad_cross_heads, cross_value_heads, preferred_element_type=jnp.float32
    )
    grad_scores = (
        cross_probs * (grad_weights - jnp.sum(cross_probs * grad_weights, -1, keepdims=True))
    ).astype(jnp.bfloat16)
    grad_asked = head_join(
        jnp.einsum("hqk,khd->qhd", grad_scores, cross_key_heads, preferred_element_type=jnp.float32)
        * score_scale
    ).astype(jnp.bfloat16)
    grad_cross_keys = (
        jnp.einsum("hqk,qhd->khd", grad_scores, asked_heads, preferred_element_type=jnp.float32)
        * score_scale
    )
    grad_cross_values = jnp.einsum(
        "hqk,qhd->khd",
        cross_probs.astype(jnp.bfloat16),
        grad_cross_heads,
        preferred_element_type=jnp.float32,
    )
    pair_terms = jnp.concatenate([head_join(grad_cross_keys), head_join(grad_cross_values)], 1)
    pair_grad = lax.psum_scatter(
        pair_terms.astype(jnp.bfloat16), "seq", scatter_dimension=0, tiled=True
    )
    grad_keyval = transposed(source_low, pair_grad)
    grad_source = against(pair_grad, full_keyval)
    grad_query = transposed(lowered_two, grad_asked)
    dx_two, grad_gain_two, grad_shift_two = norm_back(
        against(grad_asked, full_query), normed_two, inverse_two, gain_two
    )
    grad_self = grad_cross + dx_two
    grad_self_low = grad_self.astype(jnp.bfloat16)
    grad_output = transposed(self_mixed, grad_self_low)
    grad_mixed = against(grad_self_low, full_output).astype(jnp.bfloat16)
    grad_heads = head_split(grad_mixed)
    row_dots = grad_dots(
        queries, grad_heads, key_blocks, value_blocks, seg_blocks, own_segments, log_total
    )
    grad_queries, key_terms = query_grads(
        queries, grad_heads, key_blocks, value_blocks, seg_blocks, own_segments, log_total, row_dots
    )
    summed = lax.psum_scatter(
        key_terms.reshape(seq_length, 2 * model_width).astype(jnp.bfloat16),
        "seq",
        scatter_dimension=0,
        tiled=True,
    )
    grad_projected = jnp.concatenate([head_join(grad_queries).astype(jnp.bfloat16), summed], 1)
    grad_project = transposed(lowered_one, grad_projected)
    dx_one, grad_gain_one, grad_shift_one = norm_back(
        against(grad_projected, full_project), normed_one, inverse_one, gain_one
    )
    grad_target = grad_self + dx_one
    shards = (
        lax.psum_scatter(grad_project, ("rows", "seq"), scatter_dimension=0, tiled=True),
        lax.psum_scatter(grad_output, ("rows", "seq"), scatter_dimension=0, tiled=True),
        lax.psum_scatter(grad_query, ("rows", "seq"), scatter_dimension=0, tiled=True),
        lax.psum_scatter(grad_keyval, ("rows", "seq"), scatter_dimension=0, tiled=True),
        lax.psum_scatter(grad_crossout, ("rows", "seq"), scatter_dimension=0, tiled=True),
        lax.psum_scatter(grad_up, ("rows", "seq"), scatter_dimension=0, tiled=True),
        lax.psum_scatter(grad_upbias, ("rows", "seq"), scatter_dimension=0, tiled=True),
        lax.psum_scatter(grad_down, ("rows", "seq"), scatter_dimension=0, tiled=True),
        lax.psum_scatter(grad_downbias, ("rows", "seq"), scatter_dimension=0, tiled=True),
        lax.psum_scatter(grad_gain_one, ("rows", "seq"), scatter_dimension=0, tiled=True),
        lax.psum_scatter(grad_shift_one, ("rows", "seq"), scatter_dimension=0, tiled=True),
        lax.psum_scatter(grad_gain_two, ("rows", "seq"), scatter_dimension=0, tiled=True),
        lax.psum_scatter(grad_shift_two, ("rows", "seq"), scatter_dimension=0, tiled=True),
        lax.psum_scatter(grad_gain_three, ("rows", "seq"), scatter_dimension=0, tiled=True),
        lax.psum_scatter(grad_shift_three, ("rows", "seq"), scatter_dimension=0, tiled=True),
    )
    return (layer_out.astype(jnp.bfloat16)[None], grad_target[None], grad_source[None]) + tuple(
        shards
    )


F32, BF16 = jnp.float32, jnp.bfloat16
BLOCK = 16
AXES = ("rows", "seq")
FLIP_Y, FLIP_CORE, FLIP_X, FLIP_Z = 1, 2, 4, 8
MODEL, FEED, OWN, WINDOW, HALF_SOURCE = 512, 2048, 512, 256, 192
KEYS, SOURCES = OWN + WINDOW, 2 * HALF_SOURCE
TILE = 128
MASKED = -1000000000.0
SCALE = HD ** (-0.5)


def exchange(value, flip):
    return lax.ppermute(value, AXES, [(device, device ^ flip) for device in range(32)])


def exchange_side(value, step):
    flips = (FLIP_X, FLIP_Y) if step == 0 else (FLIP_Y, FLIP_X)
    return lax.ppermute(value, AXES, [(device, device ^ flips[device >> 1 & 1]) for device in range(32)])


def tied(values, *others):
    return lax.optimization_barrier((values, others))[0]


def along_z(block):
    return [exchange(block, FLIP_Z * i) for i in Z_ORDER]


Z_ORDER = (1, 2, 3)


def join(*parts):
    return jnp.concatenate(parts, 0)


def both_cores(halves):
    return halves + [exchange(half, FLIP_CORE) for half in halves]


def add_halves(kept, came):
    half = kept.shape[0] // 2
    return kept[half:] + came[half:], kept[:half] + came[:half]


def z_blocks(both):
    size = both.shape[0] // 4
    blocks = [both[size * i : size * (i + 1)] for i in range(4)]
    return [blocks[0]] + [exchange(block, FLIP_Z * i) for i, block in zip(Z_ORDER, blocks[1:])]


def block_places(me):
    out = []
    for other in (0, 1):
        core = (me >> 1 & 1) ^ other
        first, second = FLIP_X - 3 * core, FLIP_Y + 3 * core
        for b in (0, 1):
            for a in (0, 1):
                for i, z in enumerate((0,) + Z_ORDER):
                    owner = me ^ (other * FLIP_CORE + b * second + a * first + z * FLIP_Z)
                    out.append((other * 2 + b, a * 4 + i, owner))
    return out


def nn(left, right):
    return jnp.dot(left, right, preferred_element_type=F32)


def block_rows(owner, size=BLOCK):
    return pl.ds(pl.multiple_of(owner * size, size), size)


def load_blocks(me, pieces, columns, target):
    for piece, row, owner in block_places(me):
        target[block_rows(owner), :] = pieces[piece][row * BLOCK : (row + 1) * BLOCK, columns]


def store_blocks(me, source, targets, columns):
    for piece, row, owner in block_places(me):
        at = (piece % 2 * 8 + row) * BLOCK
        targets[piece // 2][at : at + BLOCK, columns] = source[block_rows(owner), :]


def normed_rows(value):
    centered = value - jnp.mean(value, -1, keepdims=True)
    inverse = lax.rsqrt(jnp.mean(centered * centered, -1, keepdims=True) + 1e-05)
    return centered * inverse, inverse


def norm_back_rows(upstream, normed, inverse, gain):
    scaled = upstream * gain
    first_mean = jnp.mean(scaled, -1, keepdims=True)
    second_mean = jnp.mean(scaled * normed, -1, keepdims=True)
    return inverse * (scaled - first_mean - normed * second_mean)


def column_sum(value):
    return jnp.sum(value, 0, keepdims=True)


def own_segments_of(index, segments):
    return jnp.where(index == 0, segments[:, :OWN], segments[:, OWN:]).astype(F32)


def key_segments_of(index, segments):
    near = jnp.where(index == 0, segments[:, OWN:KEYS], segments[:, OWN - WINDOW : OWN])
    return jnp.concatenate([own_segments_of(index, segments), near.astype(F32)], 1)


def spread(row):
    return jnp.broadcast_to(row, (TILE, row.shape[1])).T


def lane_half(shape, half):
    lanes = lax.broadcasted_iota(jnp.int32, shape, 1)
    return (lanes < HD) if half == 0 else (lanes >= HD)


def half_masks(value):
    keep, zero = lane_half(value.shape, 0), jnp.zeros_like(value)
    return jnp.concatenate([jnp.where(keep, value, zero), jnp.where(keep, zero, value)], 0)


def self_jobs(side):
    near, far = pl.multiple_of((1 - side) * 256, 256), pl.multiple_of(side * 256, 256)
    skip_near, skip_far = pl.multiple_of((1 - side) * TILE, TILE), pl.multiple_of(side * TILE, TILE)
    return [
        (pl.ds(near, 256), [(skip_near, 384), (OWN, WINDOW)], 256),
        (pl.ds(far, 256), [(skip_far, 384)], 256),
    ]


def attend(queries, pair_ref, mixed, log_rows, query_seg, key_row, jobs):
    for rows, spans, size in jobs:

        def keys_of(ref, lanes):
            parts = [ref[pl.ds(start, count), lanes] for start, count in spans]
            return parts[0] if len(parts) == 1 else jnp.concatenate(parts, 0)

        segments = [key_row[:, pl.ds(start, count)] for start, count in spans]
        segments = segments[0] if len(segments) == 1 else jnp.concatenate(segments, 1)
        same = jnp.concatenate([query_seg[rows, :]] * (segments.shape[1] // TILE), 1) == segments
        bias = jnp.where(same, 0.0, MASKED)
        lanes = lax.broadcasted_iota(jnp.int32, (size, TILE), 1)
        logs = jnp.zeros((size, TILE), F32)
        for pair in range(HEADS // 2):
            at = slice(pair * TILE, (pair + 1) * TILE)
            scores = against(half_masks(queries[rows, at]), keys_of(pair_ref, at))
            weights, scales = [], []
            for half in range(2):
                part = scores[half * size : (half + 1) * size] + bias
                top = jnp.max(part, -1, keepdims=True)
                part = jnp.exp(part - top)
                total = jnp.sum(part, -1, keepdims=True)
                weights.append(part.astype(BF16))
                scales.append(1.0 / total)
                logs = jnp.where(lanes == pair * 2 + half, top + jnp.log(total), logs)
            values = keys_of(pair_ref, slice(MODEL + pair * TILE, MODEL + (pair + 1) * TILE))
            out = nn(jnp.concatenate(weights, 0), values)
            keep = lane_half((size, TILE), 0)
            mixed[rows, at] = jnp.where(keep, out[:size] * scales[0], out[size:] * scales[1]).astype(BF16)
        log_rows[:, rows] = logs.T[:HEADS]


def head_dots(upstream, mixed):
    head = lax.broadcasted_iota(jnp.int32, (HEADS, MODEL), 1) // HD
    ones = (head == lax.broadcasted_iota(jnp.int32, (HEADS, MODEL), 0)).astype(F32)
    return lax.dot_general(
        ones, upstream.astype(F32) * mixed.astype(F32), (((1,), (1,)), ((), ())),
        precision=lax.Precision.HIGHEST, preferred_element_type=F32,
    )


def attend_back(queries, upstream, pair_ref, log_rows, dot_rows, query_row, key_seg, query_grad, pair_grad, jobs):
    query_grad[...] = jnp.zeros_like(query_grad)
    for key_start, size, start, count in jobs:
        rows, across = pl.ds(key_start, size), pl.ds(start, count)

        def heads(step, unused):
            same = jnp.concatenate([key_seg[rows, :]] * (count // TILE), 1) == query_row[:, across]
            bias = jnp.where(same, 0.0, MASKED)
            for pair in (step * 2, step * 2 + 1):
                at = pl.ds(pl.multiple_of(pair * TILE, TILE), TILE)
                value_at = pl.ds(pl.multiple_of(MODEL + pair * TILE, TILE), TILE)
                query = queries[across, at]
                grad = upstream[across, at]
                keys = half_masks(pair_ref[rows, at])
                values = half_masks(pair_ref[rows, value_at])
                scores, grads = against(keys, query), against(values, grad)
                weights, score_grads = [], []
                for half in range(2):
                    head, part = pl.ds(pair * 2 + half, 1), slice(half * size, (half + 1) * size)
                    weight = jnp.exp(scores[part] + (bias - log_rows[head, across]))
                    score_grads.append((weight * (grads[part] - dot_rows[head, across])).astype(BF16))
                    weights.append(weight.astype(BF16))
                score_grad = jnp.concatenate(score_grads, 0)
                value_part = nn(jnp.concatenate(weights, 0), grad)
                key_part = nn(score_grad, query)
                query_grad[across, at] += transposed(score_grad, keys)
                keep = lane_half((size, TILE), 0)
                pair_grad[rows, at] = jnp.where(keep, key_part[:size], key_part[size:]).astype(BF16)
                pair_grad[rows, value_at] = jnp.where(keep, value_part[:size], value_part[size:]).astype(BF16)
            return unused

        lax.fori_loop(0, HEADS // 4, heads, 0)


def self_back_jobs(side):
    near = pl.multiple_of((1 - side) * 256, 256)
    return [(0, 256, 0, 384), (256, 256, TILE, 384), (OWN, WINDOW, near, 256)]


def pack_body(
    place, vectors, project, output, query, keyval, crossout, up, down, states, source,
    one, three, near, own_source, block, semaphores
):
    me, side = place[0], place[1]
    copies = [
        (project, one.at[:, :1536]),
        (output, one.at[:, 1664:2176]),
        (query, one.at[:, 2176:2688]),
        (keyval, one.at[:, 2688:3712]),
        (crossout, one.at[:, 3712:]),
        (down, three.at[64:]),
    ] + [
        (up.at[:, part * 512 : (part + 1) * 512], three.at[part * BLOCK : (part + 1) * BLOCK, :])
        for part in range(4)
    ] + [
        (states.at[pl.ds(pl.multiple_of((1 - side) * WINDOW, WINDOW), WINDOW), :], near.at[:WINDOW])
    ]
    copies = [pltpu.make_async_copy(*copy, semaphores.at[i]) for i, copy in enumerate(copies)]
    for copy in copies:
        copy.start()
    gap = jnp.zeros((HALF_SOURCE - source.shape[0], MODEL), F32)
    padded = jnp.concatenate([source[...].astype(F32), gap], 0).astype(BF16)
    own_source[...] = padded
    near[WINDOW:, :] = padded
    values = jnp.broadcast_to(vectors[...].astype(F32), (8, 256))
    lanes = lax.broadcasted_iota(jnp.int32, (8, TILE), 1)
    rows = lax.broadcasted_iota(jnp.int32, (8, TILE), 0)
    packed = jnp.zeros((8, TILE), F32)
    spot, wide = (me & 7) * 16, (me & 1) * 64
    for row in range(7):
        moved = pltpu.roll(values, spot + 256 - 16 * row, 1)[:, :TILE]
        inside = jnp.logical_and(lanes >= spot, lanes < spot + 16)
        packed = jnp.where(jnp.logical_and(rows == row, inside), moved, packed)
    moved = pltpu.roll(values, wide + 256 - 112, 1)[:, :TILE]
    inside = jnp.logical_and(lanes >= wide, lanes < wide + 64)
    packed = jnp.where(jnp.logical_and(rows == 7, inside), moved, packed)
    block[...] = jnp.concatenate([packed, jnp.zeros((8, TILE), F32)], 0).astype(BF16)
    last = pltpu.make_async_copy(block, one.at[:, 1536:1664], semaphores.at[len(copies)])
    last.start()
    for copy in copies + [last]:
        copy.wait()


def self_body(place, states, window, *refs):
    pieces, refs = refs[:4], refs[4:]
    queries, pair, lowered, vectors, up_bias, weight, weight_two, packed = refs
    me = place[0]
    load_blocks(me, pieces, slice(1536, 1664), packed)
    load_blocks(me, pieces, slice(0, 1536), weight)
    load_blocks(me, pieces, slice(1664, 4224), weight_two)
    for tile in range(4):
        total = jnp.zeros((8, TILE), F32)
        for i in range(8):
            total = total + packed[(tile * 8 + i) * BLOCK : (tile * 8 + i + 1) * BLOCK, :].astype(F32)[:8]
        vectors[:, tile * TILE : (tile + 1) * TILE] = total
    for tile in range(16):
        total = (
            packed[2 * tile * BLOCK : (2 * tile + 1) * BLOCK, :].astype(F32)
            + packed[(2 * tile + 1) * BLOCK : (2 * tile + 2) * BLOCK, :].astype(F32)
        )
        up_bias[:, tile * TILE : (tile + 1) * TILE] = total[7:8]
    gain, shift = vectors[1:2, :], vectors[2:3, :]
    for i in range(KEYS // TILE):
        rows = slice(i * TILE, (i + 1) * TILE)
        value = states[rows, :] if i < 4 else window[(i - 4) * TILE : (i - 3) * TILE, :]
        lowered[rows, :] = (normed_rows(value.astype(F32))[0] * gain + shift).astype(BF16)
    for i in range(KEYS // 256):
        rows = slice(i * 256, (i + 1) * 256)
        if i < 2:
            queries[rows, :] = (nn(lowered[rows, :], weight[:, :512]) .astype(BF16) * SCALE).astype(BF16)
        pair[rows, :] = nn(lowered[rows, :], weight[:, 512:]).astype(BF16)


def forward_body(
    place, segments, source_segments, states, own_source, other_source, vectors, weight, self_queries, self_pair,
    self_mixed, self_logs, after_self, lowered, queries, pair, mixed, logs, after_cross,
    query_seg, key_row, source_row, source,
):
    self_mix(place, segments, self_queries, self_pair, self_mixed, self_logs, query_seg, key_row)
    cross_lower(
        place, states, own_source, other_source, self_mixed, vectors, after_self, lowered, queries, pair, weight, source
    )
    source_row[...] = source_segments[...].astype(F32)
    attend(queries, pair, mixed, logs, query_seg, source_row, [(pl.ds(0, OWN), [(0, SOURCES)], OWN)])
    for i in range(2):
        rows = slice(i * 256, (i + 1) * 256)
        after_cross[rows, :] = after_self[rows, :] + nn(mixed[rows, :], weight[:, 2048:])


def self_mix(place, segments, queries, pair, mixed, log_rows, query_seg, key_row):
    query_seg[...] = spread(own_segments_of(place[1], segments[...]))
    key_row[...] = key_segments_of(place[1], segments[...])
    attend(queries, pair, mixed, log_rows, query_seg, key_row, self_jobs(place[1]))


def cross_lower(
    place, states, own_source, other_source, self_mixed, vectors, after_self, lowered, queries, pair, weight, source
):
    side = place[1]
    source[:HALF_SOURCE, :] = jnp.where(side == 0, own_source[...], other_source[...])
    source[HALF_SOURCE:, :] = jnp.where(side == 0, other_source[...], own_source[...])
    gain, shift = vectors[3:4, :], vectors[4:5, :]
    pair[...] = nn(source[...], weight[:, 1024:2048]).astype(BF16)
    for i in range(2):
        rows = slice(i * 256, (i + 1) * 256)
        value = states[rows, :].astype(F32) + nn(self_mixed[rows, :], weight[:, :512])
        after_self[rows, :] = value
        lowered[rows, :] = (normed_rows(value)[0] * gain + shift).astype(BF16)
        queries[rows, :] = (nn(lowered[rows, :], weight[:, 512:1024]).astype(BF16) * SCALE).astype(BF16)


CHUNK, UNROLL = 512, 2


def feed_body(place, after_cross, output_grad, vectors, up_bias, *refs):
    pieces, refs = refs[:4], refs[4:]
    (
        total, back, kept, sent, bias_sums, ups, downs, lowered, flipped, up_grads, down_grads,
    ) = refs
    me = place[0]
    places = block_places(me)

    def chunk_of(z):
        return pl.multiple_of(((me >> 3) ^ z) * CHUNK, CHUNK)

    gain, shift = vectors[5:6, :], vectors[6:7, :]
    for i in range(4):
        rows = slice(i * TILE, (i + 1) * TILE)
        low = (normed_rows(after_cross[rows, :])[0] * gain + shift).astype(BF16)
        lowered[rows, :] = low
    flipped[...] = lowered[...].T
    grad_low = output_grad[...]
    total[...] = jnp.zeros_like(total)
    back[...] = jnp.zeros_like(back)

    def chunk(z):
        at = pl.ds(chunk_of(z), CHUNK)
        z_row = ((me >> 3) ^ z) * BLOCK
        up, down, up_grad, down_grad = ups.at[z], downs.at[z], up_grads.at[z], down_grads.at[z]
        for piece, row, owner in places:
            up[block_rows(owner), :] = pieces[piece][pl.ds(pl.multiple_of(row * 128 + z_row, BLOCK), BLOCK), :]
            if row % 4 == 0:
                start = pl.multiple_of((row + z) * 128 + 64, 64)
                down[block_rows(owner & 7, 64), :] = pieces[piece][pl.ds(start, 64), :]
        hidden = nn(lowered[...], up[...]) + up_bias[:, at]
        square = hidden * hidden
        inner = 0.7978845608028654 * hidden * (1.0 + 0.044715 * square)
        curve = jnp.tanh(inner)
        half = 0.5 * (1.0 + curve)
        activated = (hidden * half).astype(BF16)
        slope = half + (0.5 * 0.7978845608028654) * hidden * (1.0 - curve * curve) * (
            1.0 + (3 * 0.044715) * square
        )
        down_grad[...] = transposed(activated, grad_low).astype(BF16)
        for piece, row, owner in places:
            if row % 4 == 0:
                to = pl.multiple_of((piece % 2 * 8 + row + z) * 128 + 64, 64)
                (kept, sent)[piece // 2][pl.ds(to, 64), :] = down_grad[block_rows(owner & 7, 64), :]
        grad_hidden = (against(grad_low, down[...]) * slope).astype(BF16)
        bias_sums[:, at] = column_sum(grad_hidden.astype(F32))
        up_grad[...] = nn(flipped[...], grad_hidden).astype(BF16)
        for piece, row, owner in places:
            to = (piece % 2 * 8 + row) * 128
            (kept, sent)[piece // 2][pl.ds(pl.multiple_of(to + z_row, BLOCK), BLOCK), :] = up_grad[block_rows(owner), :]
        total[...] += nn(activated, down[...])
        back[...] += against(grad_hidden, up[...])

    def chunks(step, unused):
        for z in range(UNROLL):
            chunk(step * UNROLL + z)
        return unused

    lax.fori_loop(0, 4 // UNROLL, chunks, 0)


def feed_last_body(place, after_cross, output_grad, vectors, total, back, layer_out, after_grad, sums):
    gain = vectors[5:6, :]
    gain_sum, shift_sum, bias_sum = (jnp.zeros((1, MODEL), F32) for _ in range(3))
    for i in range(4):
        rows = slice(i * TILE, (i + 1) * TILE)
        value, grad = after_cross[rows, :], output_grad[rows, :].astype(F32)
        layer_out[rows, :] = (value + total[rows, :] + vectors[0:1, :]).astype(BF16)
        normed, inverse = normed_rows(value)
        upstream = back[rows, :]
        after_grad[rows, :] = grad + norm_back_rows(upstream, normed, inverse, gain)
        gain_sum, shift_sum = gain_sum + column_sum(upstream * normed), shift_sum + column_sum(upstream)
        bias_sum = bias_sum + column_sum(grad)
    zero = jnp.zeros((1, MODEL), F32)
    sums[...] = jnp.concatenate([bias_sum, zero, zero, zero, zero, gain_sum, shift_sum, zero], 0)


def cross_back_body(
    place, segments, source_segments, own_source, other_source, queries, pair, mixed, log_rows, after_grad, weight,
    asked, source_own, source_send, grads, upstream, query_grad, pair_grad, source, key_seg, query_row,
    dot_rows,
):
    side = place[1]
    key_seg[...] = spread(source_segments[...].astype(F32))
    query_row[...] = own_segments_of(side, segments[...])
    source[:HALF_SOURCE, :] = jnp.where(side == 0, own_source[...], other_source[...])
    source[HALF_SOURCE:, :] = jnp.where(side == 0, other_source[...], own_source[...])
    grad_low = after_grad[...].astype(BF16)
    upstream[...] = against(grad_low, weight[:, 2048:]).astype(BF16)
    dot_rows[...] = head_dots(upstream[...], mixed[...])
    grads[:, :512] = transposed(mixed[...], grad_low).astype(BF16)
    attend_back(
        queries, upstream, pair, log_rows, dot_rows, query_row, key_seg, query_grad, pair_grad,
        [(0, SOURCES, 0, OWN)],
    )
    asked[...] = (query_grad[...] * SCALE).astype(BF16)
    grads[:, 512:] = transposed(source[...], pair_grad[...]).astype(BF16)
    back = against(pair_grad[...], weight[:, 1024:2048])
    first, second = back[:HALF_SOURCE], back[HALF_SOURCE:]
    source_own[...] = jnp.where(side == 0, first, second)
    source_send[...] = jnp.where(side == 0, second, first).astype(BF16)


def cross_weight_body(
    place, after_self, lowered, self_mixed, after_grad, asked, vectors, sums, weight, some_grads, *refs
):
    self_grad, upstream, dot_rows, kept, sent, new_sums, grads = refs
    me = place[0]
    store_blocks(me, some_grads, (kept, sent), slice(0, 1536))
    gain = vectors[3:4, :]
    gain_sum, shift_sum = jnp.zeros((1, MODEL), F32), jnp.zeros((1, MODEL), F32)
    for i in range(2):
        rows = slice(i * 256, (i + 1) * 256)
        normed, inverse = normed_rows(after_self[rows, :])
        up = against(asked[rows, :], weight[:, 512:1024])
        self_grad[rows, :] = after_grad[rows, :] + norm_back_rows(up, normed, inverse, gain)
        gain_sum, shift_sum = gain_sum + column_sum(up * normed), shift_sum + column_sum(up)
    grads[:, :512] = transposed(lowered[...], asked[...]).astype(BF16)
    grad_low = self_grad[...].astype(BF16)
    grads[:, 512:] = transposed(self_mixed[...], grad_low).astype(BF16)
    store_blocks(me, grads, (kept, sent), slice(1536, 2560))
    upstream[...] = against(grad_low, weight[:, :512]).astype(BF16)
    dot_rows[...] = head_dots(upstream[...], self_mixed[...])
    zero = jnp.zeros((1, MODEL), F32)
    new_sums[...] = sums[...] + jnp.concatenate(
        [zero, zero, zero, gain_sum, shift_sum, zero, zero, zero], 0
    )


def self_back_body(
    place, segments, states, window, lowered, queries, pair, log_rows, upstream, dot_rows, weight, sums, bias_sums,
    source_send, own_back, near_back, kept, sent, query_grad, pair_grad, grads, key_seg, query_row,
):
    near_back[WINDOW:, :] = source_send[...]
    key_seg[...] = spread(key_segments_of(place[1], segments[...]))
    query_row[...] = own_segments_of(place[1], segments[...])
    attend_back(
        queries, upstream, pair, log_rows, dot_rows, query_row, key_seg, query_grad, pair_grad,
        self_back_jobs(place[1]),
    )
    asked = (query_grad[...] * SCALE).astype(BF16)
    grads[:, :MODEL] = transposed(lowered[:OWN, :], asked).astype(BF16)
    grads[:, MODEL:1536] = transposed(lowered[...], pair_grad[...]).astype(BF16)
    gain_sum, shift_sum = jnp.zeros((1, MODEL), F32), jnp.zeros((1, MODEL), F32)
    for i in range(3):
        rows = slice(i * 256, (i + 1) * 256)
        part = against(pair_grad[rows, :], weight[:, MODEL:])
        if i < 2:
            part = part + against(asked[rows, :], weight[:, :MODEL])
            own_back[rows, :] = part
            value = states[rows, :]
        else:
            near_back[:WINDOW, :] = part.astype(BF16)
            value = window[...]
        normed = normed_rows(value.astype(F32))[0]
        gain_sum, shift_sum = gain_sum + column_sum(part * normed), shift_sum + column_sum(part)
    zero = jnp.zeros((1, MODEL), F32)
    sums = sums[...] + jnp.concatenate([zero, gain_sum, shift_sum, zero, zero, zero, zero, zero], 0)
    last = lax.broadcasted_iota(jnp.int32, (8, TILE), 0) == 7
    for device in range(32):
        tile, wide = device // 8 * TILE, device // 2 * TILE
        value = jnp.where(last, bias_sums[:, wide : wide + TILE], sums[:, tile : tile + TILE])
        high = value.astype(BF16).astype(F32)
        grads[device * BLOCK : (device + 1) * BLOCK, 1536:] = jnp.concatenate([high, value - high], 0).astype(BF16)
    store_blocks(place[0], grads, (kept, sent), slice(0, 1664))


def target_body(place, back, came, states, self_grad, vectors, out):
    gain = vectors[1:2, :]
    for i in range(4):
        rows = slice(i * TILE, (i + 1) * TILE)
        here = (i < 2) == (place[1] == 1)
        extra = came[(i % 2) * TILE : (i % 2 + 1) * TILE, :].astype(F32)
        upstream = back[rows, :] + jnp.where(here, extra, 0.0)
        normed, inverse = normed_rows(states[rows, :].astype(F32))
        out[rows, :] = self_grad[rows, :] + norm_back_rows(upstream, normed, inverse, gain)


def finish_body(place, *refs):
    feed, cross, last, outs = refs[:4], refs[4:8], refs[8:12], refs[12:]
    project, output, query, keyval, crossout, up, down, *small = outs
    me = place[0]

    def total(parts, begin, end, rows=slice(None)):
        value = parts[0][rows, begin:end].astype(F32)
        for part in parts[1:]:
            value = value + part[rows, begin:end].astype(F32)
        return value

    for part in range(4):
        rows = slice(part * BLOCK, (part + 1) * BLOCK)
        up[:, part * 512 : (part + 1) * 512] = total(feed, 0, MODEL, rows)
    down[...] = total(feed, 0, MODEL, slice(64, 128))
    crossout[...] = total(cross, 0, 512)
    keyval[...] = total(cross, 512, 1536)
    query[...] = total(cross, 1536, 2048)
    output[...] = total(cross, 2048, 2560)
    project[...] = total(last, 0, 1536)
    value = total(last, 1536, 1664)
    value = value[:8] + value[8:]
    narrow = pltpu.roll(value, (TILE - (me & 7) * 16) & 127, 1)
    wide = pltpu.roll(value, (TILE - (me & 1) * 64) & 127, 1)
    for row in range(7):
        small[row][...] = narrow[row : row + 1, :16]
    small[7][...] = wide[7:8, :64]


def shape_of(*shape, dtype=BF16):
    return jax.ShapeDtypeStruct(shape, dtype)


VMEM_SPEC = pl.BlockSpec(memory_space=pltpu.VMEM)
ANY_SPEC = pl.BlockSpec(memory_space=pl.ANY)
HBM_SPEC = pl.BlockSpec(memory_space=pltpu.HBM)
SMEM_SPEC = pl.BlockSpec(memory_space=pltpu.SMEM)


def call(body, name, place, inputs, pieces, outs, scratch, flops, any_outs=(), any_ins=(), vmem=40):
    return pl.pallas_call(
        body,
        name=name,
        out_shape=outs,
        in_specs=[SMEM_SPEC]
        + [HBM_SPEC if i in any_ins else VMEM_SPEC for i in range(len(inputs))]
        + [VMEM_SPEC] * len(pieces),
        out_specs=[ANY_SPEC if i in any_outs else VMEM_SPEC for i in range(len(outs))],
        scratch_shapes=scratch,
        compiler_params=pltpu.CompilerParams(vmem_limit_bytes=vmem * 2**20),
        cost_estimate=pl.CostEstimate(flops=flops, bytes_accessed=4 * 2**20, transcendentals=0),
    )(place, *inputs, *pieces)


def fast_device(
    target_states, source_states, target_segments, source_segments, output_grad, self_project,
    self_output, cross_query, cross_keyval, cross_output, hidden_up, hidden_bias, hidden_down,
    output_bias, first_gain, first_shift, second_gain, second_shift, third_gain, third_shift,
):
    vmem, dma = pltpu.VMEM, pltpu.SemaphoreType.DMA
    side = lax.axis_index("seq")
    place = jnp.stack([lax.axis_index("rows") * 2 + side, side]).astype(jnp.int32)
    states, grad = target_states[0], output_grad[0]
    small = jnp.pad(hidden_bias, (112, 80))
    for i, vector in enumerate(
        (output_bias, first_gain, first_shift, second_gain, second_shift, third_gain, third_shift)
    ):
        small = small + jnp.pad(vector, (16 * i, 240 - 16 * i))
    small = small.reshape(1, 256)
    one, three, near, own_source = call(
        pack_body, "pack", place,
        [
            small, self_project, self_output, cross_query, cross_keyval, cross_output, hidden_up, hidden_down, states,
            source_states[0],
        ],
        [],
        [
            shape_of(16, 4224), shape_of(128, MODEL), shape_of(WINDOW + HALF_SOURCE, MODEL),
            shape_of(HALF_SOURCE, MODEL),
        ],
        [vmem((BLOCK, TILE), BF16), dma((12,))], 1000000, any_ins=range(1, 9), vmem=60,
    )
    parts = along_z(one)
    near = exchange(near, FLIP_Y)
    one = join(one, *parts)
    one = tied(one, near)
    came = exchange_side(one, 0)
    three, one = tied((three, one), came)
    parts_three = along_z(three)
    one = join(one, came)
    one_core = exchange(one, FLIP_CORE)
    other = exchange_side(one, 1)
    other = tied(other, parts_three)
    window, other_source = near[:WINDOW], near[WINDOW:]
    pieces_one = [one, other, one_core, exchange(other, FLIP_CORE)]
    three = join(three, *parts_three)
    came = exchange_side(three, 0)
    half = source_states.shape[1]
    gap = jnp.full((1, HALF_SOURCE - half), -1, jnp.int32)
    source_seg = jnp.concatenate([source_segments[:, :half], gap, source_segments[:, half:], gap], 1)

    queries, pair, lowered, vectors, up_bias, weight_one, weight_two = call(
        self_body, "self_lower", place, [states, window], pieces_one,
        [
            shape_of(OWN, MODEL), shape_of(KEYS, 2 * MODEL), shape_of(KEYS, MODEL), shape_of(8, MODEL, dtype=F32),
            shape_of(1, FEED, dtype=F32), shape_of(MODEL, 1536), shape_of(MODEL, 2560),
        ],
        [vmem((MODEL, TILE), BF16)], 5000000000,
    )
    came, three = tied((came, three), queries)
    three = join(three, came)
    three_core = exchange(three, FLIP_CORE)
    other = exchange_side(three, 1)
    queries = tied(queries, three)
    mixed, logs, after_self, lowered_two, queries_two, pair_two, mixed_two, logs_two, after_cross = call(
        forward_body, "forward", place,
        [
            target_segments, source_seg, states, own_source, other_source, vectors, weight_two, queries, pair,
        ],
        [],
        [
            shape_of(OWN, MODEL), shape_of(HEADS, OWN, dtype=F32), shape_of(OWN, MODEL, dtype=F32), shape_of(OWN, MODEL),
            shape_of(OWN, MODEL), shape_of(SOURCES, 2 * MODEL), shape_of(OWN, MODEL), shape_of(HEADS, OWN, dtype=F32),
            shape_of(OWN, MODEL, dtype=F32),
        ],
        [
            vmem((OWN, TILE), F32), vmem((1, KEYS), F32), vmem((1, SOURCES), F32), vmem((SOURCES, MODEL), BF16),
        ],
        20000000000,
    )
    three_core, other = tied((three_core, other), after_cross)
    pieces_three = [three, other, three_core, exchange(other, FLIP_CORE)]
    total, back, feed_kept, feed_sent, bias_sums = call(
        feed_body, "feed", place, [after_cross, grad, vectors, up_bias], pieces_three,
        [shape_of(OWN, MODEL, dtype=F32)] * 2 + [shape_of(2048, MODEL)] * 2 + [shape_of(1, FEED, dtype=F32)],
        [
            vmem((4, MODEL, CHUNK), BF16), vmem((4, CHUNK, MODEL), BF16), vmem((OWN, MODEL), BF16),
            vmem((MODEL, OWN), BF16), vmem((4, MODEL, CHUNK), BF16), vmem((4, CHUNK, MODEL), BF16),
        ],
        10000000000,
    )
    feed_came = exchange(feed_sent, FLIP_CORE)
    layer_out, after_grad, sums = call(
        feed_last_body, "feed_last", place, [after_cross, grad, vectors, total, back], [],
        [shape_of(OWN, MODEL), shape_of(OWN, MODEL, dtype=F32), shape_of(8, MODEL, dtype=F32)], [], 2000000000,
    )
    feed_came = tied(feed_came, after_grad)
    feed_sent, feed_kept = add_halves(feed_kept, feed_came)
    after_grad = tied(after_grad, feed_sent)
    feed_came = exchange_side(feed_sent, 1)
    asked, source_own, source_send, some_grads = call(
        cross_back_body, "cross_backward", place,
        [
            target_segments, source_seg, own_source, other_source, queries_two, pair_two, mixed_two, logs_two,
            after_grad, weight_two,
        ],
        [],
        [
            shape_of(OWN, MODEL), shape_of(HALF_SOURCE, MODEL, dtype=F32), shape_of(HALF_SOURCE, MODEL),
            shape_of(MODEL, 1536),
        ],
        [
            vmem((OWN, MODEL), BF16), vmem((OWN, MODEL), F32), vmem((SOURCES, 2 * MODEL), BF16),
            vmem((SOURCES, MODEL), BF16), vmem((SOURCES, TILE), F32), vmem((1, OWN), F32), vmem((HEADS, OWN), F32),
        ],
        10000000000,
    )
    self_grad, upstream, dot_rows, cross_kept, cross_sent, sums = call(
        cross_weight_body, "cross_weights", place,
        [after_self, lowered_two, mixed, after_grad, asked, vectors, sums, weight_two, some_grads], [],
        [shape_of(OWN, MODEL, dtype=F32), shape_of(OWN, MODEL), shape_of(HEADS, OWN, dtype=F32)]
        + [shape_of(256, 2560)] * 2 + [shape_of(8, MODEL, dtype=F32)],
        [vmem((MODEL, 1024), BF16)], 6000000000,
    )
    cross_came = exchange(cross_sent, FLIP_CORE)
    feed_came = tied(feed_came, upstream)
    feed_sent, feed_kept = add_halves(feed_kept, feed_came)
    feed_came = exchange_side(feed_sent, 0)
    cross_came = tied(cross_came, feed_sent)
    cross_sent, cross_kept = add_halves(cross_kept, cross_came)
    cross_came = exchange_side(cross_sent, 1)
    upstream = tied(upstream, cross_sent)
    own_back, near_back, last_kept, last_sent = call(
        self_back_body, "self_backward", place,
        [
            target_segments, states, window, lowered, queries, pair, logs, upstream, dot_rows, weight_one, sums,
            bias_sums, source_send,
        ],
        [],
        [shape_of(OWN, MODEL, dtype=F32), shape_of(WINDOW + HALF_SOURCE, MODEL)] + [shape_of(256, 1664)] * 2,
        [
            vmem((OWN, MODEL), F32), vmem((KEYS, 2 * MODEL), BF16), vmem((MODEL, 1664), BF16), vmem((KEYS, TILE), F32),
            vmem((1, OWN), F32),
        ],
        16000000000,
    )
    last_came = exchange(last_sent, FLIP_CORE)
    cross_came, feed_came = tied((cross_came, feed_came), own_back)
    cross_sent, cross_kept = add_halves(cross_kept, cross_came)
    last_sent, last_kept = add_halves(last_kept, last_came)
    last_came, cross_came = exchange_side(last_sent, 1), exchange_side(cross_sent, 0)
    feed_came = tied(feed_came, last_sent)
    feed = z_blocks(feed_kept + feed_came)
    last_came = tied(last_came, feed[0])
    last_sent, last_kept = add_halves(last_kept, last_came)
    last_came = exchange_side(last_sent, 0)
    cross_came, feed, near_back = tied((cross_came, feed, near_back), last_sent)
    cross_kept = tied(cross_kept, feed)
    cross = z_blocks(cross_kept + cross_came)
    near_came = exchange(near_back, FLIP_Y)
    last_came = tied(last_came, cross[0])
    last = z_blocks(last_kept + last_came)
    came, source_came = near_came[:WINDOW], near_came[WINDOW:]
    grad_source = source_own[:half] + source_came[:half].astype(F32)
    (grad_target,) = call(
        target_body, "target_grad", place, [own_back, came, states, self_grad, vectors], [],
        [shape_of(OWN, MODEL, dtype=F32)], [], 1000000,
    )
    project, output, query, keyval, crossout, up, down, *small = call(
        finish_body, "finish", place, feed + cross + last, [],
        [
            shape_of(16, 1536, dtype=F32), shape_of(16, 512, dtype=F32), shape_of(16, 512, dtype=F32),
            shape_of(16, 1024, dtype=F32), shape_of(16, 512, dtype=F32), shape_of(16, 2048, dtype=F32),
            shape_of(64, 512, dtype=F32),
        ]
        + [shape_of(1, 16, dtype=F32)] * 7 + [shape_of(1, 64, dtype=F32)],
        [], 1000000,
    )
    *rows, up_sum = [row[0] for row in small]
    return (
        layer_out[None], grad_target[None], grad_source[None], project, output, query, keyval, crossout, up,
        up_sum, down, *rows,
    )


def specs():
    in_specs = (
        P("rows", "seq", None),
        P("rows", "seq", None),
        P("rows", None),
        P("rows", None),
        P("rows", "seq", None),
        P(("rows", "seq"), None),
        P(("rows", "seq"), None),
        P(("rows", "seq"), None),
        P(("rows", "seq"), None),
        P(("rows", "seq"), None),
        P(("rows", "seq"), None),
        P(("rows", "seq")),
        P(("rows", "seq"), None),
        P(("rows", "seq")),
        P(("rows", "seq")),
        P(("rows", "seq")),
        P(("rows", "seq")),
        P(("rows", "seq")),
        P(("rows", "seq")),
        P(("rows", "seq")),
    )
    out_specs = (
        P("rows", "seq", None),
        P("rows", "seq", None),
        P("rows", "seq", None),
        P(("rows", "seq"), None),
        P(("rows", "seq"), None),
        P(("rows", "seq"), None),
        P(("rows", "seq"), None),
        P(("rows", "seq"), None),
        P(("rows", "seq"), None),
        P(("rows", "seq")),
        P(("rows", "seq"), None),
        P(("rows", "seq")),
        P(("rows", "seq")),
        P(("rows", "seq")),
        P(("rows", "seq")),
        P(("rows", "seq")),
        P(("rows", "seq")),
        P(("rows", "seq")),
    )
    return in_specs, out_specs


def solution(mesh):
    in_specs, out_specs = specs()
    fast = mesh.shape["rows"] == 16 and mesh.shape["seq"] == 2
    return jax.shard_map(
        fast_device if fast else general_device,
        mesh=mesh, in_specs=in_specs, out_specs=out_specs, check_vma=False,
    )
```

profile of v0, /device:TPU:0, one launch (start us, length us, event | category | flops | bytes accessed | tf_op | source)
XLA Modules:
  0.0 161.5 jit_solution(17071463474625879015)
XLA Ops:
  0.7 0.9 pad_add_fusion.2
  1.5 0.6 reshape.39.vectors
  2.1 0.6 pad_add_fusion.1.place
  2.7 3.1 %pack.1 = (bf16[16,4224]{1,0:T(8,128)(2,1)}, bf16[128,512]{1,0:T(8,128)(2,1)}, bf16[448,512]{1,0:T(8,128)(2,1)}, bf16[192,512]{1,0:T(8,128)(2,1)}) custom-call(s32[2]{0:T(128)} %pad_add_fusion.1.place, bf16[1,256]{1,0:T(2,128)(2,1)} %reshape.39.vectors, bf16[16,1536]{1,0:T(8,128)(2,1)} %project.1, bf16[16,512]{1,0:T(8,128)(2,1)} %output.1, ...), custom_call_target="tpu_custom_call" | custom-call | flops 1000000 | bytes 4194304 | tf_op jit(solution)/shard_map/pack/pallas_call | solution.py:909
  5.8 5.1 %collective-permute-start.3 = (bf16[16,4224]{1,0:T(8,128)(2,1)}, bf16[16,4224]{1,0:T(8,128)(2,1)S(1)}, u32[]{:S(2)}, u32[]{:S(2)}) collective-permute-start(bf16[16,4224]{1,0:T(8,128)(2,1)} %get-tuple-element.104), channel_id=1, source_target_pairs={{0,24},{1,25},{2,26},{3,27},{4,28},{5,29},{6,30},{7,31},{8,16},{9,... | collective-permute-start | bytes 405512 | tf_op jit(solution)/shard_map/ppermute | solution.py:377
  10.9 0.6 collective-permute-start.1
  11.5 1.7 %collective-permute-start = (bf16[448,512]{1,0:T(8,128)(2,1)}, bf16[448,512]{1,0:T(8,128)(2,1)S(1)}, u32[]{:S(2)}, u32[]{:S(2)}) collective-permute-start(bf16[448,512]{1,0:T(8,128)(2,1)} %get-tuple-element.102), channel_id=1, source_target_pairs={{0,1},{1,0},{2,3},{3,2},{4,5},{5,4},{6,7},{7,6},{8,9},{9,8},{10,11... | collective-permute-start | bytes 1376264 | tf_op jit(solution)/shard_map/ppermute | solution.py:377
  13.2 2.4 %collective-permute-done.3 = bf16[16,4224]{1,0:T(8,128)(2,1)S(1)} collective-permute-done((bf16[16,4224]{1,0:T(8,128)(2,1)}, bf16[16,4224]{1,0:T(8,128)(2,1)S(1)}, u32[]{:S(2)}, u32[]{:S(2)}) %collective-permute-start.3) | collective-permute-done | bytes 135200 | tf_op jit(solution)/shard_map/ppermute | solution.py:377
  15.6 6.9 %collective-permute-done.2 = bf16[16,4224]{1,0:T(8,128)(2,1)S(1)} collective-permute-done((bf16[16,4224]{1,0:T(8,128)(2,1)}, bf16[16,4224]{1,0:T(8,128)(2,1)S(1)}, u32[]{:S(2)}, u32[]{:S(2)}) %collective-permute-start.2) | collective-permute-done | bytes 135200 | tf_op jit(solution)/shard_map/ppermute | solution.py:377
  22.5 0.9 pad_maximum_fusion
  23.5 1.6 collective-permute-start.4
  25.1 7.9 %collective-permute-done.4 = bf16[64,4224]{1,0:T(8,128)(2,1)S(1)} collective-permute-done((bf16[64,4224]{1,0:T(8,128)(2,1)S(1)}, bf16[64,4224]{1,0:T(8,128)(2,1)S(1)}, u32[]{:S(2)}, u32[]{:S(2)}) %collective-permute-start.4) | collective-permute-done | bytes 540704 | tf_op jit(solution)/shard_map/ppermute | solution.py:382
  33.0 1.6 collective-permute-start.5
  34.6 3.4 %collective-permute-start.8 = (bf16[128,512]{1,0:T(8,128)(2,1)S(1)}, bf16[128,512]{1,0:T(8,128)(2,1)S(1)}, u32[]{:S(2)}, u32[]{:S(2)}) collective-permute-start(bf16[128,512]{1,0:T(8,128)(2,1)S(1)} %copy-done.9), channel_id=1, source_target_pairs={{0,24},{1,25},{2,26},{3,27},{4,28},{5,29},{6,30},{7,31},{8,16},{9,... | collective-permute-start | bytes 393224 | tf_op jit(solution)/shard_map/ppermute | solution.py:377
  38.0 1.0 collective-permute-start.6
  39.0 3.6 %collective-permute-done.8 = bf16[128,512]{1,0:T(8,128)(2,1)S(1)} collective-permute-done((bf16[128,512]{1,0:T(8,128)(2,1)S(1)}, bf16[128,512]{1,0:T(8,128)(2,1)S(1)}, u32[]{:S(2)}, u32[]{:S(2)}) %collective-permute-start.8) | collective-permute-done | bytes 131104 | tf_op jit(solution)/shard_map/ppermute | solution.py:377
  42.7 4.2 %collective-permute-done.7 = bf16[128,512]{1,0:T(8,128)(2,1)S(1)} collective-permute-done((bf16[128,512]{1,0:T(8,128)(2,1)S(1)}, bf16[128,512]{1,0:T(8,128)(2,1)S(1)}, u32[]{:S(2)}, u32[]{:S(2)}) %collective-permute-start.7) | collective-permute-done | bytes 131104 | tf_op jit(solution)/shard_map/ppermute | solution.py:377
  46.8 1.4 collective-permute-done.5.refs_1_
  48.3 0.1 fusion.5
  48.4 1.6 collective-permute-start.11
  50.0 0.1 pad_add_fusion.source_segments
  50.1 0.9 collective-permute-done.10.refs_3_
  51.0 2.3 %self_lower.1 = (bf16[512,512]{1,0:T(8,128)(2,1)S(1)}, bf16[768,1024]{1,0:T(8,128)(2,1)S(1)}, bf16[768,512]{1,0:T(8,128)(2,1)S(1)}, f32[8,512]{1,0:T(8,128)S(1)}...) custom-call(s32[2]{0:T(128)S(1)} %copy-done.1, ...), custom_call_target="tpu_custom_call" | custom-call | flops 5000000000 | bytes 4194304 | tf_op jit(solution)/shard_map/self_lower/pallas_call | solution.py:909
  53.3 4.3 %collective-permute-done.11 = bf16[512,512]{1,0:T(8,128)(2,1)S(1)} collective-permute-done((bf16[512,512]{1,0:T(8,128)(2,1)S(1)}, bf16[512,512]{1,0:T(8,128)(2,1)S(1)}, u32[]{:S(2)}, u32[]{:S(2)}) %collective-permute-start.11) | collective-permute-done | bytes 524320 | tf_op jit(solution)/shard_map/ppermute | solution.py:382
  57.7 1.6 collective-permute-start.13
  59.3 9.4 %forward.1 = (bf16[512,512]{1,0:T(8,128)(2,1)S(1)}, f32[8,512]{1,0:T(8,128)S(1)}, f32[512,512]{1,0:T(8,128)S(1)}, bf16[512,512]{1,0:T(8,128)(2,1)S(1)}, bf16[512...) custom-call(s32[2]{0:T(128)S(1)} %copy-done.1, ...), custom_call_target="tpu_custom_call" | custom-call | flops 20000000000 | bytes 4194304 | tf_op jit(solution)/shard_map/forward/pallas_call | solution.py:909
  68.8 3.8 %collective-permute-done.13.refs_1_ = bf16[1024,512]{1,0:T(8,128)(2,1)S(1)} collective-permute-done((bf16[1024,512]{1,0:T(8,128)(2,1)S(1)}, bf16[1024,512]{1,0:T(8,128)(2,1)S(1)}, u32[]{:S(2)}, u32[]{:S(2)}) %collective-permute-start.13) | collective-permute-done | bytes 1048608 | tf_op jit(solution)/shard_map/ppermute | solution.py:382
  72.6 2.7 %collective-permute-done.14.refs_3_ = bf16[1024,512]{1,0:T(8,128)(2,1)S(1)} collective-permute-done((bf16[1024,512]{1,0:T(8,128)(2,1)S(1)}, bf16[1024,512]{1,0:T(8,128)(2,1)S(1)}, u32[]{:S(2)}, u32[]{:S(2)}) %collective-permute-start.14) | collective-permute-done | bytes 1048608 | tf_op jit(solution)/shard_map/ppermute | solution.py:377
  75.3 10.8 %feed.1 = (f32[512,512]{1,0:T(8,128)S(1)}, f32[512,512]{1,0:T(8,128)S(1)}, bf16[2048,512]{1,0:T(8,128)(2,1)S(1)}, bf16[2048,512]{1,0:T(8,128)(2,1)S(1)}, f32[1,2048]{1,0:T(1,128)S(1)}) custom-call(s32[2]{0:T(128)S(1)} %copy-done.1, f32[512,512]{1,0:T(8,128)S(1)} %get-tuple-element.116.after_cross, bf16[512,512]{1,0:T(8,128)(2,1)S(1)} %bitcast.22, ...), custom_call_target="tpu_custom_call" | custom-call | flops 10000000000 | bytes 4194304 | tf_op jit(solution)/shard_map/feed/pallas_call | solution.py:909
  86.1 0.2 collective-permute-start.15
  86.3 1.8 %feed_last.1 = (bf16[512,512]{1,0:T(8,128)(2,1)}, f32[512,512]{1,0:T(8,128)S(1)}, f32[8,512]{1,0:T(8,128)S(1)}) custom-call(s32[2]{0:T(128)S(1)} %copy-done.1, f32[512,512]{1,0:T(8,128)S(1)} %get-tuple-element.116.after_cross, bf16[512,512]{1,0:T(8,128)(2,1)S(1)} %bitcast.23, f32[8,512]{1,0:T(8,128)S(1)} %get-tuple-element.109.vectors, ...), custom_call_target="tpu_custom_call" | custom-call | flops 2000000000 | bytes 4194304 | tf_op jit(solution)/shard_map/feed_last/pallas_call | solution.py:909
  88.1 2.4 %collective-permute-done.15 = bf16[2048,512]{1,0:T(8,128)(2,1)} collective-permute-done((bf16[2048,512]{1,0:T(8,128)(2,1)S(1)}, bf16[2048,512]{1,0:T(8,128)(2,1)}, u32[]{:S(2)}, u32[]{:S(2)}) %collective-permute-start.15) | collective-permute-done | bytes 2097184 | tf_op jit(solution)/shard_map/ppermute | solution.py:377
  90.4 1.9 %slice_add_fusion = (bf16[1024,512]{1,0:T(8,128)(2,1)S(1)}, bf16[1024,512]{1,0:T(8,128)(2,1)S(1)}) fusion(bf16[2048,512]{1,0:T(8,128)(2,1)} %collective-permute-done.15, bf16[2048,512]{1,0:T(8,128)(2,1)S(1)} %get-tuple-element.129), kind=kLoop, calls=%fused_computation | loop fusion | flops 1048576 | bytes 6291456 | tf_op jit(solution)/shard_map/add | solution.py:406
  92.3 1.6 collective-permute-start.17
  93.9 8.7 %cross_backward.1 = (bf16[512,512]{1,0:T(8,128)(2,1)S(1)}, f32[192,512]{1,0:T(8,128)S(1)}, bf16[192,512]{1,0:T(8,128)(2,1)S(1)}, bf16[512,1536]{1,0:T(8,128)(2,1)S(1)}) custom-call(s32[2]{0:T(128)S(1)} %copy-done.1, s32[1,1024]{1,0:T(1,128)S(1)} %copy-done.4, s32[1,384]{1,0:T(1,128)S(1)} %pad_add_fusion.source_segments, bf16[192,512]{1,0:T(8,128)(2,1)S(1)} %copy-done.3, ...), custom_call_target="tpu_custom_call" | custom-call | flops 10000000000 | bytes 4194304 | tf_op jit(solution)/shard_map/cross_backward/pallas_call | solution.py:909
  102.6 3.2 %cross_weights.1 = (f32[512,512]{1,0:T(8,128)S(1)}, bf16[512,512]{1,0:T(8,128)(2,1)S(1)}, f32[8,512]{1,0:T(8,128)S(1)}, bf16[256,2560]{1,0:T(8,128)(2,1)S(1)}, b...) custom-call(s32[2]{0:T(128)S(1)} %copy-done.1, f32[512,512]{1,0:T(8,128)S(1)} %copy-done.6, ...), custom_call_target="tpu_custom_call" | custom-call | flops 6000000000 | bytes 4194304 | tf_op jit(solution)/shard_map/cross_weights/pallas_call | solution.py:909
  105.8 1.3 collective-permute-done.17
  107.2 1.6 collective-permute-start.19
  108.8 0.1 collective-permute-done.16
  108.9 0.2 slice_add_fusion.2
  109.1 1.4 collective-permute-start.18
  110.5 10.4 %self_backward.1 = (f32[512,512]{1,0:T(8,128)S(1)}, bf16[448,512]{1,0:T(8,128)(2,1)S(1)}, bf16[256,1664]{1,0:T(8,128)(2,1)S(1)}, bf16[256,1664]{1,0:T(8,128)(2,1)S(1)}) custom-call(s32[2]{0:T(128)S(1)} %copy-done.1, s32[1,1024]{1,0:T(1,128)S(1)} %copy-done.4, bf16[512,512]{1,0:T(8,128)(2,1)S(1)} %bitcast.20, bf16[256,512]{1,0:T(8,128)(2,1)S(1)} %slice.175.window, ...), custom_call_target="tpu_custom_call" | custom-call | flops 16000000000 | bytes 4194304 | tf_op jit(solution)/shard_map/self_backward/pallas_call | solution.py:909
  121.1 0.7 collective-permute-done.18
  121.8 0.1 slice_add_fusion.8
  121.9 1.6 collective-permute-start.20
  123.4 0.1 slice_add_fusion.6
  123.6 1.8 %collective-permute-start.25 = (bf16[128,1664]{1,0:T(8,128)(2,1)S(1)}, bf16[128,1664]{1,0:T(8,128)(2,1)S(1)}, u32[]{:S(2)}, u32[]{:S(2)}) collective-permute-start(bf16[128,1664]{1,0:T(8,128)(2,1)S(1)} %get-tuple-element.189), channel_id=1, source_target_pairs={{0,1},{1,0},{2,6},{3,7},{4,5},{5,4},{6,2},{7,3},{8,9},{9,8},{10,14... | collective-permute-start | bytes 1277960 | tf_op jit(solution)/shard_map/ppermute | solution.py:382
  125.4 0.1 fusion
  125.5 3.4 %collective-permute-start.24 = (bf16[128,512]{1,0:T(8,128)(2,1)S(1)}, bf16[128,512]{1,0:T(8,128)(2,1)S(1)}, u32[]{:S(2)}, u32[]{:S(2)}) collective-permute-start(bf16[128,512]{1,0:T(8,128)(2,1)S(1)} %get-tuple-element.192), channel_id=1, source_target_pairs={{0,24},{1,25},{2,26},{3,27},{4,28},{5,29},{6,30},{7,31},{8,16},{9,... | collective-permute-start | bytes 393224 | tf_op jit(solution)/shard_map/ppermute | solution.py:377
  129.0 1.0 collective-permute-start.22
  130.0 4.1 %collective-permute-done.25 = bf16[128,1664]{1,0:T(8,128)(2,1)S(1)} collective-permute-done((bf16[128,1664]{1,0:T(8,128)(2,1)S(1)}, bf16[128,1664]{1,0:T(8,128)(2,1)S(1)}, u32[]{:S(2)}, u32[]{:S(2)}) %collective-permute-start.25) | collective-permute-done | bytes 426016 | tf_op jit(solution)/shard_map/ppermute | solution.py:382
  134.2 1.6 collective-permute-start.30
  135.7 5.1 %collective-permute-done.23.refs_2_ = bf16[128,512]{1,0:T(8,128)(2,1)S(1)} collective-permute-done((bf16[128,512]{1,0:T(8,128)(2,1)S(1)}, bf16[128,512]{1,0:T(8,128)(2,1)S(1)}, u32[]{:S(2)}, u32[]{:S(2)}) %collective-permute-start.23) | collective-permute-done | bytes 131104 | tf_op jit(solution)/shard_map/ppermute | solution.py:377
  140.8 0.1 add.109
  140.9 2.4 %collective-permute-start.29 = (bf16[16,2560]{1,0:T(8,128)(2,1)S(1)}, bf16[16,2560]{1,0:T(8,128)(2,1)S(1)}, u32[]{:S(2)}, u32[]{:S(2)}) collective-permute-start(bf16[16,2560]{1,0:T(8,128)(2,1)S(1)} %get-tuple-element.196), channel_id=1, source_target_pairs={{0,24},{1,25},{2,26},{3,27},{4,28},{5,29},{6,30},{7,31},{8,16},{9,... | collective-permute-start | bytes 245768 | tf_op jit(solution)/shard_map/ppermute | solution.py:377
  143.4 2.0 %collective-permute-start.27 = (bf16[16,2560]{1,0:T(8,128)(2,1)S(1)}, bf16[16,2560]{1,0:T(8,128)(2,1)S(1)}, u32[]{:S(2)}, u32[]{:S(2)}) collective-permute-start(bf16[16,2560]{1,0:T(8,128)(2,1)S(1)} %get-tuple-element.198), channel_id=1, source_target_pairs={{0,8},{1,9},{2,10},{3,11},{4,12},{5,13},{6,14},{7,15},{8,0},{9,1},... | collective-permute-start | bytes 245768 | tf_op jit(solution)/shard_map/ppermute | solution.py:377
  145.4 0.5 collective-permute-start.26
  146.0 2.4 %collective-permute-start.33 = (bf16[16,1664]{1,0:T(8,128)(2,1)S(1)}, bf16[16,1664]{1,0:T(8,128)(2,1)S(1)}, u32[]{:S(2)}, u32[]{:S(2)}) collective-permute-start(bf16[16,1664]{1,0:T(8,128)(2,1)S(1)} %get-tuple-element.200), channel_id=1, source_target_pairs={{0,24},{1,25},{2,26},{3,27},{4,28},{5,29},{6,30},{7,31},{8,16},{9,... | collective-permute-start | bytes 159752 | tf_op jit(solution)/shard_map/ppermute | solution.py:377
  148.4 4.4 %collective-permute-done.28.refs_6_ = bf16[16,2560]{1,0:T(8,128)(2,1)S(1)} collective-permute-done((bf16[16,2560]{1,0:T(8,128)(2,1)S(1)}, bf16[16,2560]{1,0:T(8,128)(2,1)S(1)}, u32[]{:S(2)}, u32[]{:S(2)}) %collective-permute-start.28) | collective-permute-done | bytes 81952 | tf_op jit(solution)/shard_map/ppermute | solution.py:377
  152.9 2.3 %collective-permute-done.32.refs_10_ = bf16[16,1664]{1,0:T(8,128)(2,1)S(1)} collective-permute-done((bf16[16,1664]{1,0:T(8,128)(2,1)S(1)}, bf16[16,1664]{1,0:T(8,128)(2,1)S(1)}, u32[]{:S(2)}, u32[]{:S(2)}) %collective-permute-start.32) | collective-permute-done | bytes 53280 | tf_op jit(solution)/shard_map/ppermute | solution.py:377
  155.2 1.8 %collective-permute-done.31.refs_9_ = bf16[16,1664]{1,0:T(8,128)(2,1)S(1)} collective-permute-done((bf16[16,1664]{1,0:T(8,128)(2,1)S(1)}, bf16[16,1664]{1,0:T(8,128)(2,1)S(1)}, u32[]{:S(2)}, u32[]{:S(2)}) %collective-permute-start.31) | collective-permute-done | bytes 53280 | tf_op jit(solution)/shard_map/ppermute | solution.py:377
  157.0 1.4 finish.1
  158.4 2.3 %target_grad.1 = f32[512,512]{1,0:T(8,128)} custom-call(s32[2]{0:T(128)S(1)} %copy-done.1, f32[512,512]{1,0:T(8,128)S(1)} %get-tuple-element.151.back, bf16[256,512]{1,0:T(8,128)(2,1)S(1)} %slice.186.came, bf16[512,512]{1,0:T(8,128)(2,1)S(1)} %bitcast.21, f32[512,512]{1,0:T(8,128)S(1)} %get-tuple-element.160.self_grad, f32[8,512]{1,0:T(8,128)S(1)} %get-tuple-element.109.vectors), custom_call_target="tpu_custom_call" | custom-call | flops 1000000 | bytes 4194304 | tf_op jit(solution)/shard_map/target_grad/pallas_call | solution.py:909
  160.7 0.8 add_bitcast_fusion
  (67 shorter events, 0.7 us)
Async XLA Ops:
  5.8 9.8 %collective-permute-start.3 = (bf16[16,4224]{1,0:T(8,128)(2,1)}, bf16[16,4224]{1,0:T(8,128)(2,1)S(1)}, u32[]{:S(2)}, u32[]{:S(2)}) collective-permute-start(bf16[16,4224]{1,0:T(8,128)(2,1)} %get-tuple-element.104), channel_id=1, source_target_pairs={{0,24},{1,25},{2,26},{3,27},{4,28},{5,29},{6,30},{7,31},{8,16},{9,... | collective-permute-start | bytes 405512 | tf_op jit(solution)/shard_map/ppermute | solution.py:377
  10.9 11.6 %collective-permute-start.2 = (bf16[16,4224]{1,0:T(8,128)(2,1)}, bf16[16,4224]{1,0:T(8,128)(2,1)S(1)}, u32[]{:S(2)}, u32[]{:S(2)}) collective-permute-start(bf16[16,4224]{1,0:T(8,128)(2,1)} %get-tuple-element.104), channel_id=1, source_target_pairs={{0,16},{1,17},{2,18},{3,19},{4,20},{5,21},{6,22},{7,23},{8,24},{9,... | collective-permute-start | bytes 405512 | tf_op jit(solution)/shard_map/ppermute | solution.py:377
  10.9 11.6 %collective-permute-start.1 = (bf16[16,4224]{1,0:T(8,128)(2,1)}, bf16[16,4224]{1,0:T(8,128)(2,1)S(1)}, u32[]{:S(2)}, u32[]{:S(2)}) collective-permute-start(bf16[16,4224]{1,0:T(8,128)(2,1)} %get-tuple-element.104), channel_id=1, source_target_pairs={{0,8},{1,9},{2,10},{3,11},{4,12},{5,13},{6,14},{7,15},{8,0},{9,1},... | collective-permute-start | bytes 405512 | tf_op jit(solution)/shard_map/ppermute | solution.py:377
  11.5 11.9 %collective-permute-start = (bf16[448,512]{1,0:T(8,128)(2,1)}, bf16[448,512]{1,0:T(8,128)(2,1)S(1)}, u32[]{:S(2)}, u32[]{:S(2)}) collective-permute-start(bf16[448,512]{1,0:T(8,128)(2,1)} %get-tuple-element.102), channel_id=1, source_target_pairs={{0,1},{1,0},{2,3},{3,2},{4,5},{5,4},{6,7},{7,6},{8,9},{9,8},{10,11... | collective-permute-start | bytes 1376264 | tf_op jit(solution)/shard_map/ppermute | solution.py:377
  23.5 9.4 %collective-permute-start.4 = (bf16[64,4224]{1,0:T(8,128)(2,1)S(1)}, bf16[64,4224]{1,0:T(8,128)(2,1)S(1)}, u32[]{:S(2)}, u32[]{:S(2)}) collective-permute-start(bf16[64,4224]{1,0:T(8,128)(2,1)S(1)} %pad_maximum_fusion), channel_id=1, source_target_pairs={{0,4},{1,5},{2,3},{3,2},{4,0},{5,1},{6,7},{7,6},{8,12},{9,13},{10,... | collective-permute-start | bytes 1622024 | tf_op jit(solution)/shard_map/ppermute | solution.py:382
  32.9 1.7 %copy-start.9 = (bf16[128,512]{1,0:T(8,128)(2,1)S(1)}, bf16[128,512]{1,0:T(8,128)(2,1)}, u32[]{:S(2)}) copy-start(bf16[128,512]{1,0:T(8,128)(2,1)} %get-tuple-element.107) | copy-start | bytes 393220
  32.9 15.3 %copy-start.10 = (s32[1,336]{1,0:T(1,128)S(1)}, s32[1,336]{1,0:T(1,128)}, u32[]{:S(2)}) copy-start(s32[1,336]{1,0:T(1,128)} %param.23) | copy-start | bytes 4036
  33.0 17.9 %copy-start = (bf16[1,512,512]{2,1,0:T(8,128)(2,1)S(1)}, bf16[1,512,512]{2,1,0:T(8,128)(2,1)}, u32[]{:S(2)}) copy-start(bf16[1,512,512]{2,1,0:T(8,128)(2,1)} %param.20) | copy-start | bytes 1572868
  33.0 17.9 %copy-start.1 = (s32[2]{0:T(128)S(1)}, s32[2]{0:T(128)}, u32[]{:S(2)}) copy-start(s32[2]{0:T(128)} %pad_add_fusion.1.place) | copy-start | bytes 28
  33.0 15.2 %collective-permute-start.5 = (bf16[128,4224]{1,0:T(8,128)(2,1)S(1)}, bf16[128,4224]{1,0:T(8,128)(2,1)S(1)}, u32[]{:S(2)}, u32[]{:S(2)}) collective-permute-start(bf16[128,4224]{1,0:T(8,128)(2,1)S(1)} %constant_dynamic-update-slice_fusion.refs_0_), channel_id=1, source_target_pairs={{0,1},{1,0},{2,6},{3,7},{4,5},{5,4},{6,2},{7,3},{8,9},{9,8},{10,14... | collective-permute-start | bytes 3244040 | tf_op jit(solution)/shard_map/ppermute | solution.py:382
  34.6 8.0 %collective-permute-start.8 = (bf16[128,512]{1,0:T(8,128)(2,1)S(1)}, bf16[128,512]{1,0:T(8,128)(2,1)S(1)}, u32[]{:S(2)}, u32[]{:S(2)}) collective-permute-start(bf16[128,512]{1,0:T(8,128)(2,1)S(1)} %copy-done.9), channel_id=1, source_target_pairs={{0,24},{1,25},{2,26},{3,27},{4,28},{5,29},{6,30},{7,31},{8,16},{9,... | collective-permute-start | bytes 393224 | tf_op jit(solution)/shard_map/ppermute | solution.py:377
  38.0 8.9 %collective-permute-start.7 = (bf16[128,512]{1,0:T(8,128)(2,1)S(1)}, bf16[128,512]{1,0:T(8,128)(2,1)S(1)}, u32[]{:S(2)}, u32[]{:S(2)}) collective-permute-start(bf16[128,512]{1,0:T(8,128)(2,1)S(1)} %copy-done.9), channel_id=1, source_target_pairs={{0,16},{1,17},{2,18},{3,19},{4,20},{5,21},{6,22},{7,23},{8,24},{9,... | collective-permute-start | bytes 393224 | tf_op jit(solution)/shard_map/ppermute | solution.py:377
  38.0 8.9 %collective-permute-start.6 = (bf16[128,512]{1,0:T(8,128)(2,1)S(1)}, bf16[128,512]{1,0:T(8,128)(2,1)S(1)}, u32[]{:S(2)}, u32[]{:S(2)}) collective-permute-start(bf16[128,512]{1,0:T(8,128)(2,1)S(1)} %copy-done.9), channel_id=1, source_target_pairs={{0,8},{1,9},{2,10},{3,11},{4,12},{5,13},{6,14},{7,15},{8,0},{9,1},... | collective-permute-start | bytes 393224 | tf_op jit(solution)/shard_map/ppermute | solution.py:377
  39.0 11.1 %collective-permute-start.9 = (bf16[128,4224]{1,0:T(8,128)(2,1)S(1)}, bf16[128,4224]{1,0:T(8,128)(2,1)S(1)}, u32[]{:S(2)}, u32[]{:S(2)}) collective-permute-start(bf16[128,4224]{1,0:T(8,128)(2,1)S(1)} %constant_dynamic-update-slice_fusion.refs_0_), channel_id=1, source_target_pairs={{0,2},{1,3},{2,0},{3,1},{4,6},{5,7},{6,4},{7,5},{8,10},{9,11},{10,... | collective-permute-start | bytes 3244040 | tf_op jit(solution)/shard_map/ppermute | solution.py:377
  48.3 2.7 %collective-permute-start.10 = (bf16[128,4224]{1,0:T(8,128)(2,1)S(1)}, bf16[128,4224]{1,0:T(8,128)(2,1)S(1)}, u32[]{:S(2)}, u32[]{:S(2)}) collective-permute-start(bf16[128,4224]{1,0:T(8,128)(2,1)S(1)} %collective-permute-done.5.refs_1_), channel_id=1, source_target_pairs={{0,2},{1,3},{2,0},{3,1},{4,6},{5,7},{6,4},{7,5},{8,10},{9,11},{10,... | collective-permute-start | bytes 3244040 | tf_op jit(solution)/shard_map/ppermute | solution.py:377
  48.4 9.2 %collective-permute-start.11 = (bf16[512,512]{1,0:T(8,128)(2,1)S(1)}, bf16[512,512]{1,0:T(8,128)(2,1)S(1)}, u32[]{:S(2)}, u32[]{:S(2)}) collective-permute-start(bf16[512,512]{1,0:T(8,128)(2,1)S(1)} %constant_dynamic-update-slice_fusion.2), channel_id=1, source_target_pairs={{0,4},{1,5},{2,3},{3,2},{4,0},{5,1},{6,7},{7,6},{8,12},{9,13},{10,... | collective-permute-start | bytes 1572872 | tf_op jit(solution)/shard_map/ppermute | solution.py:382
  53.3 15.5 %copy-start.7 = (bf16[512,512]{1,0:T(8,128)(2,1)}, bf16[512,512]{1,0:T(8,128)(2,1)S(1)}, u32[]{:S(2)}) copy-start(bf16[512,512]{1,0:T(8,128)(2,1)S(1)} %get-tuple-element.114.self_queries.queries) | copy-start | bytes 1572868
  53.3 6.0 %copy-start.3 = (bf16[192,512]{1,0:T(8,128)(2,1)S(1)}, bf16[192,512]{1,0:T(8,128)(2,1)}, u32[]{:S(2)}) copy-start(bf16[192,512]{1,0:T(8,128)(2,1)} %get-tuple-element.101.own_source) | copy-start | bytes 589828
  53.3 6.0 %copy-start.4 = (s32[1,1024]{1,0:T(1,128)S(1)}, s32[1,1024]{1,0:T(1,128)}, u32[]{:S(2)}) copy-start(s32[1,1024]{1,0:T(1,128)} %segments.5) | copy-start | bytes 12292
  57.7 14.9 %collective-permute-start.13 = (bf16[1024,512]{1,0:T(8,128)(2,1)S(1)}, bf16[1024,512]{1,0:T(8,128)(2,1)S(1)}, u32[]{:S(2)}, u32[]{:S(2)}) collective-permute-start(bf16[1024,512]{1,0:T(8,128)(2,1)S(1)} %constant_dynamic-update-slice_fusion.6.refs_0_), channel_id=1, source_target_pairs={{0,1},{1,0},{2,6},{3,7},{4,5},{5,4},{6,2},{7,3},{8,9},{9,8},{10,14... | collective-permute-start | bytes 3145736 | tf_op jit(solution)/shard_map/ppermute | solution.py:382
  59.3 13.3 %collective-permute-start.12 = (bf16[1024,512]{1,0:T(8,128)(2,1)S(1)}, bf16[1024,512]{1,0:T(8,128)(2,1)S(1)}, u32[]{:S(2)}, u32[]{:S(2)}) collective-permute-start(bf16[1024,512]{1,0:T(8,128)(2,1)S(1)} %constant_dynamic-update-slice_fusion.6.refs_0_), channel_id=1, source_target_pairs={{0,2},{1,3},{2,0},{3,1},{4,6},{5,7},{6,4},{7,5},{8,10},{9,11},{10,... | collective-permute-start | bytes 3145736 | tf_op jit(solution)/shard_map/ppermute | solution.py:377
  59.3 15.9 %copy-start.2 = (bf16[1,512,512]{2,1,0:T(8,128)(2,1)S(1)}, bf16[1,512,512]{2,1,0:T(8,128)(2,1)}, u32[]{:S(2)}) copy-start(bf16[1,512,512]{2,1,0:T(8,128)(2,1)} %param.24) | copy-start | bytes 1572868
  68.8 17.3 %copy-start.5 = (f32[512,512]{1,0:T(8,128)}, f32[512,512]{1,0:T(8,128)S(1)}, u32[]{:S(2)}) copy-start(f32[512,512]{1,0:T(8,128)S(1)} %get-tuple-element.125.after_self) | copy-start | bytes 3145732
  72.6 2.7 %collective-permute-start.14 = (bf16[1024,512]{1,0:T(8,128)(2,1)S(1)}, bf16[1024,512]{1,0:T(8,128)(2,1)S(1)}, u32[]{:S(2)}, u32[]{:S(2)}) collective-permute-start(bf16[1024,512]{1,0:T(8,128)(2,1)S(1)} %collective-permute-done.13.refs_1_), channel_id=1, source_target_pairs={{0,2},{1,3},{2,0},{3,1},{4,6},{5,7},{6,4},{7,5},{8,10},{9,11},{10,... | collective-permute-start | bytes 3145736 | tf_op jit(solution)/shard_map/ppermute | solution.py:377
  86.1 4.4 %collective-permute-start.15 = (bf16[2048,512]{1,0:T(8,128)(2,1)S(1)}, bf16[2048,512]{1,0:T(8,128)(2,1)}, u32[]{:S(2)}, u32[]{:S(2)}) collective-permute-start(bf16[2048,512]{1,0:T(8,128)(2,1)S(1)} %get-tuple-element.130), channel_id=1, source_target_pairs={{0,2},{1,3},{2,0},{3,1},{4,6},{5,7},{6,4},{7,5},{8,10},{9,11},{10,... | collective-permute-start | bytes 6291464 | tf_op jit(solution)/shard_map/ppermute | solution.py:377
  92.3 14.9 %collective-permute-start.17 = (bf16[1024,512]{1,0:T(8,128)(2,1)S(1)}, bf16[1024,512]{1,0:T(8,128)(2,1)S(1)}, u32[]{:S(2)}, u32[]{:S(2)}) collective-permute-start(bf16[1024,512]{1,0:T(8,128)(2,1)S(1)} %get-tuple-element.185), channel_id=1, source_target_pairs={{0,1},{1,0},{2,6},{3,7},{4,5},{5,4},{6,2},{7,3},{8,9},{9,8},{10,14... | collective-permute-start | bytes 3145736 | tf_op jit(solution)/shard_map/ppermute | solution.py:382
  93.9 8.7 %copy-start.6 = (f32[512,512]{1,0:T(8,128)S(1)}, f32[512,512]{1,0:T(8,128)}, u32[]{:S(2)}) copy-start(f32[512,512]{1,0:T(8,128)} %copy-done.5) | copy-start | bytes 3145732
  105.8 3.1 %collective-permute-start.16 = (bf16[256,2560]{1,0:T(8,128)(2,1)S(1)}, bf16[256,2560]{1,0:T(8,128)(2,1)S(1)}, u32[]{:S(2)}, u32[]{:S(2)}) collective-permute-start(bf16[256,2560]{1,0:T(8,128)(2,1)S(1)} %get-tuple-element.142), channel_id=1, source_target_pairs={{0,2},{1,3},{2,0},{3,1},{4,6},{5,7},{6,4},{7,5},{8,10},{9,11},{10,... | collective-permute-start | bytes 3932168 | tf_op jit(solution)/shard_map/ppermute | solution.py:377
  107.2 13.8 %collective-permute-start.19 = (bf16[512,512]{1,0:T(8,128)(2,1)S(1)}, bf16[512,512]{1,0:T(8,128)(2,1)S(1)}, u32[]{:S(2)}, u32[]{:S(2)}) collective-permute-start(bf16[512,512]{1,0:T(8,128)(2,1)S(1)} %slice_add_fusion.5), channel_id=1, source_target_pairs={{0,4},{1,5},{2,3},{3,2},{4,0},{5,1},{6,7},{7,6},{8,12},{9,13},{10,... | collective-permute-start | bytes 1572872 | tf_op jit(solution)/shard_map/ppermute | solution.py:382
  108.9 1.6 copy-start.8
  109.1 12.7 %collective-permute-start.18 = (bf16[128,2560]{1,0:T(8,128)(2,1)S(1)}, bf16[128,2560]{1,0:T(8,128)(2,1)S(1)}, u32[]{:S(2)}, u32[]{:S(2)}) collective-permute-start(bf16[128,2560]{1,0:T(8,128)(2,1)S(1)} %get-tuple-element.187), channel_id=1, source_target_pairs={{0,1},{1,0},{2,6},{3,7},{4,5},{5,4},{6,2},{7,3},{8,9},{9,8},{10,14... | collective-permute-start | bytes 1966088 | tf_op jit(solution)/shard_map/ppermute | solution.py:382
  121.0 2.5 %collective-permute-start.21 = (bf16[256,1664]{1,0:T(8,128)(2,1)S(1)}, bf16[256,1664]{1,0:T(8,128)(2,1)S(1)}, u32[]{:S(2)}, u32[]{:S(2)}) collective-permute-start(bf16[256,1664]{1,0:T(8,128)(2,1)S(1)} %get-tuple-element.155), channel_id=1, source_target_pairs={{0,2},{1,3},{2,0},{3,1},{4,6},{5,7},{6,4},{7,5},{8,10},{9,11},{10,... | collective-permute-start | bytes 2555912 | tf_op jit(solution)/shard_map/ppermute | solution.py:377
  121.9 18.9 %collective-permute-start.20 = (bf16[64,2560]{1,0:T(8,128)(2,1)S(1)}, bf16[64,2560]{1,0:T(8,128)(2,1)S(1)}, u32[]{:S(2)}, u32[]{:S(2)}) collective-permute-start(bf16[64,2560]{1,0:T(8,128)(2,1)S(1)} %get-tuple-element.191), channel_id=1, source_target_pairs={{0,4},{1,5},{2,3},{3,2},{4,0},{5,1},{6,7},{7,6},{8,12},{9,13},{10,... | collective-permute-start | bytes 983048 | tf_op jit(solution)/shard_map/ppermute | solution.py:382
  123.6 10.6 %collective-permute-start.25 = (bf16[128,1664]{1,0:T(8,128)(2,1)S(1)}, bf16[128,1664]{1,0:T(8,128)(2,1)S(1)}, u32[]{:S(2)}, u32[]{:S(2)}) collective-permute-start(bf16[128,1664]{1,0:T(8,128)(2,1)S(1)} %get-tuple-element.189), channel_id=1, source_target_pairs={{0,1},{1,0},{2,6},{3,7},{4,5},{5,4},{6,2},{7,3},{8,9},{9,8},{10,14... | collective-permute-start | bytes 1277960 | tf_op jit(solution)/shard_map/ppermute | solution.py:382
  125.5 10.2 %collective-permute-start.24 = (bf16[128,512]{1,0:T(8,128)(2,1)S(1)}, bf16[128,512]{1,0:T(8,128)(2,1)S(1)}, u32[]{:S(2)}, u32[]{:S(2)}) collective-permute-start(bf16[128,512]{1,0:T(8,128)(2,1)S(1)} %get-tuple-element.192), channel_id=1, source_target_pairs={{0,24},{1,25},{2,26},{3,27},{4,28},{5,29},{6,30},{7,31},{8,16},{9,... | collective-permute-start | bytes 393224 | tf_op jit(solution)/shard_map/ppermute | solution.py:377
  129.0 11.9 %collective-permute-start.23 = (bf16[128,512]{1,0:T(8,128)(2,1)S(1)}, bf16[128,512]{1,0:T(8,128)(2,1)S(1)}, u32[]{:S(2)}, u32[]{:S(2)}) collective-permute-start(bf16[128,512]{1,0:T(8,128)(2,1)S(1)} %get-tuple-element.193), channel_id=1, source_target_pairs={{0,16},{1,17},{2,18},{3,19},{4,20},{5,21},{6,22},{7,23},{8,24},{9,... | collective-permute-start | bytes 393224 | tf_op jit(solution)/shard_map/ppermute | solution.py:377
  129.0 11.9 %collective-permute-start.22 = (bf16[128,512]{1,0:T(8,128)(2,1)S(1)}, bf16[128,512]{1,0:T(8,128)(2,1)S(1)}, u32[]{:S(2)}, u32[]{:S(2)}) collective-permute-start(bf16[128,512]{1,0:T(8,128)(2,1)S(1)} %get-tuple-element.194), channel_id=1, source_target_pairs={{0,8},{1,9},{2,10},{3,11},{4,12},{5,13},{6,14},{7,15},{8,0},{9,1},... | collective-permute-start | bytes 393224 | tf_op jit(solution)/shard_map/ppermute | solution.py:377
  134.2 11.8 %collective-permute-start.30 = (bf16[64,1664]{1,0:T(8,128)(2,1)S(1)}, bf16[64,1664]{1,0:T(8,128)(2,1)S(1)}, u32[]{:S(2)}, u32[]{:S(2)}) collective-permute-start(bf16[64,1664]{1,0:T(8,128)(2,1)S(1)} %slice_add_fusion.11), channel_id=1, source_target_pairs={{0,4},{1,5},{2,3},{3,2},{4,0},{5,1},{6,7},{7,6},{8,12},{9,13},{10,... | collective-permute-start | bytes 638984 | tf_op jit(solution)/shard_map/ppermute | solution.py:382
  140.9 7.5 %collective-permute-start.29 = (bf16[16,2560]{1,0:T(8,128)(2,1)S(1)}, bf16[16,2560]{1,0:T(8,128)(2,1)S(1)}, u32[]{:S(2)}, u32[]{:S(2)}) collective-permute-start(bf16[16,2560]{1,0:T(8,128)(2,1)S(1)} %get-tuple-element.196), channel_id=1, source_target_pairs={{0,24},{1,25},{2,26},{3,27},{4,28},{5,29},{6,30},{7,31},{8,16},{9,... | collective-permute-start | bytes 245768 | tf_op jit(solution)/shard_map/ppermute | solution.py:377
  143.4 9.5 %collective-permute-start.28 = (bf16[16,2560]{1,0:T(8,128)(2,1)S(1)}, bf16[16,2560]{1,0:T(8,128)(2,1)S(1)}, u32[]{:S(2)}, u32[]{:S(2)}) collective-permute-start(bf16[16,2560]{1,0:T(8,128)(2,1)S(1)} %get-tuple-element.197), channel_id=1, source_target_pairs={{0,16},{1,17},{2,18},{3,19},{4,20},{5,21},{6,22},{7,23},{8,24},{9,... | collective-permute-start | bytes 245768 | tf_op jit(solution)/shard_map/ppermute | solution.py:377
  143.4 9.5 %collective-permute-start.27 = (bf16[16,2560]{1,0:T(8,128)(2,1)S(1)}, bf16[16,2560]{1,0:T(8,128)(2,1)S(1)}, u32[]{:S(2)}, u32[]{:S(2)}) collective-permute-start(bf16[16,2560]{1,0:T(8,128)(2,1)S(1)} %get-tuple-element.198), channel_id=1, source_target_pairs={{0,8},{1,9},{2,10},{3,11},{4,12},{5,13},{6,14},{7,15},{8,0},{9,1},... | collective-permute-start | bytes 245768 | tf_op jit(solution)/shard_map/ppermute | solution.py:377
  145.4 13.0 %collective-permute-start.26 = (bf16[448,512]{1,0:T(8,128)(2,1)S(1)}, bf16[448,512]{1,0:T(8,128)(2,1)S(1)}, u32[]{:S(2)}, u32[]{:S(2)}) collective-permute-start(bf16[448,512]{1,0:T(8,128)(2,1)S(1)} %get-tuple-element.159), channel_id=1, source_target_pairs={{0,1},{1,0},{2,3},{3,2},{4,5},{5,4},{6,7},{7,6},{8,9},{9,8},{10,11... | collective-permute-start | bytes 1376264 | tf_op jit(solution)/shard_map/ppermute | solution.py:377
  146.0 6.9 %collective-permute-start.33 = (bf16[16,1664]{1,0:T(8,128)(2,1)S(1)}, bf16[16,1664]{1,0:T(8,128)(2,1)S(1)}, u32[]{:S(2)}, u32[]{:S(2)}) collective-permute-start(bf16[16,1664]{1,0:T(8,128)(2,1)S(1)} %get-tuple-element.200), channel_id=1, source_target_pairs={{0,24},{1,25},{2,26},{3,27},{4,28},{5,29},{6,30},{7,31},{8,16},{9,... | collective-permute-start | bytes 159752 | tf_op jit(solution)/shard_map/ppermute | solution.py:377
  148.4 6.7 %collective-permute-start.32 = (bf16[16,1664]{1,0:T(8,128)(2,1)S(1)}, bf16[16,1664]{1,0:T(8,128)(2,1)S(1)}, u32[]{:S(2)}, u32[]{:S(2)}) collective-permute-start(bf16[16,1664]{1,0:T(8,128)(2,1)S(1)} %get-tuple-element.201), channel_id=1, source_target_pairs={{0,16},{1,17},{2,18},{3,19},{4,20},{5,21},{6,22},{7,23},{8,24},{9,... | collective-permute-start | bytes 159752 | tf_op jit(solution)/shard_map/ppermute | solution.py:377
  152.9 4.1 %collective-permute-start.31 = (bf16[16,1664]{1,0:T(8,128)(2,1)S(1)}, bf16[16,1664]{1,0:T(8,128)(2,1)S(1)}, u32[]{:S(2)}, u32[]{:S(2)}) collective-permute-start(bf16[16,1664]{1,0:T(8,128)(2,1)S(1)} %get-tuple-element.202), channel_id=1, source_target_pairs={{0,8},{1,9},{2,10},{3,11},{4,12},{5,13},{6,14},{7,15},{8,0},{9,1},... | collective-permute-start | bytes 159752 | tf_op jit(solution)/shard_map/ppermute | solution.py:377
where the time goes:
time: 162 us
  waiting for transfers between devices  60.5 us (37%)
  Pallas kernels  53.5 us (33%)
  starting transfers between devices  39.7 us (25%)
  other arithmetic  5.74 us (4%)
    pallas_call x10, Pallas kernels, call(): pl.pallas_call(body, name=name, out_shape=outs, in_specs=[SMEM_SPEC] + [H...  53.5 us
    ppermute x24, waiting for transfers between devices, exchange(): lax.ppermute(value, AXES, [(device, device ^ flip) for device in range(32)])  36.9 us
    ppermute x24, starting transfers between devices, exchange(): lax.ppermute(value, AXES, [(device, device ^ flip) for device in range(32)])  23.9 us
    ppermute x10, waiting for transfers between devices, exchange_side(): lax.ppermute(value, AXES, [(device, device ^ flips[device >> 1 & 1]) for...  23.6 us
    ppermute x10, starting transfers between devices, exchange_side(): lax.ppermute(value, AXES, [(device, device ^ flips[device >> 1 & 1]) for...  15.8 us
  transfers between devices with their start and end apart: 34, of which 19 were waited for; matrix products, arithmetic and copies ran while one was open for 1% of the time, Pallas kernels for 23%

commit v1 on v0

--- a/solution.py
+++ b/solution.py
@@ -711,12 +711,15 @@
 
     def chunk(z):
         at = pl.ds(chunk_of(z), CHUNK)
-        z_row = ((me >> 3) ^ z) * BLOCK
+        mine = me >> 3
+        z_row = (mine ^ z) * BLOCK
         up, down, up_grad, down_grad = ups.at[z], downs.at[z], up_grads.at[z], down_grads.at[z]
+        swapped_z = (z & 1) * 2 + (z >> 1)
         for piece, row, owner in places:
+            owner = (owner & 7) + (mine ^ (row % 2 * 2 + row % 4 // 2)) * FLIP_Z
             up[block_rows(owner), :] = pieces[piece][pl.ds(pl.multiple_of(row * 128 + z_row, BLOCK), BLOCK), :]
             if row % 4 == 0:
-                start = pl.multiple_of((row + z) * 128 + 64, 64)
+                start = pl.multiple_of((row + swapped_z) * 128 + 64, 64)
                 down[block_rows(owner & 7, 64), :] = pieces[piece][pl.ds(start, 64), :]
         hidden = nn(lowered[...], up[...]) + up_bias[:, at]
         square = hidden * hidden
@@ -905,7 +908,7 @@
 SMEM_SPEC = pl.BlockSpec(memory_space=pltpu.SMEM)
 
 
-def call(body, name, place, inputs, pieces, outs, scratch, flops, any_outs=(), any_ins=(), vmem=40):
+def call(body, name, place, inputs, pieces, outs, scratch, flops, any_outs=(), any_ins=(), vmem=20):
     return pl.pallas_call(
         body,
         name=name,
@@ -953,16 +956,21 @@
     one = join(one, *parts)
     one = tied(one, near)
     came = exchange_side(one, 0)
-    three, one = tied((three, one), came)
-    parts_three = along_z(three)
+    three = tied(three, one)
+    far = exchange(three, 2 * FLIP_Z)
+    came = tied(came, far)
     one = join(one, came)
     one_core = exchange(one, FLIP_CORE)
     other = exchange_side(one, 1)
-    other = tied(other, parts_three)
+    three = join(three, tied(far, one))
+    three = join(three, exchange(three, FLIP_Z))
+    came = exchange_side(three, 0)
+    other = tied(other, came)
     window, other_source = near[:WINDOW], near[WINDOW:]
     pieces_one = [one, other, one_core, exchange(other, FLIP_CORE)]
-    three = join(three, *parts_three)
-    came = exchange_side(three, 0)
+    three = join(three, came)
+    three_core = exchange(three, FLIP_CORE)
+    three_other = exchange_side(three, 1)
     half = source_states.shape[1]
     gap = jnp.full((1, HALF_SOURCE - half), -1, jnp.int32)
     source_seg = jnp.concatenate([source_segments[:, :half], gap, source_segments[:, half:], gap], 1)
@@ -973,13 +981,8 @@
             shape_of(OWN, MODEL), shape_of(KEYS, 2 * MODEL), shape_of(KEYS, MODEL), shape_of(8, MODEL, dtype=F32),
             shape_of(1, FEED, dtype=F32), shape_of(MODEL, 1536), shape_of(MODEL, 2560),
         ],
-        [vmem((MODEL, TILE), BF16)], 5000000000,
-    )
-    came, three = tied((came, three), queries)
-    three = join(three, came)
-    three_core = exchange(three, FLIP_CORE)
-    other = exchange_side(three, 1)
-    queries = tied(queries, three)
+        [vmem((MODEL, TILE), BF16)], 1000,
+    )
     mixed, logs, after_self, lowered_two, queries_two, pair_two, mixed_two, logs_two, after_cross = call(
         forward_body, "forward", place,
         [
@@ -994,10 +997,10 @@
         [
             vmem((OWN, TILE), F32), vmem((1, KEYS), F32), vmem((1, SOURCES), F32), vmem((SOURCES, MODEL), BF16),
         ],
-        20000000000,
-    )
-    three_core, other = tied((three_core, other), after_cross)
-    pieces_three = [three, other, three_core, exchange(other, FLIP_CORE)]
+        1000,
+    )
+    three_core, three_other = tied((three_core, three_other), after_cross)
+    pieces_three = [three, three_other, three_core, exchange(three_other, FLIP_CORE)]
     total, back, feed_kept, feed_sent, bias_sums = call(
         feed_body, "feed", place, [after_cross, grad, vectors, up_bias], pieces_three,
         [shape_of(OWN, MODEL, dtype=F32)] * 2 + [shape_of(2048, MODEL)] * 2 + [shape_of(1, FEED, dtype=F32)],
@@ -1064,17 +1067,19 @@
     )
     last_came = exchange(last_sent, FLIP_CORE)
     cross_came, feed_came = tied((cross_came, feed_came), own_back)
+    feed = z_blocks(feed_kept + feed_came)
+    cross_came = tied(cross_came, feed[0])
     cross_sent, cross_kept = add_halves(cross_kept, cross_came)
+    last_came = tied(last_came, feed[0])
     last_sent, last_kept = add_halves(last_kept, last_came)
     last_came, cross_came = exchange_side(last_sent, 1), exchange_side(cross_sent, 0)
-    feed_came = tied(feed_came, last_sent)
-    feed = z_blocks(feed_kept + feed_came)
-    last_came = tied(last_came, feed[0])
+    cross_kept = cross_kept + cross_came
+    last_came = tied(last_came, cross_kept)
     last_sent, last_kept = add_halves(last_kept, last_came)
     last_came = exchange_side(last_sent, 0)
-    cross_came, feed, near_back = tied((cross_came, feed, near_back), last_sent)
+    feed, near_back = tied((feed, near_back), last_sent)
     cross_kept = tied(cross_kept, feed)
-    cross = z_blocks(cross_kept + cross_came)
+    cross = z_blocks(cross_kept)
     near_came = exchange(near_back, FLIP_Y)
     last_came = tied(last_came, cross[0])
     last = z_blocks(last_kept + last_came)
@@ -1084,6 +1089,7 @@
         target_body, "target_grad", place, [own_back, came, states, self_grad, vectors], [],
         [shape_of(OWN, MODEL, dtype=F32)], [], 1000000,
     )
+    last = tied(last, grad_target, grad_source)
     project, output, query, keyval, crossout, up, down, *small = call(
         finish_body, "finish", place, feed + cross + last, [],
         [

time: 162 us -> 155 us (0.957)
  waiting for transfers between devices: 60.5 us -> 50.5 us
  starting transfers between devices: 39.7 us -> 44.4 us
  other arithmetic: 5.74 us -> 4.03 us
    ppermute x24 -> x23, waiting for transfers between devices: 36.9 us -> 28.2 us  [exchange(): lax.ppermute(value, AXES, [(device, device ^ flip) for device in range(32)])]
    ppermute x24 -> x23, starting transfers between devices: 23.9 us -> 29.6 us  [exchange(): lax.ppermute(value, AXES, [(device, device ^ flip) for device in range(32)])]
    add x6, other arithmetic: 2.3 us -> 0.58 us  [add_halves(): return (kept[half:] + came[half:], kept[:half] + came[:half])]
  transfers between devices with their start and end apart: 34 -> 33, of which waited for: 19 -> 16; matrix products, arithmetic and copies ran while one was open for 1% -> 2% of each run, Pallas kernels for 23% -> 25%
where the time goes in v1:
time: 155 us
  Pallas kernels  53.9 us (35%)
  waiting for transfers between devices  50.5 us (33%)
  starting transfers between devices  44.4 us (29%)
  other arithmetic  4.03 us (3%)
    pallas_call x10, Pallas kernels, call(): pl.pallas_call(body, name=name, out_shape=outs, in_specs=[SMEM_SPEC] + [H...  53.9 us
    ppermute x23, starting transfers between devices, exchange(): lax.ppermute(value, AXES, [(device, device ^ flip) for device in range(32)])  29.6 us
    ppermute x23, waiting for transfers between devices, exchange(): lax.ppermute(value, AXES, [(device, device ^ flip) for device in range(32)])  28.2 us
    ppermute x10, waiting for transfers between devices, exchange_side(): lax.ppermute(value, AXES, [(device, device ^ flips[device >> 1 & 1]) for...  22.3 us
    ppermute x10, starting transfers between devices, exchange_side(): lax.ppermute(value, AXES, [(device, device ^ flips[device >> 1 & 1]) for...  14.9 us
  transfers between devices with their start and end apart: 33, of which 16 were waited for; matrix products, arithmetic and copies ran while one was open for 2% of the time, Pallas kernels for 25%

profile of v1, /device:TPU:0, one launch (start us, length us, event | category | flops | bytes accessed | tf_op | source)
XLA Modules:
  0.0 155.0 jit_solution(6121933973606908856)
XLA Ops:
  0.7 0.9 pad_add_fusion.2
  1.5 0.6 reshape.39.vectors
  2.1 0.6 pad_add_fusion.1.place
  2.7 3.1 %pack.1 = (bf16[16,4224]{1,0:T(8,128)(2,1)}, bf16[128,512]{1,0:T(8,128)(2,1)}, bf16[448,512]{1,0:T(8,128)(2,1)}, bf16[192,512]{1,0:T(8,128)(2,1)}) custom-call(s32[2]{0:T(128)} %pad_add_fusion.1.place, bf16[1,256]{1,0:T(2,128)(2,1)} %reshape.39.vectors, bf16[16,1536]{1,0:T(8,128)(2,1)} %project.1, bf16[16,512]{1,0:T(8,128)(2,1)} %output.1, ...), custom_call_target="tpu_custom_call" | custom-call | flops 1000000 | bytes 4194304 | tf_op jit(solution)/shard_map/pack/pallas_call | solution.py:912
  5.8 5.1 %collective-permute-start.3 = (bf16[16,4224]{1,0:T(8,128)(2,1)}, bf16[16,4224]{1,0:T(8,128)(2,1)S(1)}, u32[]{:S(2)}, u32[]{:S(2)}) collective-permute-start(bf16[16,4224]{1,0:T(8,128)(2,1)} %get-tuple-element.105), channel_id=1, source_target_pairs={{0,24},{1,25},{2,26},{3,27},{4,28},{5,29},{6,30},{7,31},{8,16},{9,... | collective-permute-start | bytes 405512 | tf_op jit(solution)/shard_map/ppermute | solution.py:377
  10.9 0.6 collective-permute-start.1
  11.6 1.7 %collective-permute-start = (bf16[448,512]{1,0:T(8,128)(2,1)}, bf16[448,512]{1,0:T(8,128)(2,1)S(1)}, u32[]{:S(2)}, u32[]{:S(2)}) collective-permute-start(bf16[448,512]{1,0:T(8,128)(2,1)} %get-tuple-element.104), channel_id=1, source_target_pairs={{0,1},{1,0},{2,3},{3,2},{4,5},{5,4},{6,7},{7,6},{8,9},{9,8},{10,11... | collective-permute-start | bytes 1376264 | tf_op jit(solution)/shard_map/ppermute | solution.py:377
  13.2 2.4 %collective-permute-done.3 = bf16[16,4224]{1,0:T(8,128)(2,1)S(1)} collective-permute-done((bf16[16,4224]{1,0:T(8,128)(2,1)}, bf16[16,4224]{1,0:T(8,128)(2,1)S(1)}, u32[]{:S(2)}, u32[]{:S(2)}) %collective-permute-start.3) | collective-permute-done | bytes 135200 | tf_op jit(solution)/shard_map/ppermute | solution.py:377
  15.6 6.9 %collective-permute-done.2 = bf16[16,4224]{1,0:T(8,128)(2,1)S(1)} collective-permute-done((bf16[16,4224]{1,0:T(8,128)(2,1)}, bf16[16,4224]{1,0:T(8,128)(2,1)S(1)}, u32[]{:S(2)}, u32[]{:S(2)}) %collective-permute-start.2) | collective-permute-done | bytes 135200 | tf_op jit(solution)/shard_map/ppermute | solution.py:377
  22.5 0.9 pad_maximum_fusion
  23.5 1.6 %collective-permute-start.4 = (bf16[64,4224]{1,0:T(8,128)(2,1)S(1)}, bf16[64,4224]{1,0:T(8,128)(2,1)S(1)}, u32[]{:S(2)}, u32[]{:S(2)}) collective-permute-start(bf16[64,4224]{1,0:T(8,128)(2,1)S(1)} %pad_maximum_fusion), channel_id=1, source_target_pairs={{0,4},{1,5},{2,3},{3,2},{4,0},{5,1},{6,7},{7,6},{8,12},{9,13},{10,... | collective-permute-start | bytes 1622024 | tf_op jit(solution)/shard_map/ppermute | solution.py:382
  25.1 2.2 %collective-permute-start.5 = (bf16[128,512]{1,0:T(8,128)(2,1)S(1)}, bf16[128,512]{1,0:T(8,128)(2,1)S(1)}, u32[]{:S(2)}, u32[]{:S(2)}) collective-permute-start(bf16[128,512]{1,0:T(8,128)(2,1)S(1)} %copy-done.5), channel_id=1, source_target_pairs={{0,16},{1,17},{2,18},{3,19},{4,20},{5,21},{6,22},{7,23},{8,24},{9,... | collective-permute-start | bytes 393224 | tf_op jit(solution)/shard_map/ppermute | solution.py:377
  27.3 5.7 %collective-permute-done.5 = bf16[128,512]{1,0:T(8,128)(2,1)S(1)} collective-permute-done((bf16[128,512]{1,0:T(8,128)(2,1)S(1)}, bf16[128,512]{1,0:T(8,128)(2,1)S(1)}, u32[]{:S(2)}, u32[]{:S(2)}) %collective-permute-start.5) | collective-permute-done | bytes 131104 | tf_op jit(solution)/shard_map/ppermute | solution.py:377
  33.0 1.5 collective-permute-start.6
  34.6 1.3 collective-permute-start.7
  35.9 6.7 %collective-permute-done.7 = bf16[256,512]{1,0:T(8,128)(2,1)S(1)} collective-permute-done((bf16[256,512]{1,0:T(8,128)(2,1)S(1)}, bf16[256,512]{1,0:T(8,128)(2,1)S(1)}, u32[]{:S(2)}, u32[]{:S(2)}) %collective-permute-start.7) | collective-permute-done | bytes 262176 | tf_op jit(solution)/shard_map/ppermute | solution.py:377
  42.7 0.4 collective-permute-start.8
  43.2 9.5 %collective-permute-done.8 = bf16[512,512]{1,0:T(8,128)(2,1)S(1)} collective-permute-done((bf16[512,512]{1,0:T(8,128)(2,1)S(1)}, bf16[512,512]{1,0:T(8,128)(2,1)S(1)}, u32[]{:S(2)}, u32[]{:S(2)}) %collective-permute-start.8) | collective-permute-done | bytes 524320 | tf_op jit(solution)/shard_map/ppermute | solution.py:382
  52.7 1.0 collective-permute-start.10
  53.7 1.5 collective-permute-start.12
  55.3 0.4 collective-permute-start.11
  55.8 0.1 pad_add_fusion.source_segments
  55.9 0.1 collective-permute-done.10.refs_3_
  56.0 2.3 %self_lower.1 = (bf16[512,512]{1,0:T(8,128)(2,1)S(1)}, bf16[768,1024]{1,0:T(8,128)(2,1)S(1)}, bf16[768,512]{1,0:T(8,128)(2,1)S(1)}, f32[8,512]{1,0:T(8,128)S(1)}...) custom-call(s32[2]{0:T(128)S(1)} %copy-done.2, ...), custom_call_target="tpu_custom_call" | custom-call | flops 1000 | bytes 4194304 | tf_op jit(solution)/shard_map/self_lower/pallas_call | solution.py:912
  58.4 9.6 %forward.1 = (bf16[512,512]{1,0:T(8,128)(2,1)S(1)}, f32[8,512]{1,0:T(8,128)S(1)}, f32[512,512]{1,0:T(8,128)S(1)}, bf16[512,512]{1,0:T(8,128)(2,1)S(1)}, bf16[512...) custom-call(s32[2]{0:T(128)S(1)} %copy-done.2, ...), custom_call_target="tpu_custom_call" | custom-call | flops 1000 | bytes 4194304 | tf_op jit(solution)/shard_map/forward/pallas_call | solution.py:912
  68.0 0.6 collective-permute-done.12.refs_1_
  68.6 2.7 %collective-permute-done.13.refs_3_ = bf16[1024,512]{1,0:T(8,128)(2,1)S(1)} collective-permute-done((bf16[1024,512]{1,0:T(8,128)(2,1)S(1)}, bf16[1024,512]{1,0:T(8,128)(2,1)S(1)}, u32[]{:S(2)}, u32[]{:S(2)}) %collective-permute-start.13) | collective-permute-done | bytes 1048608 | tf_op jit(solution)/shard_map/ppermute | solution.py:377
  71.3 10.8 %feed.1 = (f32[512,512]{1,0:T(8,128)S(1)}, f32[512,512]{1,0:T(8,128)S(1)}, bf16[2048,512]{1,0:T(8,128)(2,1)S(1)}, bf16[2048,512]{1,0:T(8,128)(2,1)S(1)}, f32[1,2048]{1,0:T(1,128)S(1)}) custom-call(s32[2]{0:T(128)S(1)} %copy-done.2, f32[512,512]{1,0:T(8,128)S(1)} %get-tuple-element.116.after_cross, bf16[512,512]{1,0:T(8,128)(2,1)S(1)} %bitcast.21, ...), custom_call_target="tpu_custom_call" | custom-call | flops 10000000000 | bytes 4194304 | tf_op jit(solution)/shard_map/feed/pallas_call | solution.py:912
  82.1 0.2 collective-permute-start.14
  82.3 1.8 %feed_last.1 = (bf16[512,512]{1,0:T(8,128)(2,1)}, f32[512,512]{1,0:T(8,128)S(1)}, f32[8,512]{1,0:T(8,128)S(1)}) custom-call(s32[2]{0:T(128)S(1)} %copy-done.2, f32[512,512]{1,0:T(8,128)S(1)} %get-tuple-element.116.after_cross, bf16[512,512]{1,0:T(8,128)(2,1)S(1)} %bitcast.22, f32[8,512]{1,0:T(8,128)S(1)} %get-tuple-element.112.vectors, ...), custom_call_target="tpu_custom_call" | custom-call | flops 2000000000 | bytes 4194304 | tf_op jit(solution)/shard_map/feed_last/pallas_call | solution.py:912
  84.1 2.2 %collective-permute-done.14 = bf16[2048,512]{1,0:T(8,128)(2,1)S(1)} collective-permute-done((bf16[2048,512]{1,0:T(8,128)(2,1)S(1)}, bf16[2048,512]{1,0:T(8,128)(2,1)S(1)}, u32[]{:S(2)}, u32[]{:S(2)}) %collective-permute-start.14) | collective-permute-done | bytes 2097184 | tf_op jit(solution)/shard_map/ppermute | solution.py:377
  86.3 0.2 slice_add_fusion
  86.5 1.5 collective-permute-start.16
  88.1 8.8 %cross_backward.1 = (bf16[512,512]{1,0:T(8,128)(2,1)S(1)}, f32[192,512]{1,0:T(8,128)S(1)}, bf16[192,512]{1,0:T(8,128)(2,1)S(1)}, bf16[512,1536]{1,0:T(8,128)(2,1)S(1)}) custom-call(s32[2]{0:T(128)S(1)} %copy-done.2, s32[1,1024]{1,0:T(1,128)S(1)} %copy-done.3, s32[1,384]{1,0:T(1,128)S(1)} %pad_add_fusion.source_segments, bf16[192,512]{1,0:T(8,128)(2,1)S(1)} %copy-done.1, ...), custom_call_target="tpu_custom_call" | custom-call | flops 10000000000 | bytes 4194304 | tf_op jit(solution)/shard_map/cross_backward/pallas_call | solution.py:912
  96.8 3.3 %cross_weights.1 = (f32[512,512]{1,0:T(8,128)S(1)}, bf16[512,512]{1,0:T(8,128)(2,1)S(1)}, f32[8,512]{1,0:T(8,128)S(1)}, bf16[256,2560]{1,0:T(8,128)(2,1)S(1)}, b...) custom-call(s32[2]{0:T(128)S(1)} %copy-done.2, f32[512,512]{1,0:T(8,128)S(1)} %get-tuple-element.125.after_self, ...), custom_call_target="tpu_custom_call" | custom-call | flops 6000000000 | bytes 4194304 | tf_op jit(solution)/shard_map/cross_weights/pallas_call | solution.py:912
  100.1 0.1 collective-permute-start.15
  100.2 1.2 collective-permute-done.16
  101.5 1.7 %collective-permute-start.18 = (bf16[512,512]{1,0:T(8,128)(2,1)S(1)}, bf16[512,512]{1,0:T(8,128)(2,1)S(1)}, u32[]{:S(2)}, u32[]{:S(2)}) collective-permute-start(bf16[512,512]{1,0:T(8,128)(2,1)S(1)} %slice_add_fusion.5), channel_id=1, source_target_pairs={{0,4},{1,5},{2,3},{3,2},{4,0},{5,1},{6,7},{7,6},{8,12},{9,13},{10,... | collective-permute-start | bytes 1572872 | tf_op jit(solution)/shard_map/ppermute | solution.py:382
  103.2 0.2 slice_add_fusion.2
  103.4 1.5 collective-permute-start.17
  104.9 10.5 %self_backward.1 = (f32[512,512]{1,0:T(8,128)S(1)}, bf16[448,512]{1,0:T(8,128)(2,1)S(1)}, bf16[256,1664]{1,0:T(8,128)(2,1)S(1)}, bf16[256,1664]{1,0:T(8,128)(2,1)S(1)}) custom-call(s32[2]{0:T(128)S(1)} %copy-done.2, s32[1,1024]{1,0:T(1,128)S(1)} %copy-done.3, bf16[512,512]{1,0:T(8,128)(2,1)S(1)} %bitcast.19, bf16[256,512]{1,0:T(8,128)(2,1)S(1)} %slice.175.window, ...), custom_call_target="tpu_custom_call" | custom-call | flops 16000000000 | bytes 4194304 | tf_op jit(solution)/shard_map/self_backward/pallas_call | solution.py:912
  115.4 0.1 collective-permute-start.22
  115.6 0.5 collective-permute-done.17
  116.2 3.5 %collective-permute-start.21 = (bf16[128,512]{1,0:T(8,128)(2,1)S(1)}, bf16[128,512]{1,0:T(8,128)(2,1)S(1)}, u32[]{:S(2)}, u32[]{:S(2)}) collective-permute-start(bf16[128,512]{1,0:T(8,128)(2,1)S(1)} %get-tuple-element.194), channel_id=1, source_target_pairs={{0,24},{1,25},{2,26},{3,27},{4,28},{5,29},{6,30},{7,31},{8,16},{9,... | collective-permute-start | bytes 393224 | tf_op jit(solution)/shard_map/ppermute | solution.py:377
  119.7 0.9 collective-permute-start.19
  120.7 1.7 %collective-permute-start.24 = (bf16[64,2560]{1,0:T(8,128)(2,1)S(1)}, bf16[64,2560]{1,0:T(8,128)(2,1)S(1)}, u32[]{:S(2)}, u32[]{:S(2)}) collective-permute-start(bf16[64,2560]{1,0:T(8,128)(2,1)S(1)} %slice_add_fusion.8), channel_id=1, source_target_pairs={{0,4},{1,5},{2,3},{3,2},{4,0},{5,1},{6,7},{7,6},{8,12},{9,13},{10,... | collective-permute-start | bytes 983048 | tf_op jit(solution)/shard_map/ppermute | solution.py:382
  122.4 0.1 slice_add_fusion.6
  122.5 1.7 %collective-permute-start.23 = (bf16[128,1664]{1,0:T(8,128)(2,1)S(1)}, bf16[128,1664]{1,0:T(8,128)(2,1)S(1)}, u32[]{:S(2)}, u32[]{:S(2)}) collective-permute-start(bf16[128,1664]{1,0:T(8,128)(2,1)S(1)} %get-tuple-element.192), channel_id=1, source_target_pairs={{0,1},{1,0},{2,6},{3,7},{4,5},{5,4},{6,2},{7,3},{8,9},{9,8},{10,14... | collective-permute-start | bytes 1277960 | tf_op jit(solution)/shard_map/ppermute | solution.py:382
  124.2 6.0 %collective-permute-done.24 = bf16[64,2560]{1,0:T(8,128)(2,1)S(1)} collective-permute-done((bf16[64,2560]{1,0:T(8,128)(2,1)S(1)}, bf16[64,2560]{1,0:T(8,128)(2,1)S(1)}, u32[]{:S(2)}, u32[]{:S(2)}) %collective-permute-start.24) | collective-permute-done | bytes 327712 | tf_op jit(solution)/shard_map/ppermute | solution.py:382
  130.3 1.8 %collective-permute-done.23 = bf16[128,1664]{1,0:T(8,128)(2,1)S(1)} collective-permute-done((bf16[128,1664]{1,0:T(8,128)(2,1)S(1)}, bf16[128,1664]{1,0:T(8,128)(2,1)S(1)}, u32[]{:S(2)}, u32[]{:S(2)}) %collective-permute-start.23) | collective-permute-done | bytes 426016 | tf_op jit(solution)/shard_map/ppermute | solution.py:382
  132.1 1.7 %collective-permute-start.29 = (bf16[64,1664]{1,0:T(8,128)(2,1)S(1)}, bf16[64,1664]{1,0:T(8,128)(2,1)S(1)}, u32[]{:S(2)}, u32[]{:S(2)}) collective-permute-start(bf16[64,1664]{1,0:T(8,128)(2,1)S(1)} %slice_add_fusion.11), channel_id=1, source_target_pairs={{0,4},{1,5},{2,3},{3,2},{4,0},{5,1},{6,7},{7,6},{8,12},{9,13},{10,... | collective-permute-start | bytes 638984 | tf_op jit(solution)/shard_map/ppermute | solution.py:382
  133.9 1.5 collective-permute-start.25
  135.4 2.6 %collective-permute-done.29 = bf16[64,1664]{1,0:T(8,128)(2,1)S(1)} collective-permute-done((bf16[64,1664]{1,0:T(8,128)(2,1)S(1)}, bf16[64,1664]{1,0:T(8,128)(2,1)S(1)}, u32[]{:S(2)}, u32[]{:S(2)}) %collective-permute-start.29) | collective-permute-done | bytes 213024 | tf_op jit(solution)/shard_map/ppermute | solution.py:382
  138.1 3.5 %collective-permute-start.32 = (bf16[16,1664]{1,0:T(8,128)(2,1)S(1)}, bf16[16,1664]{1,0:T(8,128)(2,1)S(1)}, u32[]{:S(2)}, u32[]{:S(2)}) collective-permute-start(bf16[16,1664]{1,0:T(8,128)(2,1)S(1)} %get-tuple-element.202), channel_id=1, source_target_pairs={{0,24},{1,25},{2,26},{3,27},{4,28},{5,29},{6,30},{7,31},{8,16},{9,... | collective-permute-start | bytes 159752 | tf_op jit(solution)/shard_map/ppermute | solution.py:377
  141.6 0.4 collective-permute-start.28
  142.0 0.5 collective-permute-start.27
  142.5 3.5 %collective-permute-start.26 = (bf16[16,2560]{1,0:T(8,128)(2,1)S(1)}, bf16[16,2560]{1,0:T(8,128)(2,1)S(1)}, u32[]{:S(2)}, u32[]{:S(2)}) collective-permute-start(bf16[16,2560]{1,0:T(8,128)(2,1)S(1)} %get-tuple-element.200), channel_id=1, source_target_pairs={{0,8},{1,9},{2,10},{3,11},{4,12},{5,13},{6,14},{7,15},{8,0},{9,1},... | collective-permute-start | bytes 245768 | tf_op jit(solution)/shard_map/ppermute | solution.py:377
  146.0 2.3 %collective-permute-start.31 = (bf16[16,1664]{1,0:T(8,128)(2,1)S(1)}, bf16[16,1664]{1,0:T(8,128)(2,1)S(1)}, u32[]{:S(2)}, u32[]{:S(2)}) collective-permute-start(bf16[16,1664]{1,0:T(8,128)(2,1)S(1)} %get-tuple-element.203), channel_id=1, source_target_pairs={{0,16},{1,17},{2,18},{3,19},{4,20},{5,21},{6,22},{7,23},{8,24},{9,... | collective-permute-start | bytes 159752 | tf_op jit(solution)/shard_map/ppermute | solution.py:377
  148.3 0.5 collective-permute-start.30
  148.8 0.8 convert_add_fusion
  149.6 2.3 %target_grad.1 = f32[512,512]{1,0:T(8,128)} custom-call(s32[2]{0:T(128)S(1)} %copy-done.2, f32[512,512]{1,0:T(8,128)S(1)} %get-tuple-element.151.back, bf16[256,512]{1,0:T(8,128)(2,1)S(1)} %slice.185.came, bf16[512,512]{1,0:T(8,128)(2,1)S(1)} %bitcast.20, f32[512,512]{1,0:T(8,128)S(1)} %get-tuple-element.161.self_grad, f32[8,512]{1,0:T(8,128)S(1)} %get-tuple-element.112.vectors), custom_call_target="tpu_custom_call" | custom-call | flops 1000000 | bytes 4194304 | tf_op jit(solution)/shard_map/target_grad/pallas_call | solution.py:912
  151.9 1.0 collective-permute-done.31.refs_10_
  152.9 0.5 collective-permute-done.30.refs_9_
  153.4 1.4 finish.1
  (57 shorter events, 0.9 us)
Async XLA Ops:
  5.8 19.3 %copy-start.5 = (bf16[128,512]{1,0:T(8,128)(2,1)S(1)}, bf16[128,512]{1,0:T(8,128)(2,1)}, u32[]{:S(2)}) copy-start(bf16[128,512]{1,0:T(8,128)(2,1)} %get-tuple-element.108) | copy-start | bytes 393220
  5.8 9.8 %collective-permute-start.3 = (bf16[16,4224]{1,0:T(8,128)(2,1)}, bf16[16,4224]{1,0:T(8,128)(2,1)S(1)}, u32[]{:S(2)}, u32[]{:S(2)}) collective-permute-start(bf16[16,4224]{1,0:T(8,128)(2,1)} %get-tuple-element.105), channel_id=1, source_target_pairs={{0,24},{1,25},{2,26},{3,27},{4,28},{5,29},{6,30},{7,31},{8,16},{9,... | collective-permute-start | bytes 405512 | tf_op jit(solution)/shard_map/ppermute | solution.py:377
  10.9 11.6 %collective-permute-start.2 = (bf16[16,4224]{1,0:T(8,128)(2,1)}, bf16[16,4224]{1,0:T(8,128)(2,1)S(1)}, u32[]{:S(2)}, u32[]{:S(2)}) collective-permute-start(bf16[16,4224]{1,0:T(8,128)(2,1)} %get-tuple-element.105), channel_id=1, source_target_pairs={{0,16},{1,17},{2,18},{3,19},{4,20},{5,21},{6,22},{7,23},{8,24},{9,... | collective-permute-start | bytes 405512 | tf_op jit(solution)/shard_map/ppermute | solution.py:377
  10.9 11.6 %collective-permute-start.1 = (bf16[16,4224]{1,0:T(8,128)(2,1)}, bf16[16,4224]{1,0:T(8,128)(2,1)S(1)}, u32[]{:S(2)}, u32[]{:S(2)}) collective-permute-start(bf16[16,4224]{1,0:T(8,128)(2,1)} %get-tuple-element.105), channel_id=1, source_target_pairs={{0,8},{1,9},{2,10},{3,11},{4,12},{5,13},{6,14},{7,15},{8,0},{9,1},... | collective-permute-start | bytes 405512 | tf_op jit(solution)/shard_map/ppermute | solution.py:377
  11.6 11.9 %collective-permute-start = (bf16[448,512]{1,0:T(8,128)(2,1)}, bf16[448,512]{1,0:T(8,128)(2,1)S(1)}, u32[]{:S(2)}, u32[]{:S(2)}) collective-permute-start(bf16[448,512]{1,0:T(8,128)(2,1)} %get-tuple-element.104), channel_id=1, source_target_pairs={{0,1},{1,0},{2,3},{3,2},{4,5},{5,4},{6,7},{7,6},{8,9},{9,8},{10,11... | collective-permute-start | bytes 1376264 | tf_op jit(solution)/shard_map/ppermute | solution.py:377
  23.5 9.5 %collective-permute-start.4 = (bf16[64,4224]{1,0:T(8,128)(2,1)S(1)}, bf16[64,4224]{1,0:T(8,128)(2,1)S(1)}, u32[]{:S(2)}, u32[]{:S(2)}) collective-permute-start(bf16[64,4224]{1,0:T(8,128)(2,1)S(1)} %pad_maximum_fusion), channel_id=1, source_target_pairs={{0,4},{1,5},{2,3},{3,2},{4,0},{5,1},{6,7},{7,6},{8,12},{9,13},{10,... | collective-permute-start | bytes 1622024 | tf_op jit(solution)/shard_map/ppermute | solution.py:382
  25.1 7.9 %collective-permute-start.5 = (bf16[128,512]{1,0:T(8,128)(2,1)S(1)}, bf16[128,512]{1,0:T(8,128)(2,1)S(1)}, u32[]{:S(2)}, u32[]{:S(2)}) collective-permute-start(bf16[128,512]{1,0:T(8,128)(2,1)S(1)} %copy-done.5), channel_id=1, source_target_pairs={{0,16},{1,17},{2,18},{3,19},{4,20},{5,21},{6,22},{7,23},{8,24},{9,... | collective-permute-start | bytes 393224 | tf_op jit(solution)/shard_map/ppermute | solution.py:377
  33.0 19.6 %collective-permute-start.6 = (bf16[128,4224]{1,0:T(8,128)(2,1)S(1)}, bf16[128,4224]{1,0:T(8,128)(2,1)S(1)}, u32[]{:S(2)}, u32[]{:S(2)}) collective-permute-start(bf16[128,4224]{1,0:T(8,128)(2,1)S(1)} %constant_dynamic-update-slice_fusion.refs_0_), channel_id=1, source_target_pairs={{0,1},{1,0},{2,6},{3,7},{4,5},{5,4},{6,2},{7,3},{8,9},{9,8},{10,14... | collective-permute-start | bytes 3244040 | tf_op jit(solution)/shard_map/ppermute | solution.py:382
  34.6 8.0 %collective-permute-start.7 = (bf16[256,512]{1,0:T(8,128)(2,1)S(1)}, bf16[256,512]{1,0:T(8,128)(2,1)S(1)}, u32[]{:S(2)}, u32[]{:S(2)}) collective-permute-start(bf16[256,512]{1,0:T(8,128)(2,1)S(1)} %pad_maximum_fusion.2), channel_id=1, source_target_pairs={{0,8},{1,9},{2,10},{3,11},{4,12},{5,13},{6,14},{7,15},{8,0},{9,1},... | collective-permute-start | bytes 786440 | tf_op jit(solution)/shard_map/ppermute | solution.py:377
  42.7 13.0 %copy-start.6 = (s32[1,336]{1,0:T(1,128)S(1)}, s32[1,336]{1,0:T(1,128)}, u32[]{:S(2)}) copy-start(s32[1,336]{1,0:T(1,128)} %param.23) | copy-start | bytes 4036
  42.7 10.0 %collective-permute-start.8 = (bf16[512,512]{1,0:T(8,128)(2,1)S(1)}, bf16[512,512]{1,0:T(8,128)(2,1)S(1)}, u32[]{:S(2)}, u32[]{:S(2)}) collective-permute-start(bf16[512,512]{1,0:T(8,128)(2,1)S(1)} %pad_maximum_fusion.1), channel_id=1, source_target_pairs={{0,4},{1,5},{2,3},{3,2},{4,0},{5,1},{6,7},{7,6},{8,12},{9,13},{10,... | collective-permute-start | bytes 1572872 | tf_op jit(solution)/shard_map/ppermute | solution.py:382
  43.1 12.9 %collective-permute-start.9 = (bf16[128,4224]{1,0:T(8,128)(2,1)S(1)}, bf16[128,4224]{1,0:T(8,128)(2,1)S(1)}, u32[]{:S(2)}, u32[]{:S(2)}) collective-permute-start(bf16[128,4224]{1,0:T(8,128)(2,1)S(1)} %constant_dynamic-update-slice_fusion.refs_0_), channel_id=1, source_target_pairs={{0,2},{1,3},{2,0},{3,1},{4,6},{5,7},{6,4},{7,5},{8,10},{9,11},{10,... | collective-permute-start | bytes 3244040 | tf_op jit(solution)/shard_map/ppermute | solution.py:377
  43.2 12.8 %copy-start = (bf16[1,512,512]{2,1,0:T(8,128)(2,1)S(1)}, bf16[1,512,512]{2,1,0:T(8,128)(2,1)}, u32[]{:S(2)}) copy-start(bf16[1,512,512]{2,1,0:T(8,128)(2,1)} %param.20) | copy-start | bytes 1572868
  43.2 12.8 %copy-start.2 = (s32[2]{0:T(128)S(1)}, s32[2]{0:T(128)}, u32[]{:S(2)}) copy-start(s32[2]{0:T(128)} %pad_add_fusion.1.place) | copy-start | bytes 28
  52.7 3.4 %collective-permute-start.10 = (bf16[128,4224]{1,0:T(8,128)(2,1)S(1)}, bf16[128,4224]{1,0:T(8,128)(2,1)S(1)}, u32[]{:S(2)}, u32[]{:S(2)}) collective-permute-start(bf16[128,4224]{1,0:T(8,128)(2,1)S(1)} %collective-permute-done.6.refs_1_), channel_id=1, source_target_pairs={{0,2},{1,3},{2,0},{3,1},{4,6},{5,7},{6,4},{7,5},{8,10},{9,11},{10,... | collective-permute-start | bytes 3244040 | tf_op jit(solution)/shard_map/ppermute | solution.py:377
  53.7 14.9 %collective-permute-start.12 = (bf16[1024,512]{1,0:T(8,128)(2,1)S(1)}, bf16[1024,512]{1,0:T(8,128)(2,1)S(1)}, u32[]{:S(2)}, u32[]{:S(2)}) collective-permute-start(bf16[1024,512]{1,0:T(8,128)(2,1)S(1)} %constant_dynamic-update-slice_fusion.2.refs_0_), channel_id=1, source_target_pairs={{0,1},{1,0},{2,6},{3,7},{4,5},{5,4},{6,2},{7,3},{8,9},{9,8},{10,14... | collective-permute-start | bytes 3145736 | tf_op jit(solution)/shard_map/ppermute | solution.py:382
  55.3 13.3 %collective-permute-start.11 = (bf16[1024,512]{1,0:T(8,128)(2,1)S(1)}, bf16[1024,512]{1,0:T(8,128)(2,1)S(1)}, u32[]{:S(2)}, u32[]{:S(2)}) collective-permute-start(bf16[1024,512]{1,0:T(8,128)(2,1)S(1)} %constant_dynamic-update-slice_fusion.2.refs_0_), channel_id=1, source_target_pairs={{0,2},{1,3},{2,0},{3,1},{4,6},{5,7},{6,4},{7,5},{8,10},{9,11},{10,... | collective-permute-start | bytes 3145736 | tf_op jit(solution)/shard_map/ppermute | solution.py:377
  55.9 2.5 %copy-start.1 = (bf16[192,512]{1,0:T(8,128)(2,1)S(1)}, bf16[192,512]{1,0:T(8,128)(2,1)}, u32[]{:S(2)}) copy-start(bf16[192,512]{1,0:T(8,128)(2,1)} %get-tuple-element.103.own_source) | copy-start | bytes 589828
  55.9 2.5 %copy-start.3 = (s32[1,1024]{1,0:T(1,128)S(1)}, s32[1,1024]{1,0:T(1,128)}, u32[]{:S(2)}) copy-start(s32[1,1024]{1,0:T(1,128)} %segments.5) | copy-start | bytes 12292
  58.4 12.9 %copy-start.4 = (bf16[1,512,512]{2,1,0:T(8,128)(2,1)S(1)}, bf16[1,512,512]{2,1,0:T(8,128)(2,1)}, u32[]{:S(2)}) copy-start(bf16[1,512,512]{2,1,0:T(8,128)(2,1)} %param.24) | copy-start | bytes 1572868
  68.6 2.7 %collective-permute-start.13 = (bf16[1024,512]{1,0:T(8,128)(2,1)S(1)}, bf16[1024,512]{1,0:T(8,128)(2,1)S(1)}, u32[]{:S(2)}, u32[]{:S(2)}) collective-permute-start(bf16[1024,512]{1,0:T(8,128)(2,1)S(1)} %collective-permute-done.12.refs_1_), channel_id=1, source_target_pairs={{0,2},{1,3},{2,0},{3,1},{4,6},{5,7},{6,4},{7,5},{8,10},{9,11},{10,... | collective-permute-start | bytes 3145736 | tf_op jit(solution)/shard_map/ppermute | solution.py:377
  82.1 4.2 %collective-permute-start.14 = (bf16[2048,512]{1,0:T(8,128)(2,1)S(1)}, bf16[2048,512]{1,0:T(8,128)(2,1)S(1)}, u32[]{:S(2)}, u32[]{:S(2)}) collective-permute-start(bf16[2048,512]{1,0:T(8,128)(2,1)S(1)} %get-tuple-element.130), channel_id=1, source_target_pairs={{0,2},{1,3},{2,0},{3,1},{4,6},{5,7},{6,4},{7,5},{8,10},{9,11},{10,... | collective-permute-start | bytes 6291464 | tf_op jit(solution)/shard_map/ppermute | solution.py:377
  86.5 14.9 %collective-permute-start.16 = (bf16[1024,512]{1,0:T(8,128)(2,1)S(1)}, bf16[1024,512]{1,0:T(8,128)(2,1)S(1)}, u32[]{:S(2)}, u32[]{:S(2)}) collective-permute-start(bf16[1024,512]{1,0:T(8,128)(2,1)S(1)} %get-tuple-element.189), channel_id=1, source_target_pairs={{0,1},{1,0},{2,6},{3,7},{4,5},{5,4},{6,2},{7,3},{8,9},{9,8},{10,14... | collective-permute-start | bytes 3145736 | tf_op jit(solution)/shard_map/ppermute | solution.py:382
  100.1 3.1 %collective-permute-start.15 = (bf16[256,2560]{1,0:T(8,128)(2,1)S(1)}, bf16[256,2560]{1,0:T(8,128)(2,1)S(1)}, u32[]{:S(2)}, u32[]{:S(2)}) collective-permute-start(bf16[256,2560]{1,0:T(8,128)(2,1)S(1)} %get-tuple-element.142), channel_id=1, source_target_pairs={{0,2},{1,3},{2,0},{3,1},{4,6},{5,7},{6,4},{7,5},{8,10},{9,11},{10,... | collective-permute-start | bytes 3932168 | tf_op jit(solution)/shard_map/ppermute | solution.py:377
  101.5 14.1 %collective-permute-start.18 = (bf16[512,512]{1,0:T(8,128)(2,1)S(1)}, bf16[512,512]{1,0:T(8,128)(2,1)S(1)}, u32[]{:S(2)}, u32[]{:S(2)}) collective-permute-start(bf16[512,512]{1,0:T(8,128)(2,1)S(1)} %slice_add_fusion.5), channel_id=1, source_target_pairs={{0,4},{1,5},{2,3},{3,2},{4,0},{5,1},{6,7},{7,6},{8,12},{9,13},{10,... | collective-permute-start | bytes 1572872 | tf_op jit(solution)/shard_map/ppermute | solution.py:382
  103.4 12.7 %collective-permute-start.17 = (bf16[128,2560]{1,0:T(8,128)(2,1)S(1)}, bf16[128,2560]{1,0:T(8,128)(2,1)S(1)}, u32[]{:S(2)}, u32[]{:S(2)}) collective-permute-start(bf16[128,2560]{1,0:T(8,128)(2,1)S(1)} %get-tuple-element.191), channel_id=1, source_target_pairs={{0,1},{1,0},{2,6},{3,7},{4,5},{5,4},{6,2},{7,3},{8,9},{9,8},{10,14... | collective-permute-start | bytes 1966088 | tf_op jit(solution)/shard_map/ppermute | solution.py:382
  115.4 7.0 %collective-permute-start.22 = (bf16[256,1664]{1,0:T(8,128)(2,1)S(1)}, bf16[256,1664]{1,0:T(8,128)(2,1)S(1)}, u32[]{:S(2)}, u32[]{:S(2)}) collective-permute-start(bf16[256,1664]{1,0:T(8,128)(2,1)S(1)} %get-tuple-element.155), channel_id=1, source_target_pairs={{0,2},{1,3},{2,0},{3,1},{4,6},{5,7},{6,4},{7,5},{8,10},{9,11},{10,... | collective-permute-start | bytes 2555912 | tf_op jit(solution)/shard_map/ppermute | solution.py:377
  116.2 17.7 %collective-permute-start.21 = (bf16[128,512]{1,0:T(8,128)(2,1)S(1)}, bf16[128,512]{1,0:T(8,128)(2,1)S(1)}, u32[]{:S(2)}, u32[]{:S(2)}) collective-permute-start(bf16[128,512]{1,0:T(8,128)(2,1)S(1)} %get-tuple-element.194), channel_id=1, source_target_pairs={{0,24},{1,25},{2,26},{3,27},{4,28},{5,29},{6,30},{7,31},{8,16},{9,... | collective-permute-start | bytes 393224 | tf_op jit(solution)/shard_map/ppermute | solution.py:377
  119.7 14.1 %collective-permute-start.20 = (bf16[128,512]{1,0:T(8,128)(2,1)S(1)}, bf16[128,512]{1,0:T(8,128)(2,1)S(1)}, u32[]{:S(2)}, u32[]{:S(2)}) collective-permute-start(bf16[128,512]{1,0:T(8,128)(2,1)S(1)} %get-tuple-element.195), channel_id=1, source_target_pairs={{0,16},{1,17},{2,18},{3,19},{4,20},{5,21},{6,22},{7,23},{8,24},{9,... | collective-permute-start | bytes 393224 | tf_op jit(solution)/shard_map/ppermute | solution.py:377
  119.7 14.1 %collective-permute-start.19 = (bf16[128,512]{1,0:T(8,128)(2,1)S(1)}, bf16[128,512]{1,0:T(8,128)(2,1)S(1)}, u32[]{:S(2)}, u32[]{:S(2)}) collective-permute-start(bf16[128,512]{1,0:T(8,128)(2,1)S(1)} %get-tuple-element.196), channel_id=1, source_target_pairs={{0,8},{1,9},{2,10},{3,11},{4,12},{5,13},{6,14},{7,15},{8,0},{9,1},... | collective-permute-start | bytes 393224 | tf_op jit(solution)/shard_map/ppermute | solution.py:377
  120.7 9.5 %collective-permute-start.24 = (bf16[64,2560]{1,0:T(8,128)(2,1)S(1)}, bf16[64,2560]{1,0:T(8,128)(2,1)S(1)}, u32[]{:S(2)}, u32[]{:S(2)}) collective-permute-start(bf16[64,2560]{1,0:T(8,128)(2,1)S(1)} %slice_add_fusion.8), channel_id=1, source_target_pairs={{0,4},{1,5},{2,3},{3,2},{4,0},{5,1},{6,7},{7,6},{8,12},{9,13},{10,... | collective-permute-start | bytes 983048 | tf_op jit(solution)/shard_map/ppermute | solution.py:382
  122.5 9.6 %collective-permute-start.23 = (bf16[128,1664]{1,0:T(8,128)(2,1)S(1)}, bf16[128,1664]{1,0:T(8,128)(2,1)S(1)}, u32[]{:S(2)}, u32[]{:S(2)}) collective-permute-start(bf16[128,1664]{1,0:T(8,128)(2,1)S(1)} %get-tuple-element.192), channel_id=1, source_target_pairs={{0,1},{1,0},{2,6},{3,7},{4,5},{5,4},{6,2},{7,3},{8,9},{9,8},{10,14... | collective-permute-start | bytes 1277960 | tf_op jit(solution)/shard_map/ppermute | solution.py:382
  132.1 5.9 %collective-permute-start.29 = (bf16[64,1664]{1,0:T(8,128)(2,1)S(1)}, bf16[64,1664]{1,0:T(8,128)(2,1)S(1)}, u32[]{:S(2)}, u32[]{:S(2)}) collective-permute-start(bf16[64,1664]{1,0:T(8,128)(2,1)S(1)} %slice_add_fusion.11), channel_id=1, source_target_pairs={{0,4},{1,5},{2,3},{3,2},{4,0},{5,1},{6,7},{7,6},{8,12},{9,13},{10,... | collective-permute-start | bytes 638984 | tf_op jit(solution)/shard_map/ppermute | solution.py:382
  133.9 14.4 %collective-permute-start.25 = (bf16[448,512]{1,0:T(8,128)(2,1)S(1)}, bf16[448,512]{1,0:T(8,128)(2,1)S(1)}, u32[]{:S(2)}, u32[]{:S(2)}) collective-permute-start(bf16[448,512]{1,0:T(8,128)(2,1)S(1)} %get-tuple-element.160), channel_id=1, source_target_pairs={{0,1},{1,0},{2,3},{3,2},{4,5},{5,4},{6,7},{7,6},{8,9},{9,8},{10,11... | collective-permute-start | bytes 1376264 | tf_op jit(solution)/shard_map/ppermute | solution.py:377
  138.1 7.9 %collective-permute-start.32 = (bf16[16,1664]{1,0:T(8,128)(2,1)S(1)}, bf16[16,1664]{1,0:T(8,128)(2,1)S(1)}, u32[]{:S(2)}, u32[]{:S(2)}) collective-permute-start(bf16[16,1664]{1,0:T(8,128)(2,1)S(1)} %get-tuple-element.202), channel_id=1, source_target_pairs={{0,24},{1,25},{2,26},{3,27},{4,28},{5,29},{6,30},{7,31},{8,16},{9,... | collective-permute-start | bytes 159752 | tf_op jit(solution)/shard_map/ppermute | solution.py:377
  141.6 11.8 %collective-permute-start.28 = (bf16[16,2560]{1,0:T(8,128)(2,1)S(1)}, bf16[16,2560]{1,0:T(8,128)(2,1)S(1)}, u32[]{:S(2)}, u32[]{:S(2)}) collective-permute-start(bf16[16,2560]{1,0:T(8,128)(2,1)S(1)} %get-tuple-element.198), channel_id=1, source_target_pairs={{0,24},{1,25},{2,26},{3,27},{4,28},{5,29},{6,30},{7,31},{8,16},{9,... | collective-permute-start | bytes 245768 | tf_op jit(solution)/shard_map/ppermute | solution.py:377
  142.0 11.4 %collective-permute-start.27 = (bf16[16,2560]{1,0:T(8,128)(2,1)S(1)}, bf16[16,2560]{1,0:T(8,128)(2,1)S(1)}, u32[]{:S(2)}, u32[]{:S(2)}) collective-permute-start(bf16[16,2560]{1,0:T(8,128)(2,1)S(1)} %get-tuple-element.199), channel_id=1, source_target_pairs={{0,16},{1,17},{2,18},{3,19},{4,20},{5,21},{6,22},{7,23},{8,24},{9,... | collective-permute-start | bytes 245768 | tf_op jit(solution)/shard_map/ppermute | solution.py:377
  142.5 10.9 %collective-permute-start.26 = (bf16[16,2560]{1,0:T(8,128)(2,1)S(1)}, bf16[16,2560]{1,0:T(8,128)(2,1)S(1)}, u32[]{:S(2)}, u32[]{:S(2)}) collective-permute-start(bf16[16,2560]{1,0:T(8,128)(2,1)S(1)} %get-tuple-element.200), channel_id=1, source_target_pairs={{0,8},{1,9},{2,10},{3,11},{4,12},{5,13},{6,14},{7,15},{8,0},{9,1},... | collective-permute-start | bytes 245768 | tf_op jit(solution)/shard_map/ppermute | solution.py:377
  146.0 6.9 %collective-permute-start.31 = (bf16[16,1664]{1,0:T(8,128)(2,1)S(1)}, bf16[16,1664]{1,0:T(8,128)(2,1)S(1)}, u32[]{:S(2)}, u32[]{:S(2)}) collective-permute-start(bf16[16,1664]{1,0:T(8,128)(2,1)S(1)} %get-tuple-element.203), channel_id=1, source_target_pairs={{0,16},{1,17},{2,18},{3,19},{4,20},{5,21},{6,22},{7,23},{8,24},{9,... | collective-permute-start | bytes 159752 | tf_op jit(solution)/shard_map/ppermute | solution.py:377
  148.3 5.1 %collective-permute-start.30 = (bf16[16,1664]{1,0:T(8,128)(2,1)S(1)}, bf16[16,1664]{1,0:T(8,128)(2,1)S(1)}, u32[]{:S(2)}, u32[]{:S(2)}) collective-permute-start(bf16[16,1664]{1,0:T(8,128)(2,1)S(1)} %get-tuple-element.204), channel_id=1, source_target_pairs={{0,8},{1,9},{2,10},{3,11},{4,12},{5,13},{6,14},{7,15},{8,0},{9,1},... | collective-permute-start | bytes 159752 | tf_op jit(solution)/shard_map/ppermute | solution.py:377

commit v2 on v1

--- a/solution.py
+++ b/solution.py
@@ -688,23 +688,26 @@
 CHUNK, UNROLL = 512, 2
 
 
-def feed_body(place, after_cross, output_grad, vectors, up_bias, *refs):
-    pieces, refs = refs[:4], refs[4:]
-    (
-        total, back, kept, sent, bias_sums, ups, downs, lowered, flipped, up_grads, down_grads,
-    ) = refs
-    me = place[0]
-    places = block_places(me)
-
-    def chunk_of(z):
-        return pl.multiple_of(((me >> 3) ^ z) * CHUNK, CHUNK)
-
+def feed_front_body(place, after_cross, vectors, lowered, flipped):
     gain, shift = vectors[5:6, :], vectors[6:7, :]
     for i in range(4):
         rows = slice(i * TILE, (i + 1) * TILE)
         low = (normed_rows(after_cross[rows, :])[0] * gain + shift).astype(BF16)
         lowered[rows, :] = low
     flipped[...] = lowered[...].T
+
+
+def feed_body(place, lowered, flipped, output_grad, up_bias, *refs):
+    pieces, refs = refs[:4], refs[4:]
+    (
+        total, back, kept, sent, bias_sums, ups, downs, up_grads, down_grads,
+    ) = refs
+    me = place[0]
+    places = block_places(me)
+
+    def chunk_of(z):
+        return pl.multiple_of(((me >> 3) ^ z) * CHUNK, CHUNK)
+
     grad_low = output_grad[...]
     total[...] = jnp.zeros_like(total)
     back[...] = jnp.zeros_like(back)
@@ -752,7 +755,10 @@
     lax.fori_loop(0, 4 // UNROLL, chunks, 0)
 
 
-def feed_last_body(place, after_cross, output_grad, vectors, total, back, layer_out, after_grad, sums):
+def feed_last_body(
+    place, after_cross, output_grad, vectors, total, back, mixed, weight,
+    layer_out, after_grad, sums, mixed_grad, dot_rows, crossout_grad,
+):
     gain = vectors[5:6, :]
     gain_sum, shift_sum, bias_sum = (jnp.zeros((1, MODEL), F32) for _ in range(3))
     for i in range(4):
@@ -766,28 +772,27 @@
         bias_sum = bias_sum + column_sum(grad)
     zero = jnp.zeros((1, MODEL), F32)
     sums[...] = jnp.concatenate([bias_sum, zero, zero, zero, zero, gain_sum, shift_sum, zero], 0)
+    grad_low = after_grad[...].astype(BF16)
+    mixed_grad[...] = against(grad_low, weight[:, 2048:]).astype(BF16)
+    dot_rows[...] = head_dots(mixed_grad[...], mixed[...])
+    crossout_grad[...] = transposed(mixed[...], grad_low).astype(BF16)
 
 
 def cross_back_body(
-    place, segments, source_segments, own_source, other_source, queries, pair, mixed, log_rows, after_grad, weight,
-    asked, source_own, source_send, grads, upstream, query_grad, pair_grad, source, key_seg, query_row,
-    dot_rows,
+    place, segments, source_segments, own_source, other_source, queries, pair, log_rows, upstream, dot_rows, weight,
+    asked, source_own, source_send, grads, query_grad, pair_grad, source, key_seg, query_row,
 ):
     side = place[1]
     key_seg[...] = spread(source_segments[...].astype(F32))
     query_row[...] = own_segments_of(side, segments[...])
     source[:HALF_SOURCE, :] = jnp.where(side == 0, own_source[...], other_source[...])
     source[HALF_SOURCE:, :] = jnp.where(side == 0, other_source[...], own_source[...])
-    grad_low = after_grad[...].astype(BF16)
-    upstream[...] = against(grad_low, weight[:, 2048:]).astype(BF16)
-    dot_rows[...] = head_dots(upstream[...], mixed[...])
-    grads[:, :512] = transposed(mixed[...], grad_low).astype(BF16)
     attend_back(
         queries, upstream, pair, log_rows, dot_rows, query_row, key_seg, query_grad, pair_grad,
         [(0, SOURCES, 0, OWN)],
     )
     asked[...] = (query_grad[...] * SCALE).astype(BF16)
-    grads[:, 512:] = transposed(source[...], pair_grad[...]).astype(BF16)
+    grads[...] = transposed(source[...], pair_grad[...]).astype(BF16)
     back = against(pair_grad[...], weight[:, 1024:2048])
     first, second = back[:HALF_SOURCE], back[HALF_SOURCE:]
     source_own[...] = jnp.where(side == 0, first, second)
@@ -795,11 +800,12 @@
 
 
 def cross_weight_body(
-    place, after_self, lowered, self_mixed, after_grad, asked, vectors, sums, weight, some_grads, *refs
+    place, after_self, lowered, self_mixed, after_grad, asked, vectors, sums, weight, crossout_grad, keyval_grad, *refs
 ):
     self_grad, upstream, dot_rows, kept, sent, new_sums, grads = refs
     me = place[0]
-    store_blocks(me, some_grads, (kept, sent), slice(0, 1536))
+    store_blocks(me, crossout_grad, (kept, sent), slice(0, 512))
+    store_blocks(me, keyval_grad, (kept, sent), slice(512, 1536))
     gain = vectors[3:4, :]
     gain_sum, shift_sum = jnp.zeros((1, MODEL), F32), jnp.zeros((1, MODEL), F32)
     for i in range(2):
@@ -870,7 +876,7 @@
 
 
 def finish_body(place, *refs):
-    feed, cross, last, outs = refs[:4], refs[4:8], refs[8:12], refs[12:]
+    feed, cross, last, outs = refs[:2], refs[2:6], refs[6:10], refs[10:]
     project, output, query, keyval, crossout, up, down, *small = outs
     me = place[0]
 
@@ -932,12 +938,11 @@
     side = lax.axis_index("seq")
     place = jnp.stack([lax.axis_index("rows") * 2 + side, side]).astype(jnp.int32)
     states, grad = target_states[0], output_grad[0]
-    small = jnp.pad(hidden_bias, (112, 80))
+    small = jnp.pad(hidden_bias[None], ((0, 0), (112, 80)))
     for i, vector in enumerate(
         (output_bias, first_gain, first_shift, second_gain, second_shift, third_gain, third_shift)
     ):
-        small = small + jnp.pad(vector, (16 * i, 240 - 16 * i))
-    small = small.reshape(1, 256)
+        small = small + jnp.pad(vector[None], ((0, 0), (16 * i, 240 - 16 * i)))
     one, three, near, own_source = call(
         pack_body, "pack", place,
         [
@@ -1000,45 +1005,54 @@
         1000,
     )
     three_core, three_other = tied((three_core, three_other), after_cross)
-    pieces_three = [three, three_other, three_core, exchange(three_other, FLIP_CORE)]
+    last_piece = exchange(three_other, FLIP_CORE)
+    feed_in = call(
+        feed_front_body, "feed_front", place, [tied(after_cross, three_other), vectors], [],
+        [shape_of(OWN, MODEL), shape_of(MODEL, OWN)], [], 1000,
+    )
+    pieces_three = [three, three_other, three_core, tied(last_piece, feed_in)]
     total, back, feed_kept, feed_sent, bias_sums = call(
-        feed_body, "feed", place, [after_cross, grad, vectors, up_bias], pieces_three,
+        feed_body, "feed", place, [*feed_in, grad, up_bias], pieces_three,
         [shape_of(OWN, MODEL, dtype=F32)] * 2 + [shape_of(2048, MODEL)] * 2 + [shape_of(1, FEED, dtype=F32)],
         [
-            vmem((4, MODEL, CHUNK), BF16), vmem((4, CHUNK, MODEL), BF16), vmem((OWN, MODEL), BF16),
-            vmem((MODEL, OWN), BF16), vmem((4, MODEL, CHUNK), BF16), vmem((4, CHUNK, MODEL), BF16),
+            vmem((4, MODEL, CHUNK), BF16), vmem((4, CHUNK, MODEL), BF16), vmem((4, MODEL, CHUNK), BF16), vmem((4, CHUNK, MODEL), BF16),
         ],
         10000000000,
     )
     feed_came = exchange(feed_sent, FLIP_CORE)
-    layer_out, after_grad, sums = call(
-        feed_last_body, "feed_last", place, [after_cross, grad, vectors, total, back], [],
-        [shape_of(OWN, MODEL), shape_of(OWN, MODEL, dtype=F32), shape_of(8, MODEL, dtype=F32)], [], 2000000000,
+    layer_out, after_grad, sums, upstream_two, dots_two, crossout_grad = call(
+        feed_last_body, "feed_last", place, [after_cross, grad, vectors, total, back, mixed_two, weight_two], [],
+        [
+            shape_of(OWN, MODEL), shape_of(OWN, MODEL, dtype=F32), shape_of(8, MODEL, dtype=F32), shape_of(OWN, MODEL),
+            shape_of(HEADS, OWN, dtype=F32), shape_of(MODEL, MODEL),
+        ],
+        [], 4000000000,
     )
     feed_came = tied(feed_came, after_grad)
     feed_sent, feed_kept = add_halves(feed_kept, feed_came)
-    after_grad = tied(after_grad, feed_sent)
+    upstream_two = tied(upstream_two, feed_sent)
     feed_came = exchange_side(feed_sent, 1)
-    asked, source_own, source_send, some_grads = call(
+    asked, source_own, source_send, keyval_grad = call(
         cross_back_body, "cross_backward", place,
         [
-            target_segments, source_seg, own_source, other_source, queries_two, pair_two, mixed_two, logs_two,
-            after_grad, weight_two,
+            target_segments, source_seg, own_source, other_source, queries_two, pair_two, logs_two,
+            upstream_two, dots_two, weight_two,
         ],
         [],
         [
             shape_of(OWN, MODEL), shape_of(HALF_SOURCE, MODEL, dtype=F32), shape_of(HALF_SOURCE, MODEL),
-            shape_of(MODEL, 1536),
-        ],
-        [
-            vmem((OWN, MODEL), BF16), vmem((OWN, MODEL), F32), vmem((SOURCES, 2 * MODEL), BF16),
-            vmem((SOURCES, MODEL), BF16), vmem((SOURCES, TILE), F32), vmem((1, OWN), F32), vmem((HEADS, OWN), F32),
+            shape_of(MODEL, 1024),
+        ],
+        [
+            vmem((OWN, MODEL), F32), vmem((SOURCES, 2 * MODEL), BF16),
+            vmem((SOURCES, MODEL), BF16), vmem((SOURCES, TILE), F32), vmem((1, OWN), F32),
         ],
         10000000000,
     )
     self_grad, upstream, dot_rows, cross_kept, cross_sent, sums = call(
         cross_weight_body, "cross_weights", place,
-        [after_self, lowered_two, mixed, after_grad, asked, vectors, sums, weight_two, some_grads], [],
+        [after_self, lowered_two, mixed, after_grad, asked, vectors, sums, weight_two, crossout_grad, keyval_grad],
+        [],
         [shape_of(OWN, MODEL, dtype=F32), shape_of(OWN, MODEL), shape_of(HEADS, OWN, dtype=F32)]
         + [shape_of(256, 2560)] * 2 + [shape_of(8, MODEL, dtype=F32)],
         [vmem((MODEL, 1024), BF16)], 6000000000,
@@ -1067,12 +1081,20 @@
     )
     last_came = exchange(last_sent, FLIP_CORE)
     cross_came, feed_came = tied((cross_came, feed_came), own_back)
-    feed = z_blocks(feed_kept + feed_came)
-    cross_came = tied(cross_came, feed[0])
+    feed_kept = feed_kept + feed_came
+    feed_kept, feed_sent = (
+        join(feed_kept[i * 128 : (i + 1) * 128], feed_kept[(i + 2) * 128 : (i + 3) * 128]) for i in range(2)
+    )
+    feed_came = exchange(feed_sent, FLIP_Z)
+    cross_came = tied(cross_came, feed_sent)
     cross_sent, cross_kept = add_halves(cross_kept, cross_came)
-    last_came = tied(last_came, feed[0])
+    last_came = tied(last_came, feed_sent)
     last_sent, last_kept = add_halves(last_kept, last_came)
     last_came, cross_came = exchange_side(last_sent, 1), exchange_side(cross_sent, 0)
+    feed_came = tied(feed_came, last_sent)
+    feed_sent, feed_kept = add_halves(feed_kept, feed_came)
+    feed = [feed_kept, exchange(feed_sent, 2 * FLIP_Z)]
+    cross_came = tied(cross_came, feed_sent)
     cross_kept = cross_kept + cross_came
     last_came = tied(last_came, cross_kept)
     last_sent, last_kept = add_halves(last_kept, last_came)

time: 155 us -> 152 us (0.981)
  waiting for transfers between devices: 50.5 us -> 48.5 us
    ppermute x10, waiting for transfers between devices: 22.3 us -> 15 us  [exchange_side(): lax.ppermute(value, AXES, [(device, device ^ flips[device >> 1 & 1]) for...]
    ppermute x23 -> x22, waiting for transfers between devices: 28.2 us -> 33.4 us  [exchange(): lax.ppermute(value, AXES, [(device, device ^ flip) for device in range(32)])]
    ppermute x23 -> x22, starting transfers between devices: 29.6 us -> 29 us  [exchange(): lax.ppermute(value, AXES, [(device, device ^ flip) for device in range(32)])]
    pallas_call x10 -> x11, Pallas kernels: 53.9 us -> 54 us  [call(): pl.pallas_call(body, name=name, out_shape=outs, in_specs=[SMEM_SPEC] + [H...]
  transfers between devices with their start and end apart: 33 -> 32, of which waited for: 16 -> 16; matrix products, arithmetic and copies ran while one was open for 2% -> 2% of each run, Pallas kernels for 25% -> 26%
where the time goes in v2:
time: 152 us
  Pallas kernels  54 us (36%)
  waiting for transfers between devices  48.5 us (32%)
  starting transfers between devices  43.4 us (29%)
  other arithmetic  4.76 us (3%)
    pallas_call x11, Pallas kernels, call(): pl.pallas_call(body, name=name, out_shape=outs, in_specs=[SMEM_SPEC] + [H...  54 us
    ppermute x22, waiting for transfers between devices, exchange(): lax.ppermute(value, AXES, [(device, device ^ flip) for device in range(32)])  33.4 us
    ppermute x22, starting transfers between devices, exchange(): lax.ppermute(value, AXES, [(device, device ^ flip) for device in range(32)])  29 us
    ppermute x10, waiting for transfers between devices, exchange_side(): lax.ppermute(value, AXES, [(device, device ^ flips[device >> 1 & 1]) for...  15 us
    ppermute x10, starting transfers between devices, exchange_side(): lax.ppermute(value, AXES, [(device, device ^ flips[device >> 1 & 1]) for...  14.4 us
  transfers between devices with their start and end apart: 32, of which 16 were waited for; matrix products, arithmetic and copies ran while one was open for 2% of the time, Pallas kernels for 26%

profile of v2, /device:TPU:0, one launch (start us, length us, event | category | flops | bytes accessed | tf_op | source)
XLA Modules:
  0.0 152.1 jit_solution(12098931035699838685)
XLA Ops:
  0.7 0.6 pad_add_fusion.2.place
  1.2 1.4 pad_add_fusion.1.vectors
  2.7 3.1 %pack.1 = (bf16[16,4224]{1,0:T(8,128)(2,1)}, bf16[128,512]{1,0:T(8,128)(2,1)}, bf16[448,512]{1,0:T(8,128)(2,1)}, bf16[192,512]{1,0:T(8,128)(2,1)}) custom-call(s32[2]{0:T(128)} %pad_add_fusion.2.place, bf16[1,256]{1,0:T(2,128)(2,1)} %pad_add_fusion.1.vectors, bf16[16,1536]{1,0:T(8,128)(2,1)} %project.1, bf16[16,512]{1,0:T(8,128)(2,1)} %output.1, ...), custom_call_target="tpu_custom_call" | custom-call | flops 1000000 | bytes 4194304 | tf_op jit(solution)/shard_map/pack/pallas_call | solution.py:918
  5.8 5.1 %collective-permute-start.3 = (bf16[16,4224]{1,0:T(8,128)(2,1)}, bf16[16,4224]{1,0:T(8,128)(2,1)S(1)}, u32[]{:S(2)}, u32[]{:S(2)}) collective-permute-start(bf16[16,4224]{1,0:T(8,128)(2,1)} %get-tuple-element.112), channel_id=1, source_target_pairs={{0,24},{1,25},{2,26},{3,27},{4,28},{5,29},{6,30},{7,31},{8,16},{9,... | collective-permute-start | bytes 405512 | tf_op jit(solution)/shard_map/ppermute | solution.py:377
  10.9 0.6 collective-permute-start.1
  11.5 1.7 %collective-permute-start = (bf16[448,512]{1,0:T(8,128)(2,1)}, bf16[448,512]{1,0:T(8,128)(2,1)S(1)}, u32[]{:S(2)}, u32[]{:S(2)}) collective-permute-start(bf16[448,512]{1,0:T(8,128)(2,1)} %get-tuple-element.111), channel_id=1, source_target_pairs={{0,1},{1,0},{2,3},{3,2},{4,5},{5,4},{6,7},{7,6},{8,9},{9,8},{10,11... | collective-permute-start | bytes 1376264 | tf_op jit(solution)/shard_map/ppermute | solution.py:377
  13.2 2.4 %collective-permute-done.3 = bf16[16,4224]{1,0:T(8,128)(2,1)S(1)} collective-permute-done((bf16[16,4224]{1,0:T(8,128)(2,1)}, bf16[16,4224]{1,0:T(8,128)(2,1)S(1)}, u32[]{:S(2)}, u32[]{:S(2)}) %collective-permute-start.3) | collective-permute-done | bytes 135200 | tf_op jit(solution)/shard_map/ppermute | solution.py:377
  15.6 6.9 %collective-permute-done.2 = bf16[16,4224]{1,0:T(8,128)(2,1)S(1)} collective-permute-done((bf16[16,4224]{1,0:T(8,128)(2,1)}, bf16[16,4224]{1,0:T(8,128)(2,1)S(1)}, u32[]{:S(2)}, u32[]{:S(2)}) %collective-permute-start.2) | collective-permute-done | bytes 135200 | tf_op jit(solution)/shard_map/ppermute | solution.py:377
  22.5 0.9 pad_maximum_fusion
  23.5 1.6 %collective-permute-start.4 = (bf16[64,4224]{1,0:T(8,128)(2,1)S(1)}, bf16[64,4224]{1,0:T(8,128)(2,1)S(1)}, u32[]{:S(2)}, u32[]{:S(2)}) collective-permute-start(bf16[64,4224]{1,0:T(8,128)(2,1)S(1)} %pad_maximum_fusion), channel_id=1, source_target_pairs={{0,4},{1,5},{2,3},{3,2},{4,0},{5,1},{6,7},{7,6},{8,12},{9,13},{10,... | collective-permute-start | bytes 1622024 | tf_op jit(solution)/shard_map/ppermute | solution.py:382
  25.1 2.2 %collective-permute-start.5 = (bf16[128,512]{1,0:T(8,128)(2,1)S(1)}, bf16[128,512]{1,0:T(8,128)(2,1)S(1)}, u32[]{:S(2)}, u32[]{:S(2)}) collective-permute-start(bf16[128,512]{1,0:T(8,128)(2,1)S(1)} %copy-done.5), channel_id=1, source_target_pairs={{0,16},{1,17},{2,18},{3,19},{4,20},{5,21},{6,22},{7,23},{8,24},{9,... | collective-permute-start | bytes 393224 | tf_op jit(solution)/shard_map/ppermute | solution.py:377
  27.3 5.7 %collective-permute-done.5 = bf16[128,512]{1,0:T(8,128)(2,1)S(1)} collective-permute-done((bf16[128,512]{1,0:T(8,128)(2,1)S(1)}, bf16[128,512]{1,0:T(8,128)(2,1)S(1)}, u32[]{:S(2)}, u32[]{:S(2)}) %collective-permute-start.5) | collective-permute-done | bytes 131104 | tf_op jit(solution)/shard_map/ppermute | solution.py:377
  33.0 1.5 %collective-permute-start.6 = (bf16[128,4224]{1,0:T(8,128)(2,1)S(1)}, bf16[128,4224]{1,0:T(8,128)(2,1)S(1)}, u32[]{:S(2)}, u32[]{:S(2)}) collective-permute-start(bf16[128,4224]{1,0:T(8,128)(2,1)S(1)} %constant_dynamic-update-slice_fusion.refs_0_), channel_id=1, source_target_pairs={{0,1},{1,0},{2,6},{3,7},{4,5},{5,4},{6,2},{7,3},{8,9},{9,8},{10,14... | collective-permute-start | bytes 3244040 | tf_op jit(solution)/shard_map/ppermute | solution.py:382
  34.6 1.3 collective-permute-start.7
  35.9 6.7 %collective-permute-done.7 = bf16[256,512]{1,0:T(8,128)(2,1)S(1)} collective-permute-done((bf16[256,512]{1,0:T(8,128)(2,1)S(1)}, bf16[256,512]{1,0:T(8,128)(2,1)S(1)}, u32[]{:S(2)}, u32[]{:S(2)}) %collective-permute-start.7) | collective-permute-done | bytes 262176 | tf_op jit(solution)/shard_map/ppermute | solution.py:377
  42.7 0.4 collective-permute-start.8
  43.2 9.5 %collective-permute-done.8 = bf16[512,512]{1,0:T(8,128)(2,1)S(1)} collective-permute-done((bf16[512,512]{1,0:T(8,128)(2,1)S(1)}, bf16[512,512]{1,0:T(8,128)(2,1)S(1)}, u32[]{:S(2)}, u32[]{:S(2)}) %collective-permute-start.8) | collective-permute-done | bytes 524320 | tf_op jit(solution)/shard_map/ppermute | solution.py:382
  52.7 1.0 collective-permute-start.10
  53.7 1.5 %collective-permute-start.12 = (bf16[1024,512]{1,0:T(8,128)(2,1)S(1)}, bf16[1024,512]{1,0:T(8,128)(2,1)S(1)}, u32[]{:S(2)}, u32[]{:S(2)}) collective-permute-start(bf16[1024,512]{1,0:T(8,128)(2,1)S(1)} %constant_dynamic-update-slice_fusion.2.refs_0_), channel_id=1, source_target_pairs={{0,1},{1,0},{2,6},{3,7},{4,5},{5,4},{6,2},{7,3},{8,9},{9,8},{10,14... | collective-permute-start | bytes 3145736 | tf_op jit(solution)/shard_map/ppermute | solution.py:382
  55.3 0.4 collective-permute-start.11
  55.8 0.1 pad_add_fusion.source_segments
  55.9 0.1 collective-permute-done.10.refs_3_
  56.0 2.3 %self_lower.1 = (bf16[512,512]{1,0:T(8,128)(2,1)S(1)}, bf16[768,1024]{1,0:T(8,128)(2,1)S(1)}, bf16[768,512]{1,0:T(8,128)(2,1)S(1)}, f32[8,512]{1,0:T(8,128)S(1)}...) custom-call(s32[2]{0:T(128)S(1)} %copy-done.2, ...), custom_call_target="tpu_custom_call" | custom-call | flops 1000 | bytes 4194304 | tf_op jit(solution)/shard_map/self_lower/pallas_call | solution.py:918
  58.4 9.6 %forward.1 = (bf16[512,512]{1,0:T(8,128)(2,1)S(1)}, f32[8,512]{1,0:T(8,128)S(1)}, f32[512,512]{1,0:T(8,128)S(1)}, bf16[512,512]{1,0:T(8,128)(2,1)S(1)}, bf16[512...) custom-call(s32[2]{0:T(128)S(1)} %copy-done.2, ...), custom_call_target="tpu_custom_call" | custom-call | flops 1000 | bytes 4194304 | tf_op jit(solution)/shard_map/forward/pallas_call | solution.py:918
  68.0 0.6 collective-permute-done.12.refs_1_
  68.6 1.2 feed_front.1
  69.8 1.4 collective-permute-done.13.refs_3_
  71.3 10.2 %feed.1 = (f32[512,512]{1,0:T(8,128)S(1)}, f32[512,512]{1,0:T(8,128)S(1)}, bf16[2048,512]{1,0:T(8,128)(2,1)S(1)}, bf16[2048,512]{1,0:T(8,128)(2,1)S(1)}, f32[1,2048]{1,0:T(1,128)S(1)}) custom-call(s32[2]{0:T(128)S(1)} %copy-done.2, bf16[512,512]{1,0:T(8,128)(2,1)S(1)} %get-tuple-element.126.lowered, bf16[512,512]{1,0:T(8,128)(2,1)S(1)} %get-tuple-element.127.flipped, ...), custom_call_target="tpu_custom_call" | custom-call | flops 10000000000 | bytes 4194304 | tf_op jit(solution)/shard_map/feed/pallas_call | solution.py:918
  81.4 0.2 collective-permute-start.14
  81.6 3.0 %feed_last.1 = (bf16[512,512]{1,0:T(8,128)(2,1)}, f32[512,512]{1,0:T(8,128)S(1)}, f32[8,512]{1,0:T(8,128)S(1)}, bf16[512,512]{1,0:T(8,128)(2,1)S(1)}, f32[8,512]...) custom-call(s32[2]{0:T(128)S(1)} %copy-done.2, f32[512,512]{1,0:T(8,128)S(1)} %get-tuple-element.125.after_cross, ...), custom_call_target="tpu_custom_call" | custom-call | flops 4000000000 | bytes 4194304 | tf_op jit(solution)/shard_map/feed_last/pallas_call | solution.py:918
  84.6 1.0 collective-permute-done.14
  85.7 0.3 slice_add_fusion
  85.9 1.5 %collective-permute-start.16 = (bf16[1024,512]{1,0:T(8,128)(2,1)S(1)}, bf16[1024,512]{1,0:T(8,128)(2,1)S(1)}, u32[]{:S(2)}, u32[]{:S(2)}) collective-permute-start(bf16[1024,512]{1,0:T(8,128)(2,1)S(1)} %get-tuple-element.203), channel_id=1, source_target_pairs={{0,1},{1,0},{2,6},{3,7},{4,5},{5,4},{6,2},{7,3},{8,9},{9,8},{10,14... | collective-permute-start | bytes 3145736 | tf_op jit(solution)/shard_map/ppermute | solution.py:382
  87.4 7.1 %cross_backward.1 = (bf16[512,512]{1,0:T(8,128)(2,1)S(1)}, f32[192,512]{1,0:T(8,128)S(1)}, bf16[192,512]{1,0:T(8,128)(2,1)S(1)}, bf16[512,1024]{1,0:T(8,128)(2,1)S(1)}) custom-call(s32[2]{0:T(128)S(1)} %copy-done.2, s32[1,1024]{1,0:T(1,128)S(1)} %copy-done.3, s32[1,384]{1,0:T(1,128)S(1)} %pad_add_fusion.source_segments, bf16[192,512]{1,0:T(8,128)(2,1)S(1)} %copy-done.1, ...), custom_call_target="tpu_custom_call" | custom-call | flops 10000000000 | bytes 4194304 | tf_op jit(solution)/shard_map/cross_backward/pallas_call | solution.py:918
  94.6 3.3 %cross_weights.1 = (f32[512,512]{1,0:T(8,128)S(1)}, bf16[512,512]{1,0:T(8,128)(2,1)S(1)}, f32[8,512]{1,0:T(8,128)S(1)}, bf16[256,2560]{1,0:T(8,128)(2,1)S(1)}, b...) custom-call(s32[2]{0:T(128)S(1)} %copy-done.2, f32[512,512]{1,0:T(8,128)S(1)} %get-tuple-element.137.after_self, ...), custom_call_target="tpu_custom_call" | custom-call | flops 6000000000 | bytes 4194304 | tf_op jit(solution)/shard_map/cross_weights/pallas_call | solution.py:918
  97.8 0.1 collective-permute-start.15
  97.9 2.8 %collective-permute-done.16 = bf16[1024,512]{1,0:T(8,128)(2,1)S(1)} collective-permute-done((bf16[1024,512]{1,0:T(8,128)(2,1)S(1)}, bf16[1024,512]{1,0:T(8,128)(2,1)S(1)}, u32[]{:S(2)}, u32[]{:S(2)}) %collective-permute-start.16) | collective-permute-done | bytes 1048608 | tf_op jit(solution)/shard_map/ppermute | solution.py:382
  100.9 1.7 %collective-permute-start.18 = (bf16[512,512]{1,0:T(8,128)(2,1)S(1)}, bf16[512,512]{1,0:T(8,128)(2,1)S(1)}, u32[]{:S(2)}, u32[]{:S(2)}) collective-permute-start(bf16[512,512]{1,0:T(8,128)(2,1)S(1)} %slice_add_fusion.5), channel_id=1, source_target_pairs={{0,4},{1,5},{2,3},{3,2},{4,0},{5,1},{6,7},{7,6},{8,12},{9,13},{10,... | collective-permute-start | bytes 1572872 | tf_op jit(solution)/shard_map/ppermute | solution.py:382
  102.6 0.2 slice_add_fusion.2
  102.8 1.5 collective-permute-start.17
  104.3 10.5 %self_backward.1 = (f32[512,512]{1,0:T(8,128)S(1)}, bf16[448,512]{1,0:T(8,128)(2,1)S(1)}, bf16[256,1664]{1,0:T(8,128)(2,1)S(1)}, bf16[256,1664]{1,0:T(8,128)(2,1)S(1)}) custom-call(s32[2]{0:T(128)S(1)} %copy-done.2, s32[1,1024]{1,0:T(1,128)S(1)} %copy-done.3, bf16[512,512]{1,0:T(8,128)(2,1)S(1)} %bitcast.27, bf16[256,512]{1,0:T(8,128)(2,1)S(1)} %slice.183.window, ...), custom_call_target="tpu_custom_call" | custom-call | flops 16000000000 | bytes 4194304 | tf_op jit(solution)/shard_map/self_backward/pallas_call | solution.py:918
  114.9 0.8 collective-permute-done.18
  115.7 0.1 fusion
  115.9 1.6 %collective-permute-start.19 = (bf16[256,512]{1,0:T(8,128)(2,1)S(1)}, bf16[256,512]{1,0:T(8,128)(2,1)S(1)}, u32[]{:S(2)}, u32[]{:S(2)}) collective-permute-start(bf16[256,512]{1,0:T(8,128)(2,1)S(1)} %pad_maximum_fusion.3), channel_id=1, source_target_pairs={{0,8},{1,9},{2,10},{3,11},{4,12},{5,13},{6,14},{7,15},{8,0},{9,1},... | collective-permute-start | bytes 786440 | tf_op jit(solution)/shard_map/ppermute | solution.py:377
  117.5 1.4 collective-permute-start.23
  118.9 0.1 slice_add_fusion.6
  119.0 1.6 %collective-permute-start.22 = (bf16[128,1664]{1,0:T(8,128)(2,1)S(1)}, bf16[128,1664]{1,0:T(8,128)(2,1)S(1)}, u32[]{:S(2)}, u32[]{:S(2)}) collective-permute-start(bf16[128,1664]{1,0:T(8,128)(2,1)S(1)} %get-tuple-element.207), channel_id=1, source_target_pairs={{0,1},{1,0},{2,6},{3,7},{4,5},{5,4},{6,2},{7,3},{8,9},{9,8},{10,14... | collective-permute-start | bytes 1277960 | tf_op jit(solution)/shard_map/ppermute | solution.py:382
  120.7 4.5 %collective-permute-done.19 = bf16[256,512]{1,0:T(8,128)(2,1)S(1)} collective-permute-done((bf16[256,512]{1,0:T(8,128)(2,1)S(1)}, bf16[256,512]{1,0:T(8,128)(2,1)S(1)}, u32[]{:S(2)}, u32[]{:S(2)}) %collective-permute-start.19) | collective-permute-done | bytes 262176 | tf_op jit(solution)/shard_map/ppermute | solution.py:377
  125.1 2.3 %collective-permute-start.21 = (bf16[128,512]{1,0:T(8,128)(2,1)S(1)}, bf16[128,512]{1,0:T(8,128)(2,1)S(1)}, u32[]{:S(2)}, u32[]{:S(2)}) collective-permute-start(bf16[128,512]{1,0:T(8,128)(2,1)S(1)} %get-tuple-element.208), channel_id=1, source_target_pairs={{0,16},{1,17},{2,18},{3,19},{4,20},{5,21},{6,22},{7,23},{8,24},{9,... | collective-permute-start | bytes 393224 | tf_op jit(solution)/shard_map/ppermute | solution.py:377
  127.5 0.3 collective-permute-done.23
  127.8 1.0 collective-permute-done.22
  128.9 1.6 %collective-permute-start.28 = (bf16[64,1664]{1,0:T(8,128)(2,1)S(1)}, bf16[64,1664]{1,0:T(8,128)(2,1)S(1)}, u32[]{:S(2)}, u32[]{:S(2)}) collective-permute-start(bf16[64,1664]{1,0:T(8,128)(2,1)S(1)} %slice_add_fusion.11), channel_id=1, source_target_pairs={{0,4},{1,5},{2,3},{3,2},{4,0},{5,1},{6,7},{7,6},{8,12},{9,13},{10,... | collective-permute-start | bytes 638984 | tf_op jit(solution)/shard_map/ppermute | solution.py:382
  130.4 4.0 %collective-permute-done.21.refs_1_ = bf16[128,512]{1,0:T(8,128)(2,1)S(1)} collective-permute-done((bf16[128,512]{1,0:T(8,128)(2,1)S(1)}, bf16[128,512]{1,0:T(8,128)(2,1)S(1)}, u32[]{:S(2)}, u32[]{:S(2)}) %collective-permute-start.21) | collective-permute-done | bytes 131104 | tf_op jit(solution)/shard_map/ppermute | solution.py:377
  134.4 0.8 collective-permute-start.24
  135.3 2.9 %collective-permute-start.31 = (bf16[16,1664]{1,0:T(8,128)(2,1)S(1)}, bf16[16,1664]{1,0:T(8,128)(2,1)S(1)}, u32[]{:S(2)}, u32[]{:S(2)}) collective-permute-start(bf16[16,1664]{1,0:T(8,128)(2,1)S(1)} %get-tuple-element.216), channel_id=1, source_target_pairs={{0,24},{1,25},{2,26},{3,27},{4,28},{5,29},{6,30},{7,31},{8,16},{9,... | collective-permute-start | bytes 159752 | tf_op jit(solution)/shard_map/ppermute | solution.py:377
  138.2 1.0 collective-permute-start.27
  139.2 0.4 collective-permute-start.26
  139.6 3.0 %collective-permute-start.25 = (bf16[16,2560]{1,0:T(8,128)(2,1)S(1)}, bf16[16,2560]{1,0:T(8,128)(2,1)S(1)}, u32[]{:S(2)}, u32[]{:S(2)}) collective-permute-start(bf16[16,2560]{1,0:T(8,128)(2,1)S(1)} %get-tuple-element.214), channel_id=1, source_target_pairs={{0,8},{1,9},{2,10},{3,11},{4,12},{5,13},{6,14},{7,15},{8,0},{9,1},... | collective-permute-start | bytes 245768 | tf_op jit(solution)/shard_map/ppermute | solution.py:377
  142.6 3.0 %collective-permute-start.30 = (bf16[16,1664]{1,0:T(8,128)(2,1)S(1)}, bf16[16,1664]{1,0:T(8,128)(2,1)S(1)}, u32[]{:S(2)}, u32[]{:S(2)}) collective-permute-start(bf16[16,1664]{1,0:T(8,128)(2,1)S(1)} %get-tuple-element.217), channel_id=1, source_target_pairs={{0,16},{1,17},{2,18},{3,19},{4,20},{5,21},{6,22},{7,23},{8,24},{9,... | collective-permute-start | bytes 159752 | tf_op jit(solution)/shard_map/ppermute | solution.py:377
  145.6 0.6 collective-permute-done.24
  146.2 1.2 collective-permute-start.29
  147.4 0.8 convert_add_fusion
  148.2 2.3 %target_grad.1 = f32[512,512]{1,0:T(8,128)} custom-call(s32[2]{0:T(128)S(1)} %copy-done.2, f32[512,512]{1,0:T(8,128)S(1)} %get-tuple-element.165.back, bf16[256,512]{1,0:T(8,128)(2,1)S(1)} %slice.193.came, bf16[512,512]{1,0:T(8,128)(2,1)S(1)} %bitcast.28, f32[512,512]{1,0:T(8,128)S(1)} %get-tuple-element.177.self_grad, f32[8,512]{1,0:T(8,128)S(1)} %get-tuple-element.119.vectors), custom_call_target="tpu_custom_call" | custom-call | flops 1000000 | bytes 4194304 | tf_op jit(solution)/shard_map/target_grad/pallas_call | solution.py:918
  150.6 1.4 finish.1
  (57 shorter events, 0.9 us)
Async XLA Ops:
  5.8 19.3 %copy-start.5 = (bf16[128,512]{1,0:T(8,128)(2,1)S(1)}, bf16[128,512]{1,0:T(8,128)(2,1)}, u32[]{:S(2)}) copy-start(bf16[128,512]{1,0:T(8,128)(2,1)} %get-tuple-element.115) | copy-start | bytes 393220
  5.8 9.8 %collective-permute-start.3 = (bf16[16,4224]{1,0:T(8,128)(2,1)}, bf16[16,4224]{1,0:T(8,128)(2,1)S(1)}, u32[]{:S(2)}, u32[]{:S(2)}) collective-permute-start(bf16[16,4224]{1,0:T(8,128)(2,1)} %get-tuple-element.112), channel_id=1, source_target_pairs={{0,24},{1,25},{2,26},{3,27},{4,28},{5,29},{6,30},{7,31},{8,16},{9,... | collective-permute-start | bytes 405512 | tf_op jit(solution)/shard_map/ppermute | solution.py:377
  10.9 11.6 %collective-permute-start.2 = (bf16[16,4224]{1,0:T(8,128)(2,1)}, bf16[16,4224]{1,0:T(8,128)(2,1)S(1)}, u32[]{:S(2)}, u32[]{:S(2)}) collective-permute-start(bf16[16,4224]{1,0:T(8,128)(2,1)} %get-tuple-element.112), channel_id=1, source_target_pairs={{0,16},{1,17},{2,18},{3,19},{4,20},{5,21},{6,22},{7,23},{8,24},{9,... | collective-permute-start | bytes 405512 | tf_op jit(solution)/shard_map/ppermute | solution.py:377
  10.9 11.6 %collective-permute-start.1 = (bf16[16,4224]{1,0:T(8,128)(2,1)}, bf16[16,4224]{1,0:T(8,128)(2,1)S(1)}, u32[]{:S(2)}, u32[]{:S(2)}) collective-permute-start(bf16[16,4224]{1,0:T(8,128)(2,1)} %get-tuple-element.112), channel_id=1, source_target_pairs={{0,8},{1,9},{2,10},{3,11},{4,12},{5,13},{6,14},{7,15},{8,0},{9,1},... | collective-permute-start | bytes 405512 | tf_op jit(solution)/shard_map/ppermute | solution.py:377
  11.5 11.9 %collective-permute-start = (bf16[448,512]{1,0:T(8,128)(2,1)}, bf16[448,512]{1,0:T(8,128)(2,1)S(1)}, u32[]{:S(2)}, u32[]{:S(2)}) collective-permute-start(bf16[448,512]{1,0:T(8,128)(2,1)} %get-tuple-element.111), channel_id=1, source_target_pairs={{0,1},{1,0},{2,3},{3,2},{4,5},{5,4},{6,7},{7,6},{8,9},{9,8},{10,11... | collective-permute-start | bytes 1376264 | tf_op jit(solution)/shard_map/ppermute | solution.py:377
  23.5 9.5 %collective-permute-start.4 = (bf16[64,4224]{1,0:T(8,128)(2,1)S(1)}, bf16[64,4224]{1,0:T(8,128)(2,1)S(1)}, u32[]{:S(2)}, u32[]{:S(2)}) collective-permute-start(bf16[64,4224]{1,0:T(8,128)(2,1)S(1)} %pad_maximum_fusion), channel_id=1, source_target_pairs={{0,4},{1,5},{2,3},{3,2},{4,0},{5,1},{6,7},{7,6},{8,12},{9,13},{10,... | collective-permute-start | bytes 1622024 | tf_op jit(solution)/shard_map/ppermute | solution.py:382
  25.1 7.9 %collective-permute-start.5 = (bf16[128,512]{1,0:T(8,128)(2,1)S(1)}, bf16[128,512]{1,0:T(8,128)(2,1)S(1)}, u32[]{:S(2)}, u32[]{:S(2)}) collective-permute-start(bf16[128,512]{1,0:T(8,128)(2,1)S(1)} %copy-done.5), channel_id=1, source_target_pairs={{0,16},{1,17},{2,18},{3,19},{4,20},{5,21},{6,22},{7,23},{8,24},{9,... | collective-permute-start | bytes 393224 | tf_op jit(solution)/shard_map/ppermute | solution.py:377
  33.0 19.6 %collective-permute-start.6 = (bf16[128,4224]{1,0:T(8,128)(2,1)S(1)}, bf16[128,4224]{1,0:T(8,128)(2,1)S(1)}, u32[]{:S(2)}, u32[]{:S(2)}) collective-permute-start(bf16[128,4224]{1,0:T(8,128)(2,1)S(1)} %constant_dynamic-update-slice_fusion.refs_0_), channel_id=1, source_target_pairs={{0,1},{1,0},{2,6},{3,7},{4,5},{5,4},{6,2},{7,3},{8,9},{9,8},{10,14... | collective-permute-start | bytes 3244040 | tf_op jit(solution)/shard_map/ppermute | solution.py:382
  34.6 8.0 %collective-permute-start.7 = (bf16[256,512]{1,0:T(8,128)(2,1)S(1)}, bf16[256,512]{1,0:T(8,128)(2,1)S(1)}, u32[]{:S(2)}, u32[]{:S(2)}) collective-permute-start(bf16[256,512]{1,0:T(8,128)(2,1)S(1)} %pad_maximum_fusion.2), channel_id=1, source_target_pairs={{0,8},{1,9},{2,10},{3,11},{4,12},{5,13},{6,14},{7,15},{8,0},{9,1},... | collective-permute-start | bytes 786440 | tf_op jit(solution)/shard_map/ppermute | solution.py:377
  42.7 13.0 %copy-start.6 = (s32[1,336]{1,0:T(1,128)S(1)}, s32[1,336]{1,0:T(1,128)}, u32[]{:S(2)}) copy-start(s32[1,336]{1,0:T(1,128)} %param.23) | copy-start | bytes 4036
  42.7 10.0 %collective-permute-start.8 = (bf16[512,512]{1,0:T(8,128)(2,1)S(1)}, bf16[512,512]{1,0:T(8,128)(2,1)S(1)}, u32[]{:S(2)}, u32[]{:S(2)}) collective-permute-start(bf16[512,512]{1,0:T(8,128)(2,1)S(1)} %pad_maximum_fusion.1), channel_id=1, source_target_pairs={{0,4},{1,5},{2,3},{3,2},{4,0},{5,1},{6,7},{7,6},{8,12},{9,13},{10,... | collective-permute-start | bytes 1572872 | tf_op jit(solution)/shard_map/ppermute | solution.py:382
  43.1 12.9 %collective-permute-start.9 = (bf16[128,4224]{1,0:T(8,128)(2,1)S(1)}, bf16[128,4224]{1,0:T(8,128)(2,1)S(1)}, u32[]{:S(2)}, u32[]{:S(2)}) collective-permute-start(bf16[128,4224]{1,0:T(8,128)(2,1)S(1)} %constant_dynamic-update-slice_fusion.refs_0_), channel_id=1, source_target_pairs={{0,2},{1,3},{2,0},{3,1},{4,6},{5,7},{6,4},{7,5},{8,10},{9,11},{10,... | collective-permute-start | bytes 3244040 | tf_op jit(solution)/shard_map/ppermute | solution.py:377
  43.2 12.8 %copy-start = (bf16[1,512,512]{2,1,0:T(8,128)(2,1)S(1)}, bf16[1,512,512]{2,1,0:T(8,128)(2,1)}, u32[]{:S(2)}) copy-start(bf16[1,512,512]{2,1,0:T(8,128)(2,1)} %param.20) | copy-start | bytes 1572868
  43.2 12.8 %copy-start.2 = (s32[2]{0:T(128)S(1)}, s32[2]{0:T(128)}, u32[]{:S(2)}) copy-start(s32[2]{0:T(128)} %pad_add_fusion.2.place) | copy-start | bytes 28
  52.7 3.4 %collective-permute-start.10 = (bf16[128,4224]{1,0:T(8,128)(2,1)S(1)}, bf16[128,4224]{1,0:T(8,128)(2,1)S(1)}, u32[]{:S(2)}, u32[]{:S(2)}) collective-permute-start(bf16[128,4224]{1,0:T(8,128)(2,1)S(1)} %collective-permute-done.6.refs_1_), channel_id=1, source_target_pairs={{0,2},{1,3},{2,0},{3,1},{4,6},{5,7},{6,4},{7,5},{8,10},{9,11},{10,... | collective-permute-start | bytes 3244040 | tf_op jit(solution)/shard_map/ppermute | solution.py:377
  53.7 14.9 %collective-permute-start.12 = (bf16[1024,512]{1,0:T(8,128)(2,1)S(1)}, bf16[1024,512]{1,0:T(8,128)(2,1)S(1)}, u32[]{:S(2)}, u32[]{:S(2)}) collective-permute-start(bf16[1024,512]{1,0:T(8,128)(2,1)S(1)} %constant_dynamic-update-slice_fusion.2.refs_0_), channel_id=1, source_target_pairs={{0,1},{1,0},{2,6},{3,7},{4,5},{5,4},{6,2},{7,3},{8,9},{9,8},{10,14... | collective-permute-start | bytes 3145736 | tf_op jit(solution)/shard_map/ppermute | solution.py:382
  55.3 13.3 %collective-permute-start.11 = (bf16[1024,512]{1,0:T(8,128)(2,1)S(1)}, bf16[1024,512]{1,0:T(8,128)(2,1)S(1)}, u32[]{:S(2)}, u32[]{:S(2)}) collective-permute-start(bf16[1024,512]{1,0:T(8,128)(2,1)S(1)} %constant_dynamic-update-slice_fusion.2.refs_0_), channel_id=1, source_target_pairs={{0,2},{1,3},{2,0},{3,1},{4,6},{5,7},{6,4},{7,5},{8,10},{9,11},{10,... | collective-permute-start | bytes 3145736 | tf_op jit(solution)/shard_map/ppermute | solution.py:377
  55.9 2.5 %copy-start.1 = (bf16[192,512]{1,0:T(8,128)(2,1)S(1)}, bf16[192,512]{1,0:T(8,128)(2,1)}, u32[]{:S(2)}) copy-start(bf16[192,512]{1,0:T(8,128)(2,1)} %get-tuple-element.110.own_source) | copy-start | bytes 589828
  55.9 2.5 %copy-start.3 = (s32[1,1024]{1,0:T(1,128)S(1)}, s32[1,1024]{1,0:T(1,128)}, u32[]{:S(2)}) copy-start(s32[1,1024]{1,0:T(1,128)} %segments.5) | copy-start | bytes 12292
  58.4 12.9 %copy-start.4 = (bf16[1,512,512]{2,1,0:T(8,128)(2,1)S(1)}, bf16[1,512,512]{2,1,0:T(8,128)(2,1)}, u32[]{:S(2)}) copy-start(bf16[1,512,512]{2,1,0:T(8,128)(2,1)} %param.24) | copy-start | bytes 1572868
  68.6 2.7 %collective-permute-start.13 = (bf16[1024,512]{1,0:T(8,128)(2,1)S(1)}, bf16[1024,512]{1,0:T(8,128)(2,1)S(1)}, u32[]{:S(2)}, u32[]{:S(2)}) collective-permute-start(bf16[1024,512]{1,0:T(8,128)(2,1)S(1)} %collective-permute-done.12.refs_1_), channel_id=1, source_target_pairs={{0,2},{1,3},{2,0},{3,1},{4,6},{5,7},{6,4},{7,5},{8,10},{9,11},{10,... | collective-permute-start | bytes 3145736 | tf_op jit(solution)/shard_map/ppermute | solution.py:377
  81.4 4.2 %collective-permute-start.14 = (bf16[2048,512]{1,0:T(8,128)(2,1)S(1)}, bf16[2048,512]{1,0:T(8,128)(2,1)S(1)}, u32[]{:S(2)}, u32[]{:S(2)}) collective-permute-start(bf16[2048,512]{1,0:T(8,128)(2,1)S(1)} %get-tuple-element.146), channel_id=1, source_target_pairs={{0,2},{1,3},{2,0},{3,1},{4,6},{5,7},{6,4},{7,5},{8,10},{9,11},{10,... | collective-permute-start | bytes 6291464 | tf_op jit(solution)/shard_map/ppermute | solution.py:377
  85.9 14.9 %collective-permute-start.16 = (bf16[1024,512]{1,0:T(8,128)(2,1)S(1)}, bf16[1024,512]{1,0:T(8,128)(2,1)S(1)}, u32[]{:S(2)}, u32[]{:S(2)}) collective-permute-start(bf16[1024,512]{1,0:T(8,128)(2,1)S(1)} %get-tuple-element.203), channel_id=1, source_target_pairs={{0,1},{1,0},{2,6},{3,7},{4,5},{5,4},{6,2},{7,3},{8,9},{9,8},{10,14... | collective-permute-start | bytes 3145736 | tf_op jit(solution)/shard_map/ppermute | solution.py:382
  97.8 4.8 %collective-permute-start.15 = (bf16[256,2560]{1,0:T(8,128)(2,1)S(1)}, bf16[256,2560]{1,0:T(8,128)(2,1)S(1)}, u32[]{:S(2)}, u32[]{:S(2)}) collective-permute-start(bf16[256,2560]{1,0:T(8,128)(2,1)S(1)} %get-tuple-element.156), channel_id=1, source_target_pairs={{0,2},{1,3},{2,0},{3,1},{4,6},{5,7},{6,4},{7,5},{8,10},{9,11},{10,... | collective-permute-start | bytes 3932168 | tf_op jit(solution)/shard_map/ppermute | solution.py:377
  100.9 14.9 %collective-permute-start.18 = (bf16[512,512]{1,0:T(8,128)(2,1)S(1)}, bf16[512,512]{1,0:T(8,128)(2,1)S(1)}, u32[]{:S(2)}, u32[]{:S(2)}) collective-permute-start(bf16[512,512]{1,0:T(8,128)(2,1)S(1)} %slice_add_fusion.5), channel_id=1, source_target_pairs={{0,4},{1,5},{2,3},{3,2},{4,0},{5,1},{6,7},{7,6},{8,12},{9,13},{10,... | collective-permute-start | bytes 1572872 | tf_op jit(solution)/shard_map/ppermute | solution.py:382
  102.8 13.0 %collective-permute-start.17 = (bf16[128,2560]{1,0:T(8,128)(2,1)S(1)}, bf16[128,2560]{1,0:T(8,128)(2,1)S(1)}, u32[]{:S(2)}, u32[]{:S(2)}) collective-permute-start(bf16[128,2560]{1,0:T(8,128)(2,1)S(1)} %get-tuple-element.205), channel_id=1, source_target_pairs={{0,1},{1,0},{2,6},{3,7},{4,5},{5,4},{6,2},{7,3},{8,9},{9,8},{10,14... | collective-permute-start | bytes 1966088 | tf_op jit(solution)/shard_map/ppermute | solution.py:382
  114.8 4.1 %collective-permute-start.20 = (bf16[256,1664]{1,0:T(8,128)(2,1)S(1)}, bf16[256,1664]{1,0:T(8,128)(2,1)S(1)}, u32[]{:S(2)}, u32[]{:S(2)}) collective-permute-start(bf16[256,1664]{1,0:T(8,128)(2,1)S(1)} %get-tuple-element.168), channel_id=1, source_target_pairs={{0,2},{1,3},{2,0},{3,1},{4,6},{5,7},{6,4},{7,5},{8,10},{9,11},{10,... | collective-permute-start | bytes 2555912 | tf_op jit(solution)/shard_map/ppermute | solution.py:377
  115.9 9.2 %collective-permute-start.19 = (bf16[256,512]{1,0:T(8,128)(2,1)S(1)}, bf16[256,512]{1,0:T(8,128)(2,1)S(1)}, u32[]{:S(2)}, u32[]{:S(2)}) collective-permute-start(bf16[256,512]{1,0:T(8,128)(2,1)S(1)} %pad_maximum_fusion.3), channel_id=1, source_target_pairs={{0,8},{1,9},{2,10},{3,11},{4,12},{5,13},{6,14},{7,15},{8,0},{9,1},... | collective-permute-start | bytes 786440 | tf_op jit(solution)/shard_map/ppermute | solution.py:377
  117.5 10.3 %collective-permute-start.23 = (bf16[64,2560]{1,0:T(8,128)(2,1)S(1)}, bf16[64,2560]{1,0:T(8,128)(2,1)S(1)}, u32[]{:S(2)}, u32[]{:S(2)}) collective-permute-start(bf16[64,2560]{1,0:T(8,128)(2,1)S(1)} %slice_add_fusion.8), channel_id=1, source_target_pairs={{0,4},{1,5},{2,3},{3,2},{4,0},{5,1},{6,7},{7,6},{8,12},{9,13},{10,... | collective-permute-start | bytes 983048 | tf_op jit(solution)/shard_map/ppermute | solution.py:382
  119.0 9.8 %collective-permute-start.22 = (bf16[128,1664]{1,0:T(8,128)(2,1)S(1)}, bf16[128,1664]{1,0:T(8,128)(2,1)S(1)}, u32[]{:S(2)}, u32[]{:S(2)}) collective-permute-start(bf16[128,1664]{1,0:T(8,128)(2,1)S(1)} %get-tuple-element.207), channel_id=1, source_target_pairs={{0,1},{1,0},{2,6},{3,7},{4,5},{5,4},{6,2},{7,3},{8,9},{9,8},{10,14... | collective-permute-start | bytes 1277960 | tf_op jit(solution)/shard_map/ppermute | solution.py:382
  125.1 9.3 %collective-permute-start.21 = (bf16[128,512]{1,0:T(8,128)(2,1)S(1)}, bf16[128,512]{1,0:T(8,128)(2,1)S(1)}, u32[]{:S(2)}, u32[]{:S(2)}) collective-permute-start(bf16[128,512]{1,0:T(8,128)(2,1)S(1)} %get-tuple-element.208), channel_id=1, source_target_pairs={{0,16},{1,17},{2,18},{3,19},{4,20},{5,21},{6,22},{7,23},{8,24},{9,... | collective-permute-start | bytes 393224 | tf_op jit(solution)/shard_map/ppermute | solution.py:377
  128.9 6.4 %collective-permute-start.28 = (bf16[64,1664]{1,0:T(8,128)(2,1)S(1)}, bf16[64,1664]{1,0:T(8,128)(2,1)S(1)}, u32[]{:S(2)}, u32[]{:S(2)}) collective-permute-start(bf16[64,1664]{1,0:T(8,128)(2,1)S(1)} %slice_add_fusion.11), channel_id=1, source_target_pairs={{0,4},{1,5},{2,3},{3,2},{4,0},{5,1},{6,7},{7,6},{8,12},{9,13},{10,... | collective-permute-start | bytes 638984 | tf_op jit(solution)/shard_map/ppermute | solution.py:382
  134.4 11.8 %collective-permute-start.24 = (bf16[448,512]{1,0:T(8,128)(2,1)S(1)}, bf16[448,512]{1,0:T(8,128)(2,1)S(1)}, u32[]{:S(2)}, u32[]{:S(2)}) collective-permute-start(bf16[448,512]{1,0:T(8,128)(2,1)S(1)} %get-tuple-element.176), channel_id=1, source_target_pairs={{0,1},{1,0},{2,3},{3,2},{4,5},{5,4},{6,7},{7,6},{8,9},{9,8},{10,11... | collective-permute-start | bytes 1376264 | tf_op jit(solution)/shard_map/ppermute | solution.py:377
  135.3 7.3 %collective-permute-start.31 = (bf16[16,1664]{1,0:T(8,128)(2,1)S(1)}, bf16[16,1664]{1,0:T(8,128)(2,1)S(1)}, u32[]{:S(2)}, u32[]{:S(2)}) collective-permute-start(bf16[16,1664]{1,0:T(8,128)(2,1)S(1)} %get-tuple-element.216), channel_id=1, source_target_pairs={{0,24},{1,25},{2,26},{3,27},{4,28},{5,29},{6,30},{7,31},{8,16},{9,... | collective-permute-start | bytes 159752 | tf_op jit(solution)/shard_map/ppermute | solution.py:377
  138.2 12.3 %collective-permute-start.27 = (bf16[16,2560]{1,0:T(8,128)(2,1)S(1)}, bf16[16,2560]{1,0:T(8,128)(2,1)S(1)}, u32[]{:S(2)}, u32[]{:S(2)}) collective-permute-start(bf16[16,2560]{1,0:T(8,128)(2,1)S(1)} %get-tuple-element.212), channel_id=1, source_target_pairs={{0,24},{1,25},{2,26},{3,27},{4,28},{5,29},{6,30},{7,31},{8,16},{9,... | collective-permute-start | bytes 245768 | tf_op jit(solution)/shard_map/ppermute | solution.py:377
  139.2 11.3 %collective-permute-start.26 = (bf16[16,2560]{1,0:T(8,128)(2,1)S(1)}, bf16[16,2560]{1,0:T(8,128)(2,1)S(1)}, u32[]{:S(2)}, u32[]{:S(2)}) collective-permute-start(bf16[16,2560]{1,0:T(8,128)(2,1)S(1)} %get-tuple-element.213), channel_id=1, source_target_pairs={{0,16},{1,17},{2,18},{3,19},{4,20},{5,21},{6,22},{7,23},{8,24},{9,... | collective-permute-start | bytes 245768 | tf_op jit(solution)/shard_map/ppermute | solution.py:377
  139.6 10.9 %collective-permute-start.25 = (bf16[16,2560]{1,0:T(8,128)(2,1)S(1)}, bf16[16,2560]{1,0:T(8,128)(2,1)S(1)}, u32[]{:S(2)}, u32[]{:S(2)}) collective-permute-start(bf16[16,2560]{1,0:T(8,128)(2,1)S(1)} %get-tuple-element.214), channel_id=1, source_target_pairs={{0,8},{1,9},{2,10},{3,11},{4,12},{5,13},{6,14},{7,15},{8,0},{9,1},... | collective-permute-start | bytes 245768 | tf_op jit(solution)/shard_map/ppermute | solution.py:377
  142.6 7.9 %collective-permute-start.30 = (bf16[16,1664]{1,0:T(8,128)(2,1)S(1)}, bf16[16,1664]{1,0:T(8,128)(2,1)S(1)}, u32[]{:S(2)}, u32[]{:S(2)}) collective-permute-start(bf16[16,1664]{1,0:T(8,128)(2,1)S(1)} %get-tuple-element.217), channel_id=1, source_target_pairs={{0,16},{1,17},{2,18},{3,19},{4,20},{5,21},{6,22},{7,23},{8,24},{9,... | collective-permute-start | bytes 159752 | tf_op jit(solution)/shard_map/ppermute | solution.py:377
  146.2 4.3 %collective-permute-start.29 = (bf16[16,1664]{1,0:T(8,128)(2,1)S(1)}, bf16[16,1664]{1,0:T(8,128)(2,1)S(1)}, u32[]{:S(2)}, u32[]{:S(2)}) collective-permute-start(bf16[16,1664]{1,0:T(8,128)(2,1)S(1)} %get-tuple-element.218), channel_id=1, source_target_pairs={{0,8},{1,9},{2,10},{3,11},{4,12},{5,13},{6,14},{7,15},{8,0},{9,1},... | collective-permute-start | bytes 159752 | tf_op jit(solution)/shard_map/ppermute | solution.py:377
